TPU v7x, 512 devices: a whole 4x4x16 slice. The times are simulated.
512 devices in a mesh: wide: 64 (over y, z), tensor: 8 (over x, core).
Axes of the slice: x: 4, y: 4, z: 16, core: 2. Of those that a mesh axis runs over, the one named last changes fastest.
Arguments:
- hidden: bfloat16 [256, 8192], P('wide', 'tensor'), may hold values from -6 to 6
- q_base: bfloat16 [256, 8192], P('wide', 'tensor'), may hold values from -14 to 14
- base_key: bfloat16 [256, 1024], P('wide', 'tensor'), may hold values from -6 to 6
- base_value: bfloat16 [256, 1024], P('wide', 'tensor'), may hold values from -6 to 6
- paged_key_cache: bfloat16 [2048, 128, 1024], P('wide', None, 'tensor'), may hold values from -6 to 6
- paged_value_cache: bfloat16 [2048, 128, 1024], P('wide', None, 'tensor'), may hold values from -6 to 6
- page_table: int32 [256, 8], P('wide'), may hold values from 0 to 31, as said below
- context_len: int32 [256], P('wide'), may hold values from 128 to 1024, as said below
- adapter_id: int32 [256], P('wide'), may hold values from 0 to 127
- adapter_slot: int32 [128], replicated, may hold values from 0 to 127, each once
- query_key_value_down: bfloat16 [128, 8192, 192], P('wide', 'tensor'), may hold values from -0.0625 to 0.0625
- query_up_weight: bfloat16 [128, 64, 8192], P('wide', None, 'tensor'), may hold values from -0.75 to 0.75
- key_up_weight: bfloat16 [128, 64, 1024], P('wide', None, 'tensor'), may hold values from -0.75 to 0.75
- value_up_weight: bfloat16 [128, 64, 1024], P('wide', None, 'tensor'), may hold values from -0.75 to 0.75
- output_down_weight: bfloat16 [128, 8192, 64], P('wide', 'tensor'), may hold values from -0.0625 to 0.0625
- output_up_weight: bfloat16 [128, 64, 8192], P('wide', None, 'tensor'), may hold values from -0.75 to 0.75
Outputs:
- attention: bfloat16 [256, 8192], P('wide', 'tensor')
- output_adapter_term: bfloat16 [256, 8192], P('wide', 'tensor')
Inputs may be any that keep to these rules, and one draw needn't show every extreme that they name: `page_table`: the 8 entries of the rows of the 4 requests of one index of wide are distinct page numbers of that index's 32 pages. `context_len`: some request holds exactly 1024 positions.
All inputs are finite; a program needn't handle non-finite values.
Results may differ from a plain program's by a relative error of at most 0.01595.
Values may be sent and summed in bfloat16 or wider, within the bound.
No kernel may reach another device: no remote copies, remote signals or barrier semaphores. Data moves between devices by JAX's collectives and lax.ppermute only.
A program may use at most 64 MiB of HBM per device.

v0:
```python
import jax
import jax.numpy as jnp
from jax import lax
from jax.sharding import PartitionSpec as P

HEAD_SIZE = 128


adapter_scale = 2.0


def rounded_values(gathered_values):
    return lax.optimization_barrier(gathered_values.astype(jnp.bfloat16)).astype(jnp.float32)


def body(
    hidden,
    q_base,
    base_key,
    base_value,
    paged_key_cache,
    paged_value_cache,
    page_table,
    context_len,
    adapter_id,
    adapter_slot,
    query_key_value_down,
    query_up_weight,
    key_up_weight,
    value_up_weight,
    output_down_weight,
    output_up_weight,
):
    local_rows = hidden.shape[0]
    local_count = query_key_value_down.shape[0]
    all_ids = lax.all_gather(adapter_id, "wide", axis=0, tiled=True)
    lookup = jnp.arange(adapter_slot.shape[0], dtype=jnp.int32)
    slot_of = jnp.sum(
        jnp.where(all_ids[:, None] == lookup[None, :], adapter_slot[None, :], 0), axis=1
    )
    my_index = lax.axis_index("wide")
    first_slot = my_index * local_count
    owned_slots = first_slot + jnp.arange(local_count, dtype=jnp.int32)
    owned_mask = (slot_of[:, None] == owned_slots[None, :]).astype(jnp.float32)

    def grow_terms(rank_row_values, picked_adapters, up_weight_list):
        attention_outputs = []
        for number, up_weight_pages in enumerate(up_weight_list):
            rank_width = up_weight_pages.shape[1]
            selected = rank_row_values[:, number * rank_width : (number + 1) * rank_width]
            matrix_product = jnp.einsum(
                "nr,jro->njo", selected, up_weight_pages, preferred_element_type=jnp.float32
            )
            attention_outputs.append(
                jnp.sum(
                    rounded_values(adapter_scale * matrix_product) * picked_adapters[:, :, None],
                    axis=1,
                )
            )
        return jnp.concatenate(attention_outputs, axis=1)

    def owner_adapter(block_of_rows, down_weight_pages, up_weight_list):
        picked_adapters = owned_mask
        matrix_product = jnp.einsum(
            "nd,jdr->njr",
            lax.all_gather(block_of_rows, "wide", axis=0, tiled=True),
            down_weight_pages,
            preferred_element_type=jnp.float32,
        )
        partial_rank = jnp.sum(matrix_product * picked_adapters[:, :, None], axis=1)
        rank_row_values = lax.psum(partial_rank, "tensor").astype(jnp.bfloat16)
        picked_adapters = owned_mask
        return lax.psum_scatter(
            grow_terms(rank_row_values, picked_adapters, up_weight_list),
            "wide",
            scatter_dimension=0,
            tiled=True,
        )

    adapter_delta = owner_adapter(
        hidden, query_key_value_down, (query_up_weight, key_up_weight, value_up_weight)
    )
    width_q = q_base.shape[1]
    width_k = base_key.shape[1]
    query_vector = (q_base.astype(jnp.float32) + adapter_delta[:, 0:width_q]).astype(jnp.bfloat16)
    new_token_key = (
        base_key.astype(jnp.float32) + adapter_delta[:, width_q : width_q + width_k]
    ).astype(jnp.bfloat16)
    new_token_value = (
        base_value.astype(jnp.float32) + adapter_delta[:, width_q + width_k : width_q + 2 * width_k]
    ).astype(jnp.bfloat16)
    kv_local = width_k // HEAD_SIZE
    head_group = width_q // width_k
    gathered_keys = paged_key_cache[page_table].reshape(local_rows, -1, kv_local, HEAD_SIZE)
    gathered_values = paged_value_cache[page_table].reshape(local_rows, -1, kv_local, HEAD_SIZE)
    query_heads = query_vector.reshape(local_rows, kv_local, head_group, HEAD_SIZE)
    inverse = 1.0 / HEAD_SIZE**0.5
    scores = (
        jnp.einsum(
            "bkgd,btkd->bkgt", query_heads, gathered_keys, preferred_element_type=jnp.float32
        )
        * inverse
    )
    own_score = (
        jnp.einsum(
            "txvc,txc->txv",
            query_heads,
            new_token_key.reshape(local_rows, kv_local, HEAD_SIZE),
            preferred_element_type=jnp.float32,
        )
        * inverse
    )
    positions = jnp.arange(gathered_keys.shape[1], dtype=jnp.int32)
    live = (positions[None, :] < context_len[:, None])[:, None, None, :]
    scores = jnp.where(live, scores, jnp.float32(-1e30))
    top = jnp.maximum(jnp.max(scores, axis=-1), own_score)
    weights = jnp.where(live, jnp.exp(scores - top[..., None]), jnp.float32(0.0))
    own_weight = jnp.exp(own_score - top)
    total = jnp.sum(weights, axis=-1) + own_weight
    mixed = jnp.einsum(
        "bkgt,btkd->bkgd",
        weights.astype(jnp.bfloat16),
        gathered_values,
        preferred_element_type=jnp.float32,
    )
    fresh_wide = new_token_value.reshape(local_rows, kv_local, 1, HEAD_SIZE).astype(jnp.float32)
    mixed = mixed + rounded_values(own_weight)[..., None] * fresh_wide
    attention = (mixed / total[..., None]).reshape(local_rows, width_q).astype(jnp.bfloat16)
    output_adapter_term = owner_adapter(attention, output_down_weight, (output_up_weight,))
    return (attention, output_adapter_term.astype(jnp.bfloat16))


def solution(mesh):
    return jax.shard_map(
        body,
        mesh=mesh,
        in_specs=(
            P("wide", "tensor"),
            P("wide", "tensor"),
            P("wide", "tensor"),
            P("wide", "tensor"),
            P("wide", None, "tensor"),
            P("wide", None, "tensor"),
            P("wide", None),
            P("wide"),
            P("wide"),
            P(),
            P("wide", "tensor", None),
            P("wide", None, "tensor"),
            P("wide", None, "tensor"),
            P("wide", None, "tensor"),
            P("wide", "tensor", None),
            P("wide", None, "tensor"),
        ),
        out_specs=(P("wide", "tensor"), P("wide", "tensor")),
        check_vma=False,
    )
```

profile of v0, /device:TPU:6, one launch (start us, length us, event | category | flops | bytes accessed | tf_op | source)
XLA Modules:
  0.0 855.8 jit_solution(2734930860051340617)
XLA Ops:
  7.3 1.4 fusion.27
  9.3 0.9 dynamic-update-slice
  10.2 34.4 %all-reduce = s32[256]{0:T(256)S(1)} all-reduce(s32[256]{0:T(256)S(1)} %dynamic-update-slice), channel_id=1, replica_groups=mesh['wide'=64,'tensor'=8] {'wide'}, use_global_device_ids=true, to_apply=%add | all-reduce | flops 256 | bytes 2048
  44.6 97.4 %all-gather = bf16[64,4,1024]{2,1,0:T(4,128)(2,1)S(1)} all-gather(bf16[1,4,1024]{2,1,0:T(4,128)(2,1)} %bitcast.64), channel_id=1, replica_groups=mesh['wide'=64,'tensor'=8] {'wide'}, dimensions={0}, use_global_device_ids=true | all-gather | bytes 532480 | tf_op jit(solution)/shard_map/all_gather | solution.py:66
  141.9 0.1 reshape.154
  142.1 0.2 select_reduce_fusion
  142.4 0.4 fusion.29
  142.8 22.4 %all-reduce.8 = bf16[256,192]{0,1:T(8,128)(2,1)S(1)} all-reduce(f32[256,192]{0,1:T(8,128)S(1)} %multiply_reduce_fusion.2), channel_id=1, replica_groups=mesh['wide'=64,'tensor'=8] {'tensor'}, use_global_device_ids=true, to_apply=%region_2.3 | all-reduce | flops 49152 | bytes 294912 | tf_op jit(solution)/shard_map/psum | solution.py:71
  165.2 0.2 fusion
  165.4 0.2 fusion.1
  165.7 0.5 multiply_convert_fusion.1
  166.1 0.2 multiply_reduce_fusion.1
  166.3 0.1 multiply_reduce_fusion.4
  166.5 1.2 pad_maximum_fusion
  167.7 0.7 copy-done.8
  168.5 0.7 gather_fusion
  169.3 2.0 gather_fusion.1
  172.0 266.9 %all-reduce.7.cloned.1.call-done = f32[256,1280]{1,0:T(8,128)} async-done(((f32[256,1280]{1,0:T(8,128)}), f32[256,1280]{1,0:T(8,128)}) %all-reduce.7.cloned.1.call-update) | async-done | bytes 1310736
  438.9 0.8 fusion.14
  439.7 0.9 fusion.24
  440.7 0.5 fusion.28
  441.1 0.2 fusion.5
  441.4 0.3 fusion.4
  441.7 98.4 %all-gather.1 = bf16[64,4,1024]{2,1,0:T(4,128)(2,1)S(1)} all-gather(bf16[1,4,1024]{2,1,0:T(4,128)(2,1)S(1)} %reshape.155), channel_id=1, replica_groups=mesh['wide'=64,'tensor'=8] {'wide'}, dimensions={0}, use_global_device_ids=true | all-gather | bytes 532480 | tf_op jit(solution)/shard_map/all_gather | solution.py:66
  540.1 0.1 reshape.156
  540.3 0.3 fusion.30
  540.6 21.0 %psum.15 = bf16[256,64]{0,1:T(8,128)(2,1)S(1)} all-reduce(f32[256,64]{0,1:T(8,128)S(1)} %multiply_reduce_fusion.5), channel_id=1, replica_groups=mesh['wide'=64,'tensor'=8] {'tensor'}, use_global_device_ids=true, to_apply=%region_10.11 | all-reduce | flops 16384 | bytes 98304 | tf_op jit(solution)/shard_map/psum | solution.py:71
  561.6 0.5 multiply_convert_fusion
  562.1 0.2 multiply_reduce_fusion
  562.3 285.4 %all-reduce.9 = bf16[256,1024]{1,0:T(8,128)(2,1)S(1)} all-reduce(f32[256,1024]{1,0:T(8,128)S(1)} %multiply_reduce_fusion), channel_id=3, replica_groups=mesh['wide'=64,'tensor'=8] {'wide'}, use_global_device_ids=true, to_apply=%region_12.13.clone | all-reduce | flops 262144 | bytes 1572864
  847.8 0.6 dynamic-slice_convert_fusion
  848.4 0.6 copy.37
  (41 shorter events, 0.6 us)
Async XLA Ops:
  7.2 161.3 %copy-start = (bf16[32,128,128]{2,1,0:T(8,128)(2,1)S(1)}, bf16[32,128,128]{2,1,0:T(8,128)(2,1)}, u32[]{:S(2)}) copy-start(bf16[32,128,128]{2,1,0:T(8,128)(2,1)} %param.20) | copy-start | bytes 3145732
  7.2 134.9 %copy-start.11 = (s32[128]{0:T(128)S(1)}, s32[128]{0:T(128)}, u32[]{:S(2)}) copy-start(s32[128]{0:T(128)} %param.25) | copy-start | bytes 1540
  7.2 135.2 %copy-start.1 = (bf16[2,1024,192]{1,2,0:T(8,128)(2,1)S(1)}, bf16[2,1024,192]{1,2,0:T(8,128)(2,1)}, u32[]{:S(2)}) copy-start(bf16[2,1024,192]{1,2,0:T(8,128)(2,1)} %param.26) | copy-start | bytes 2359300
  7.2 431.7 %all-reduce.7.cloned.1.call-start = ((), (), s32[]{:S(2)}) async-start(), calls=%async_computation | async-start | bytes 2621440
  142.1 23.1 %copy-start.5 = (bf16[2,64,128]{2,1,0:T(8,128)(2,1)S(1)}, bf16[2,64,128]{2,1,0:T(8,128)(2,1)}, u32[]{:S(2)}) copy-start(bf16[2,64,128]{2,1,0:T(8,128)(2,1)} %param.28) | copy-start | bytes 98308
  142.3 23.1 %copy-start.6 = (bf16[2,64,128]{2,1,0:T(8,128)(2,1)S(1)}, bf16[2,64,128]{2,1,0:T(8,128)(2,1)}, u32[]{:S(2)}) copy-start(bf16[2,64,128]{2,1,0:T(8,128)(2,1)} %param.29) | copy-start | bytes 98308
  142.4 23.3 %copy-start.3 = (bf16[2,64,1024]{2,1,0:T(8,128)(2,1)S(1)}, bf16[2,64,1024]{2,1,0:T(8,128)(2,1)}, u32[]{:S(2)}) copy-start(bf16[2,64,1024]{2,1,0:T(8,128)(2,1)} %param.27) | copy-start | bytes 786436
  167.7 0.7 copy-start.8
  169.2 2.7 copy-start.12
  169.2 269.7 %copy-start.7 = (bf16[4,1024]{1,0:T(4,128)(2,1)S(1)}, bf16[4,1024]{1,0:T(4,128)(2,1)}, u32[]{:S(2)}) copy-start(bf16[4,1024]{1,0:T(4,128)(2,1)} %param.17) | copy-start | bytes 24580
  169.2 270.4 %copy-start.9 = (bf16[4,128]{1,0:T(4,128)(2,1)S(1)}, bf16[4,128]{1,0:T(4,128)(2,1)}, u32[]{:S(2)}) copy-start(bf16[4,128]{1,0:T(4,128)(2,1)} %param.19) | copy-start | bytes 3076
  169.3 270.4 %copy-start.10 = (bf16[4,128]{1,0:T(4,128)(2,1)S(1)}, bf16[4,128]{1,0:T(4,128)(2,1)}, u32[]{:S(2)}) copy-start(bf16[4,128]{1,0:T(4,128)(2,1)} %param.18) | copy-start | bytes 3076
  441.4 98.9 %copy-start.2 = (bf16[2,1024,64]{1,2,0:T(8,128)(2,1)S(1)}, bf16[2,1024,64]{1,2,0:T(8,128)(2,1)}, u32[]{:S(2)}) copy-start(bf16[2,1024,64]{1,2,0:T(8,128)(2,1)} %param.30) | copy-start | bytes 786436
  441.7 119.9 %copy-start.4 = (bf16[2,64,1024]{2,1,0:T(8,128)(2,1)S(1)}, bf16[2,64,1024]{2,1,0:T(8,128)(2,1)}, u32[]{:S(2)}) copy-start(bf16[2,64,1024]{2,1,0:T(8,128)(2,1)} %param.31) | copy-start | bytes 786436
Sparse Core Ops, SparseCore 0:
  167.8 271.0 all-reduce.6
where the time goes:
time: 856 us
  blocking collectives  559 us (65%)
  waiting for transfers between devices  267 us (31%)
  between operations  15.6 us (2%)
    unnamed x2, blocking collectives  320 us
    unnamed x2, waiting for transfers between devices  267 us
    all_gather x2, blocking collectives, owner_adapter(): lax.all_gather(block_of_rows, 'wide', axis=0, tiled=True)  196 us
    psum x2, blocking collectives, owner_adapter(): rank_row_values = lax.psum(partial_rank, 'tensor').astype(jnp.bfloat16)  43.4 us
  transfers between devices with their start and end apart: 1, of which 1 were waited for; matrix products, arithmetic and copies ran while one was open for 0% of the time, Pallas kernels for 0%

commit v1 on v0

v1 whole, which is shorter than its diff:
```python
import jax
import jax.numpy as jnp
import numpy as np
from jax import lax
from jax.sharding import Mesh, PartitionSpec as P

HEAD_SIZE = 128
adapter_scale = 2.0
Y, Z, T = "y", "z", "tensor"


def rounded_values(values):
    return lax.optimization_barrier(values.astype(jnp.bfloat16)).astype(jnp.float32)


def exchange(blocks, axis):
    return lax.all_to_all(blocks, axis, 0, 0)


def spread(block, axis):
    copies = jnp.broadcast_to(block[None], (lax.axis_size(axis),) + block.shape)
    return exchange(copies, axis)


def partial_ranks(rows, weight_pages, mask):
    product = jnp.einsum("nd,jdr->njr", rows, weight_pages, preferred_element_type=jnp.float32)
    return jnp.sum(product * mask[:, :, None], axis=1)


def summed(parts):
    return jnp.sum(parts.astype(jnp.float32), axis=0)


def up(ranks, weight_pages, mask):
    count, rank, width = weight_pages.shape
    picked = (ranks[:, None, :] * mask.astype(jnp.bfloat16)[:, :, None]).reshape(-1, count * rank)
    product = jnp.dot(
        picked, weight_pages.reshape(count * rank, width), preferred_element_type=jnp.float32
    )
    return (adapter_scale * product).astype(jnp.bfloat16)


def to_requests(rows):
    return summed(exchange(rows.reshape(lax.axis_size(Z), -1, rows.shape[1]), Z))


def body(
    hidden,
    q_base,
    base_key,
    base_value,
    paged_key_cache,
    paged_value_cache,
    page_table,
    context_len,
    adapter_id,
    adapter_slot,
    query_key_value_down,
    query_up_weight,
    key_up_weight,
    value_up_weight,
    output_down_weight,
    output_up_weight,
):
    local_rows, local_width = hidden.shape
    local_count = query_key_value_down.shape[0]
    lookup = jnp.arange(adapter_slot.shape[0], dtype=jnp.int32)
    own_slots = jnp.sum(
        jnp.where(adapter_id[:, None] == lookup[None, :], adapter_slot[None, :], 0), axis=1
    )
    tags = jnp.broadcast_to(own_slots.astype(jnp.bfloat16)[:, None], (local_rows, 128))
    column = [
        lax.all_gather(weight, Y, axis=0, tiled=True)
        for weight in (query_up_weight, key_up_weight, value_up_weight, output_down_weight, output_up_weight)
    ]
    y_size, z_size, t_size = lax.axis_size(Y), lax.axis_size(Z), lax.axis_size(T)
    z_rows = spread(jnp.concatenate([hidden, tags], axis=1), Z).reshape(z_size * local_rows, -1)
    all_rows = spread(z_rows, Y).reshape(y_size * z_size * local_rows, -1)

    numbers = jnp.arange(local_count, dtype=jnp.int32)
    first = lax.axis_index(Z) * local_count
    owned_slots = lax.axis_index(Y) * z_size * local_count + first + numbers
    column_slots = (
        jnp.arange(y_size, dtype=jnp.int32)[:, None] * (z_size * local_count) + first + numbers[None, :]
    ).reshape(-1)
    all_slots = all_rows[:, local_width].astype(jnp.int32)
    owned_mask = (all_slots[:, None] == owned_slots[None, :]).astype(jnp.float32)
    z_slots = z_rows[:, local_width].astype(jnp.int32)
    column_mask = (z_slots[:, None] == column_slots[None, :]).astype(jnp.float32)

    part = partial_ranks(all_rows[:, :local_width], query_key_value_down, owned_mask)
    share = z_size * local_rows // t_size
    shares = exchange(part.reshape(y_size * t_size, share, -1), (Y, T))
    ranks = spread(summed(shares).astype(jnp.bfloat16), T).reshape(z_size * local_rows, -1)
    width = query_up_weight.shape[1]
    delta = jnp.concatenate(
        [up(ranks[:, i * width : (i + 1) * width], column[i], column_mask) for i in range(3)],
        axis=1,
    )
    adapter_delta = to_requests(delta)
    width_q = q_base.shape[1]
    width_k = base_key.shape[1]
    query_vector = (q_base.astype(jnp.float32) + adapter_delta[:, 0:width_q]).astype(jnp.bfloat16)
    new_token_key = (
        base_key.astype(jnp.float32) + adapter_delta[:, width_q : width_q + width_k]
    ).astype(jnp.bfloat16)
    new_token_value = (
        base_value.astype(jnp.float32) + adapter_delta[:, width_q + width_k : width_q + 2 * width_k]
    ).astype(jnp.bfloat16)
    kv_local = width_k // HEAD_SIZE
    head_group = width_q // width_k
    gathered_keys = paged_key_cache[page_table].reshape(local_rows, -1, kv_local, HEAD_SIZE)
    gathered_values = paged_value_cache[page_table].reshape(local_rows, -1, kv_local, HEAD_SIZE)
    query_heads = query_vector.reshape(local_rows, kv_local, head_group, HEAD_SIZE)
    inverse = 1.0 / HEAD_SIZE**0.5
    scores = (
        jnp.einsum(
            "bkgd,btkd->bkgt", query_heads, gathered_keys, preferred_element_type=jnp.float32
        )
        * inverse
    )
    own_score = (
        jnp.einsum(
            "txvc,txc->txv",
            query_heads,
            new_token_key.reshape(local_rows, kv_local, HEAD_SIZE),
            preferred_element_type=jnp.float32,
        )
        * inverse
    )
    positions = jnp.arange(gathered_keys.shape[1], dtype=jnp.int32)
    live = (positions[None, :] < context_len[:, None])[:, None, None, :]
    scores = jnp.where(live, scores, jnp.float32(-1e30))
    top = jnp.maximum(jnp.max(scores, axis=-1), own_score)
    weights = jnp.where(live, jnp.exp(scores - top[..., None]), jnp.float32(0.0))
    own_weight = jnp.exp(own_score - top)
    total = jnp.sum(weights, axis=-1) + own_weight
    mixed = jnp.einsum(
        "bkgt,btkd->bkgd",
        weights.astype(jnp.bfloat16),
        gathered_values,
        preferred_element_type=jnp.float32,
    )
    fresh_wide = new_token_value.reshape(local_rows, kv_local, 1, HEAD_SIZE).astype(jnp.float32)
    mixed = mixed + rounded_values(own_weight)[..., None] * fresh_wide
    attention = (mixed / total[..., None]).reshape(local_rows, width_q).astype(jnp.bfloat16)
    out_rows = spread(attention, Z).reshape(z_size * local_rows, -1)
    out_ranks = summed(spread(partial_ranks(out_rows, column[3], column_mask), T))
    output_adapter_term = to_requests(up(out_ranks.astype(jnp.bfloat16), column[4], column_mask))
    return (attention, output_adapter_term.astype(jnp.bfloat16))


def solution(mesh):
    chips_y = 4
    wide, tensor = mesh.devices.shape
    devices = np.asarray(mesh.devices).reshape(chips_y, wide // chips_y, tensor)
    W = (Y, Z)
    return jax.shard_map(
        body,
        mesh=Mesh(devices, (Y, Z, T)),
        in_specs=(
            P(W, T),
            P(W, T),
            P(W, T),
            P(W, T),
            P(W, None, T),
            P(W, None, T),
            P(W, None),
            P(W),
            P(W),
            P(),
            P(W, T, None),
            P(W, None, T),
            P(W, None, T),
            P(W, None, T),
            P(W, T, None),
            P(W, None, T),
        ),
        out_specs=(P(W, T), P(W, T)),
        check_vma=False,
    )
```

time: 856 us -> 186 us (0.22)
  blocking collectives: 559 us -> 70.7 us
  waiting for transfers between devices: 267 us -> 40 us
  starting transfers between devices: 0.04 us -> 40.8 us
    unnamed x2 -> x0, blocking collectives: 320 us -> none
    unnamed x2 -> x3, waiting for transfers between devices: 267 us -> 2.05 us
    all_gather x2, blocking collectives: 196 us -> 25.5 us  [body(): lax.all_gather(weight, Y, axis=0, tiled=True)]
    all_to_all x0 -> x3, blocking collectives: none -> 45.2 us  [exchange(): return lax.all_to_all(blocks, axis, 0, 0)]
    psum x2 -> x0, blocking collectives: 43.4 us -> none  [owner_adapter(): rank_row_values = lax.psum(partial_rank, 'tensor').astype(jnp.bfloat16)]
    all_to_all x0 -> x5, starting transfers between devices: none -> 40.7 us  [exchange(): return lax.all_to_all(blocks, axis, 0, 0)]
    all_to_all x0 -> x5, waiting for transfers between devices: none -> 37.9 us  [exchange(): return lax.all_to_all(blocks, axis, 0, 0)]
  transfers between devices with their start and end apart: 1 -> 8, of which waited for: 1 -> 4; matrix products, arithmetic and copies ran while one was open for 0% -> 8% of each run, Pallas kernels for 0% -> 0%
where the time goes in v1:
time: 186 us; the launch traced here: 184 us
  blocking collectives  70.7 us (38%)
  starting transfers between devices  40.8 us (22%)
  waiting for transfers between devices  40 us (22%)
  between operations  14.1 us (8%)
  local copies, waits for them, and re-layouts  9.08 us (5%)
  matrix products  6.99 us (4%)
  other arithmetic  2.78 us (1%)
    all_to_all x3, blocking collectives, exchange(): return lax.all_to_all(blocks, axis, 0, 0)  45.2 us
    all_to_all x5, starting transfers between devices, exchange(): return lax.all_to_all(blocks, axis, 0, 0)  40.7 us
    all_to_all x5, waiting for transfers between devices, exchange(): return lax.all_to_all(blocks, axis, 0, 0)  37.9 us
    all_gather x2, blocking collectives, body(): lax.all_gather(weight, Y, axis=0, tiled=True)  25.5 us
    dot_general x4, matrix products, up(): jnp.dot(picked, weight_pages.reshape(count * rank, width), preferred_elem...  3.84 us
  transfers between devices with their start and end apart: 8, of which 4 were waited for; matrix products, arithmetic and copies ran while one was open for 8% of the time, Pallas kernels for 0%

profile of v1, /device:TPU:6, one launch (start us, length us, event | category | flops | bytes accessed | tf_op | source)
XLA Modules:
  0.0 184.5 jit_solution(961123086343019621)
XLA Ops:
  7.3 0.7 all-gather.4.cloned.1.call-update
  8.2 0.7 broadcast_in_dim.46
  9.0 15.2 %all-to-all-start = ((bf16[16,4,1152]{2,1,0:T(4,128)(2,1)}), bf16[16,4,1152]{2,1,0:T(4,128)(2,1)S(1)}, u32[]{:S(2)}, u32[]{:S(2)}) async-start(bf16[16,4,1152]{2,1,0:T(4,128)(2,1)} %broadcast_in_dim.46), calls=%async_computation | async-start | bytes 294912 | tf_op jit(solution)/shard_map/all_to_all | solution.py:17
  24.2 0.7 all-gather.6.cloned.1.call-update
  24.9 14.4 %all-to-all-done = bf16[16,4,1152]{2,1,0:T(4,128)(2,1)S(1)} async-done(((bf16[16,4,1152]{2,1,0:T(4,128)(2,1)}), bf16[16,4,1152]{2,1,0:T(4,128)(2,1)S(1)}, u32[]{:S(2)}, u32[]{:S(2)}) %all-to-all-start) | async-done | bytes 147488 | tf_op jit(solution)/shard_map/all_to_all | solution.py:17
  39.3 0.9 broadcast_in_dim.52
  40.2 4.6 %all-to-all-start.1 = ((bf16[4,64,1152]{2,1,0:T(8,128)(2,1)}), bf16[4,64,1152]{2,1,0:T(8,128)(2,1)S(1)}, u32[]{:S(2)}, u32[]{:S(2)}) async-start(bf16[4,64,1152]{2,1,0:T(8,128)(2,1)} %broadcast_in_dim.52), calls=%async_computation.1 | async-start | bytes 1179648 | tf_op jit(solution)/shard_map/all_to_all | solution.py:17
  44.9 8.4 %all-to-all-done.1 = bf16[4,64,1152]{2,1,0:T(8,128)(2,1)S(1)} async-done(((bf16[4,64,1152]{2,1,0:T(8,128)(2,1)}), bf16[4,64,1152]{2,1,0:T(8,128)(2,1)S(1)}, u32[]{:S(2)}, u32[]{:S(2)}) %all-to-all-start.1) | async-done | bytes 589856 | tf_op jit(solution)/shard_map/all_to_all | solution.py:17
  53.9 0.9 copy.23
  54.7 5.7 %all-to-all-start.2 = ((f32[32,8,192]{2,1,0:T(8,128)}), f32[32,8,192]{2,1,0:T(8,128)S(1)}, u32[]{:S(2)}, u32[]{:S(2)}) async-start(f32[32,8,192]{2,1,0:T(8,128)} %bitcast.4), calls=%async_computation.2 | async-start | bytes 524288 | tf_op jit(solution)/shard_map/all_to_all | solution.py:17
  60.4 13.4 %all_gather.16 = bf16[8,64,128]{2,1,0:T(8,128)(2,1)S(1)} all-gather(bf16[2,64,128]{2,1,0:T(8,128)(2,1)S(1)} %copy-done.2), channel_id=1, replica_groups=mesh['y'=4,'z'=16,'tensor'=8] {'y'}, dimensions={0}, use_global_device_ids=true | all-gather | bytes 163840 | tf_op jit(solution)/shard_map/all_gather | solution.py:73
  73.8 12.1 %all_gather.17 = bf16[8,64,128]{2,1,0:T(8,128)(2,1)S(1)} all-gather(bf16[2,64,128]{2,1,0:T(8,128)(2,1)S(1)} %copy-done.3), channel_id=1, replica_groups=mesh['y'=4,'z'=16,'tensor'=8] {'y'}, dimensions={0}, use_global_device_ids=true | all-gather | bytes 163840 | tf_op jit(solution)/shard_map/all_gather | solution.py:73
  86.1 0.6 broadcast_in_dim.53
  86.8 4.6 %all-to-all-start.3 = ((bf16[8,8,192]{2,1,0:T(8,128)(2,1)}), bf16[8,8,192]{2,1,0:T(8,128)(2,1)S(1)}, u32[]{:S(2)}, u32[]{:S(2)}) async-start(bf16[8,8,192]{2,1,0:T(8,128)(2,1)} %broadcast_in_dim.53), calls=%async_computation.3 | async-start | bytes 65536 | tf_op jit(solution)/shard_map/all_to_all | solution.py:17
  91.4 3.3 %all-to-all-done.3 = bf16[8,8,192]{2,1,0:T(8,128)(2,1)S(1)} async-done(((bf16[8,8,192]{2,1,0:T(8,128)(2,1)}), bf16[8,8,192]{2,1,0:T(8,128)(2,1)S(1)}, u32[]{:S(2)}, u32[]{:S(2)}) %all-to-all-start.3) | async-done | bytes 24608 | tf_op jit(solution)/shard_map/all_to_all | solution.py:17
  95.4 1.6 fusion.2
  97.1 0.7 reshape.258
  97.8 10.7 %all-to-all-start.4 = ((bf16[16,4,1280]{2,1,0:T(4,128)(2,1)}), bf16[16,4,1280]{2,1,0:T(4,128)(2,1)S(1)}, u32[]{:S(2)}, u32[]{:S(2)}) async-start(bf16[16,4,1280]{2,1,0:T(4,128)(2,1)} %reshape.258), calls=%async_computation.4 | async-start | bytes 327680 | tf_op jit(solution)/shard_map/all_to_all | solution.py:17
  108.6 0.7 all-gather.8.cloned.1.call-update
  109.4 0.7 gather_fusion
  110.1 2.0 %gather_fusion.1 = bf16[32,128,128]{2,1,0:T(8,128)(2,1)S(1)} fusion(bf16[32,128,128]{2,1,0:T(8,128)(2,1)} %param.21, s32[1024]{0:T(1024)S(1)} %pad_clamp_fusion), kind=kCustom, calls=%fused_computation.1 | custom fusion | bytes 2097280 | tf_op jit(solution)/shard_map/gather | solution.py:113
  112.2 11.8 %all-to-all-done.4 = bf16[16,4,1280]{2,1,0:T(4,128)(2,1)S(1)} async-done(((bf16[16,4,1280]{2,1,0:T(4,128)(2,1)}), bf16[16,4,1280]{2,1,0:T(4,128)(2,1)S(1)}, u32[]{:S(2)}, u32[]{:S(2)}) %all-to-all-start.4) | async-done | bytes 163872 | tf_op jit(solution)/shard_map/all_to_all | solution.py:17
  124.2 0.6 copy-done.8
  126.0 0.5 copy-done.4
  126.6 18.5 %all_to_all.40 = bf16[16,4,1024]{2,1,0:T(4,128)(2,1)S(1)} all-to-all(bf16[16,4,1024]{2,1,0:T(4,128)(2,1)S(1)} %broadcast_in_dim.57), channel_id=1, replica_groups=mesh['y'=4,'z'=16,'tensor'=8] {'z'}, dimensions={0} | all-to-all | bytes 262144 | tf_op jit(solution)/shard_map/all_to_all | solution.py:17
  145.2 1.9 %fusion.4 = f32[64,64]{1,0:T(8,128)S(1)} fusion(bf16[64,1024,1]{1,0,2:T(8,128)(2,1)S(1)} %reshape.296, bf16[8,1024,64]{1,2,0:T(8,128)(2,1)} %all-gather.6.cloned.1.call-done, f32[64,8]{0,1:T(8,128)S(1)} %get-tuple-element.9), kind=kOutput, calls=%fused_computation.9 | convolution fusion | flops 67170304 | bytes 1198080 | tf_op jit(solution)/shard_map/nd,jdr->njr/dot_general | solution.py:26
  147.3 8.5 %all_to_all.41 = f32[8,1,4096]{2,1,0:T(1,128)S(1)} all-to-all(f32[8,1,4096]{2,1,0:T(1,128)S(1)} %reshape.301), channel_id=1, replica_groups=mesh['y'=4,'z'=16,'tensor'=8] {'tensor'}, dimensions={0} | all-to-all | bytes 262144 | tf_op jit(solution)/shard_map/all_to_all | solution.py:17
  155.8 0.5 broadcast.145
  156.3 1.0 reduce.9
  157.4 1.6 fusion.3
  159.1 18.1 %all_to_all.42 = bf16[16,4,1024]{2,1,0:T(4,128)(2,1)S(1)} all-to-all(bf16[16,4,1024]{2,1,0:T(4,128)(2,1)S(1)} %reshape.263), channel_id=1, replica_groups=mesh['y'=4,'z'=16,'tensor'=8] {'z'}, dimensions={0} | all-to-all | bytes 262144 | tf_op jit(solution)/shard_map/all_to_all | solution.py:17
  177.3 0.7 reduce_sum.82
  (73 shorter events, 4.1 us)
Async XLA Ops:
  7.2 102.2 %copy-start = (bf16[32,128,128]{2,1,0:T(8,128)(2,1)S(1)}, bf16[32,128,128]{2,1,0:T(8,128)(2,1)}, u32[]{:S(2)}) copy-start(bf16[32,128,128]{2,1,0:T(8,128)(2,1)} %param.20) | copy-start | bytes 3145732
  7.2 0.8 copy-start.11
  7.2 0.8 copy-start.12
  7.2 88.2 %all-gather.4.cloned.1.call-start = ((), (), s32[]{:S(2)}) async-start(), calls=%async_computation.8 | async-start | bytes 1310720 | tf_op jit(solution)/shard_map/all_gather | solution.py:73
  7.2 1.0 copy-start.5
  9.0 30.3 %all-to-all-start = ((bf16[16,4,1152]{2,1,0:T(4,128)(2,1)}), bf16[16,4,1152]{2,1,0:T(4,128)(2,1)S(1)}, u32[]{:S(2)}, u32[]{:S(2)}) async-start(bf16[16,4,1152]{2,1,0:T(4,128)(2,1)} %broadcast_in_dim.46), calls=%async_computation | async-start | bytes 294912 | tf_op jit(solution)/shard_map/all_to_all | solution.py:17
  24.2 121.0 %all-gather.6.cloned.1.call-start = ((), (), s32[]{:S(2)}) async-start(), calls=%async_computation.9 | async-start | bytes 1310720 | tf_op jit(solution)/shard_map/all_gather | solution.py:73
  40.2 13.2 %copy-start.1 = (bf16[2,1024,192]{1,2,0:T(8,128)(2,1)S(1)}, bf16[2,1024,192]{1,2,0:T(8,128)(2,1)}, u32[]{:S(2)}) copy-start(bf16[2,1024,192]{1,2,0:T(8,128)(2,1)} %param.26) | copy-start | bytes 2359300
  40.2 13.0 %all-to-all-start.1 = ((bf16[4,64,1152]{2,1,0:T(8,128)(2,1)}), bf16[4,64,1152]{2,1,0:T(8,128)(2,1)S(1)}, u32[]{:S(2)}, u32[]{:S(2)}) async-start(bf16[4,64,1152]{2,1,0:T(8,128)(2,1)} %broadcast_in_dim.52), calls=%async_computation.1 | async-start | bytes 1179648 | tf_op jit(solution)/shard_map/all_to_all | solution.py:17
  54.7 5.7 %copy-start.2 = (bf16[2,64,128]{2,1,0:T(8,128)(2,1)S(1)}, bf16[2,64,128]{2,1,0:T(8,128)(2,1)}, u32[]{:S(2)}) copy-start(bf16[2,64,128]{2,1,0:T(8,128)(2,1)} %param.28) | copy-start | bytes 98308
  54.7 31.4 %all-to-all-start.2 = ((f32[32,8,192]{2,1,0:T(8,128)}), f32[32,8,192]{2,1,0:T(8,128)S(1)}, u32[]{:S(2)}, u32[]{:S(2)}) async-start(f32[32,8,192]{2,1,0:T(8,128)} %bitcast.4), calls=%async_computation.2 | async-start | bytes 524288 | tf_op jit(solution)/shard_map/all_to_all | solution.py:17
  60.4 13.4 %copy-start.3 = (bf16[2,64,128]{2,1,0:T(8,128)(2,1)S(1)}, bf16[2,64,128]{2,1,0:T(8,128)(2,1)}, u32[]{:S(2)}) copy-start(bf16[2,64,128]{2,1,0:T(8,128)(2,1)} %param.29) | copy-start | bytes 98308
  86.8 8.0 %all-to-all-start.3 = ((bf16[8,8,192]{2,1,0:T(8,128)(2,1)}), bf16[8,8,192]{2,1,0:T(8,128)(2,1)S(1)}, u32[]{:S(2)}, u32[]{:S(2)}) async-start(bf16[8,8,192]{2,1,0:T(8,128)(2,1)} %broadcast_in_dim.53), calls=%async_computation.3 | async-start | bytes 65536 | tf_op jit(solution)/shard_map/all_to_all | solution.py:17
  97.8 26.3 %all-to-all-start.4 = ((bf16[16,4,1280]{2,1,0:T(4,128)(2,1)}), bf16[16,4,1280]{2,1,0:T(4,128)(2,1)S(1)}, u32[]{:S(2)}, u32[]{:S(2)}) async-start(bf16[16,4,1280]{2,1,0:T(4,128)(2,1)} %reshape.258), calls=%async_computation.4 | async-start | bytes 327680 | tf_op jit(solution)/shard_map/all_to_all | solution.py:17
  108.5 0.8 copy-start.7
  108.5 48.9 %all-gather.8.cloned.1.call-start = ((), (), s32[]{:S(2)}) async-start(), calls=%async_computation.10 | async-start | bytes 1310720 | tf_op jit(solution)/shard_map/all_gather | solution.py:73
  110.1 2.0 %copy-start.10 = (s32[4]{0:T(128)S(1)}, s32[4]{0:T(128)}, u32[]{:S(2)}) copy-start(s32[4]{0:T(128)} %param.23) | copy-start | bytes 52
  112.2 11.9 %copy-start.6 = (bf16[4,1024]{1,0:T(4,128)(2,1)S(1)}, bf16[4,1024]{1,0:T(4,128)(2,1)}, u32[]{:S(2)}) copy-start(bf16[4,1024]{1,0:T(4,128)(2,1)} %param.17) | copy-start | bytes 24580
  124.1 0.7 copy-start.8
  124.2 0.7 copy-start.9
  126.0 0.6 copy-start.4
Sparse Core Ops, SparseCore 0:
  10.1 36.3 all-gather.3
  48.6 35.3 all-gather.5
  111.5 31.1 all-gather.7

commit v2 on v1

--- a/solution.py
+++ b/solution.py
@@ -69,32 +69,46 @@
         jnp.where(adapter_id[:, None] == lookup[None, :], adapter_slot[None, :], 0), axis=1
     )
     tags = jnp.broadcast_to(own_slots.astype(jnp.bfloat16)[:, None], (local_rows, 128))
-    column = [
+    y_size, z_size = lax.axis_size(Y), lax.axis_size(Z)
+    pages = [query_key_value_down] + [
+        lax.ppermute(query_key_value_down, Y, [(i, (i + k) % y_size) for i in range(y_size)])
+        for k in range(1, y_size)
+    ]
+    up_weights = jnp.concatenate([query_up_weight, key_up_weight, value_up_weight], axis=2)
+    column_up, column_out_down, column_out_up = [
         lax.all_gather(weight, Y, axis=0, tiled=True)
-        for weight in (query_up_weight, key_up_weight, value_up_weight, output_down_weight, output_up_weight)
+        for weight in (up_weights, output_down_weight, output_up_weight)
     ]
-    y_size, z_size, t_size = lax.axis_size(Y), lax.axis_size(Z), lax.axis_size(T)
     z_rows = spread(jnp.concatenate([hidden, tags], axis=1), Z).reshape(z_size * local_rows, -1)
-    all_rows = spread(z_rows, Y).reshape(y_size * z_size * local_rows, -1)
+    z_slots = z_rows[:, local_width].astype(jnp.int32)
+    own_y = lax.axis_index(Y)
 
-    numbers = jnp.arange(local_count, dtype=jnp.int32)
-    first = lax.axis_index(Z) * local_count
-    owned_slots = lax.axis_index(Y) * z_size * local_count + first + numbers
-    column_slots = (
-        jnp.arange(y_size, dtype=jnp.int32)[:, None] * (z_size * local_count) + first + numbers[None, :]
-    ).reshape(-1)
-    all_slots = all_rows[:, local_width].astype(jnp.int32)
-    owned_mask = (all_slots[:, None] == owned_slots[None, :]).astype(jnp.float32)
-    z_slots = z_rows[:, local_width].astype(jnp.int32)
-    column_mask = (z_slots[:, None] == column_slots[None, :]).astype(jnp.float32)
+    def mask_of(y):
+        numbers = jnp.arange(local_count, dtype=jnp.int32)
+        slots = (y[:, None] * z_size + lax.axis_index(Z)) * local_count + numbers[None, :]
+        return (z_slots[:, None] == slots.reshape(-1)[None, :]).astype(jnp.float32)
 
-    part = partial_ranks(all_rows[:, :local_width], query_key_value_down, owned_mask)
-    share = z_size * local_rows // t_size
-    shares = exchange(part.reshape(y_size * t_size, share, -1), (Y, T))
-    ranks = spread(summed(shares).astype(jnp.bfloat16), T).reshape(z_size * local_rows, -1)
-    width = query_up_weight.shape[1]
+    places = jnp.arange(y_size, dtype=jnp.int32)
+    column_mask = mask_of(places)
+    shifted_mask = mask_of((own_y - places) % y_size)
+    part = sum(
+        partial_ranks(
+            z_rows[:, :local_width], page, shifted_mask[:, k * local_count : (k + 1) * local_count]
+        )
+        for k, page in enumerate(pages)
+    )
+    ranks = summed(spread(part, T)).astype(jnp.bfloat16)
+    width, width_q, width_k = query_up_weight.shape[1], q_base.shape[1], base_key.shape[1]
+    cuts = (0, width_q, width_q + width_k, width_q + 2 * width_k)
     delta = jnp.concatenate(
-        [up(ranks[:, i * width : (i + 1) * width], column[i], column_mask) for i in range(3)],
+        [
+            up(
+                ranks[:, i * width : (i + 1) * width],
+                column_up[:, :, cuts[i] : cuts[i + 1]],
+                column_mask,
+            )
+            for i in range(3)
+        ],
         axis=1,
     )
     adapter_delta = to_requests(delta)
@@ -145,8 +159,8 @@
     mixed = mixed + rounded_values(own_weight)[..., None] * fresh_wide
     attention = (mixed / total[..., None]).reshape(local_rows, width_q).astype(jnp.bfloat16)
     out_rows = spread(attention, Z).reshape(z_size * local_rows, -1)
-    out_ranks = summed(spread(partial_ranks(out_rows, column[3], column_mask), T))
-    output_adapter_term = to_requests(up(out_ranks.astype(jnp.bfloat16), column[4], column_mask))
+    out_ranks = summed(spread(partial_ranks(out_rows, column_out_down, column_mask), T))
+    output_adapter_term = to_requests(up(out_ranks.astype(jnp.bfloat16), column_out_up, column_mask))
     return (attention, output_adapter_term.astype(jnp.bfloat16))
 
 

time: 186 us -> 173 us (0.930)
  the two profiles are of different devices: /device:TPU:6 before, /device:TPU:8 now
where the time goes in v2:
time: 173 us; the launch traced here: 172 us
  blocking collectives  59.7 us (35%)
  starting transfers between devices  41.2 us (24%)
  waiting for transfers between devices  31.5 us (18%)
  between operations  14.1 us (8%)
  matrix products  11.1 us (6%)
  local copies, waits for them, and re-layouts  7.53 us (4%)
  other arithmetic  7.1 us (4%)
    all_to_all x4, blocking collectives, exchange(): return lax.all_to_all(blocks, axis, 0, 0)  59.7 us
    all_to_all x2, starting transfers between devices, exchange(): return lax.all_to_all(blocks, axis, 0, 0)  27.4 us
    all_to_all x2, waiting for transfers between devices, exchange(): return lax.all_to_all(blocks, axis, 0, 0)  23.8 us
    ppermute x3, starting transfers between devices, body(): lax.ppermute(query_key_value_down, Y, [(i, (i + k) % y_size) for i in ran...  13.6 us
    ppermute x3, waiting for transfers between devices, body(): lax.ppermute(query_key_value_down, Y, [(i, (i + k) % y_size) for i in ran...  6.26 us
    dot_general x4, matrix products, up(): jnp.dot(picked, weight_pages.reshape(count * rank, width), preferred_elem...  5.68 us
    dot_general x5, matrix products, partial_ranks(): jnp.einsum('nd,jdr->njr', rows, weight_pages, preferred_element_type=jnp....  4.51 us
  transfers between devices with their start and end apart: 8, of which 3 were waited for; matrix products, arithmetic and copies ran while one was open for 12% of the time, Pallas kernels for 0%

profile of v2, /device:TPU:8, one launch (start us, length us, event | category | flops | bytes accessed | tf_op | source)
XLA Modules:
  0.0 172.2 jit_solution(10445519992597221193)
XLA Ops:
  7.2 1.9 %pad_maximum_fusion = bf16[2,64,1280]{2,1,0:T(8,128)(2,1)} fusion(bf16[2,64,128]{2,1,0:T(8,128)(2,1)} %param.29, bf16[2,64,128]{2,1,0:T(8,128)(2,1)} %param.28, bf16[2,64,1024]{2,1,0:T(8,128)(2,1)} %param.27), kind=kLoop, calls=%fused_computation.31 | loop fusion | flops 983040 | bytes 655360 | tf_op jit(solution)/shard_map/concatenate | solution.py:77
  9.1 3.5 %collective-permute-start = (bf16[2,1024,192]{1,2,0:T(8,128)(2,1)}, bf16[2,1024,192]{1,2,0:T(8,128)(2,1)}, u32[]{:S(2)}, u32[]{:S(2)}) collective-permute-start(bf16[2,1024,192]{1,2,0:T(8,128)(2,1)} %param.26), channel_id=1, source_target_pairs={{0,128},{128,256},{256,384},{384,0},{1,129},{129,257},{257,385},{3... | collective-permute-start | bytes 2359304 | tf_op jit(solution)/shard_map/ppermute | solution.py:74
  12.6 8.2 %collective-permute-start.1 = (bf16[2,1024,192]{1,2,0:T(8,128)(2,1)}, bf16[2,1024,192]{1,2,0:T(8,128)(2,1)S(1)}, u32[]{:S(2)}, u32[]{:S(2)}) collective-permute-start(bf16[2,1024,192]{1,2,0:T(8,128)(2,1)} %param.26), channel_id=1, source_target_pairs={{0,256},{128,384},{256,0},{384,128},{1,257},{129,385},{257,1},{385... | collective-permute-start | bytes 2359304 | tf_op jit(solution)/shard_map/ppermute | solution.py:74
  20.8 1.9 %collective-permute-start.2 = (bf16[2,1024,192]{1,2,0:T(8,128)(2,1)}, bf16[2,1024,192]{1,2,0:T(8,128)(2,1)S(1)}, u32[]{:S(2)}, u32[]{:S(2)}) collective-permute-start(bf16[2,1024,192]{1,2,0:T(8,128)(2,1)} %param.26), channel_id=1, source_target_pairs={{0,384},{128,0},{256,128},{384,256},{1,385},{129,1},{257,129},{385... | collective-permute-start | bytes 2359304 | tf_op jit(solution)/shard_map/ppermute | solution.py:74
  22.8 0.9 select_reduce_fusion
  23.7 0.7 pad_maximum_fusion.2
  24.4 0.7 broadcast_in_dim.42
  25.1 12.3 %all-to-all-start = ((bf16[16,4,1152]{2,1,0:T(4,128)(2,1)}), bf16[16,4,1152]{2,1,0:T(4,128)(2,1)}, u32[]{:S(2)}, u32[]{:S(2)}) async-start(bf16[16,4,1152]{2,1,0:T(4,128)(2,1)} %broadcast_in_dim.42), calls=%async_computation | async-start | bytes 294912 | tf_op jit(solution)/shard_map/all_to_all | solution.py:17
  37.4 0.7 all-gather.6.cloned.1.call-update
  38.3 0.6 add.118
  39.5 12.3 %all-to-all-done = bf16[16,4,1152]{2,1,0:T(4,128)(2,1)} async-done(((bf16[16,4,1152]{2,1,0:T(4,128)(2,1)}), bf16[16,4,1152]{2,1,0:T(4,128)(2,1)}, u32[]{:S(2)}, u32[]{:S(2)}) %all-to-all-start) | async-done | bytes 147488 | tf_op jit(solution)/shard_map/all_to_all | solution.py:17
  51.7 1.0 reshape.260
  52.8 1.3 compare_convert_fusion
  54.5 1.5 fusion.7
  56.4 6.3 %collective-permute-done.2 = bf16[2,1024,192]{1,2,0:T(8,128)(2,1)S(1)} collective-permute-done((bf16[2,1024,192]{1,2,0:T(8,128)(2,1)}, bf16[2,1024,192]{1,2,0:T(8,128)(2,1)S(1)}, u32[]{:S(2)}, u32[]{:S(2)}) %collective-permute-start.2) | collective-permute-done | bytes 786464 | tf_op jit(solution)/shard_map/ppermute | solution.py:74
  63.1 14.5 %all_to_all.30 = f32[8,64,192]{2,1,0:T(8,128)S(1)} all-to-all(f32[8,64,192]{2,1,0:T(8,128)S(1)} %broadcast_in_dim.43), channel_id=1, replica_groups=mesh['y'=4,'z'=16,'tensor'=8] {'tensor'}, dimensions={0} | all-to-all | bytes 786432 | tf_op jit(solution)/shard_map/all_to_all | solution.py:17
  77.7 1.2 fusion.12
  78.9 1.2 fusion.13
  80.1 1.7 fusion.2
  81.8 0.7 reshape.261
  82.5 15.2 %all-to-all-start.2 = ((bf16[16,4,1280]{2,1,0:T(4,128)(2,1)}), bf16[16,4,1280]{2,1,0:T(4,128)(2,1)S(1)}, u32[]{:S(2)}, u32[]{:S(2)}) async-start(bf16[16,4,1280]{2,1,0:T(4,128)(2,1)} %reshape.261), calls=%async_computation.2 | async-start | bytes 327680 | tf_op jit(solution)/shard_map/all_to_all | solution.py:17
  97.8 0.7 all-gather.8.cloned.1.call-update
  98.6 0.7 gather_fusion
  99.4 2.0 %gather_fusion.1 = bf16[32,128,128]{2,1,0:T(8,128)(2,1)S(1)} fusion(bf16[32,128,128]{2,1,0:T(8,128)(2,1)} %param.21, s32[1024]{0:T(1024)S(1)} %pad_clamp_fusion), kind=kCustom, calls=%fused_computation.1 | custom fusion | bytes 2097280 | tf_op jit(solution)/shard_map/gather | solution.py:127
  101.4 11.6 %all-to-all-done.2 = bf16[16,4,1280]{2,1,0:T(4,128)(2,1)S(1)} async-done(((bf16[16,4,1280]{2,1,0:T(4,128)(2,1)}), bf16[16,4,1280]{2,1,0:T(4,128)(2,1)S(1)}, u32[]{:S(2)}, u32[]{:S(2)}) %all-to-all-start.2) | async-done | bytes 163872 | tf_op jit(solution)/shard_map/all_to_all | solution.py:17
  114.3 18.4 %all_to_all.31 = bf16[16,4,1024]{2,1,0:T(4,128)(2,1)S(1)} all-to-all(bf16[16,4,1024]{2,1,0:T(4,128)(2,1)S(1)} %broadcast_in_dim.47), channel_id=1, replica_groups=mesh['y'=4,'z'=16,'tensor'=8] {'z'}, dimensions={0} | all-to-all | bytes 262144 | tf_op jit(solution)/shard_map/all_to_all | solution.py:17
  132.8 1.9 %fusion.4 = f32[64,64]{1,0:T(8,128)S(1)} fusion(bf16[64,1024,1]{1,0,2:T(8,128)(2,1)S(1)} %reshape.297, bf16[8,1024,64]{1,2,0:T(8,128)(2,1)} %all-gather.6.cloned.1.call-done, f32[64,8]{0,1:T(8,128)S(1)} %copy-done.3), kind=kOutput, calls=%fused_computation.9 | convolution fusion | flops 67170304 | bytes 1198080 | tf_op jit(solution)/shard_map/nd,jdr->njr/dot_general | solution.py:26
  134.9 8.5 %all_to_all.32 = f32[8,1,4096]{2,1,0:T(1,128)S(1)} all-to-all(f32[8,1,4096]{2,1,0:T(1,128)S(1)} %reshape.301), channel_id=1, replica_groups=mesh['y'=4,'z'=16,'tensor'=8] {'tensor'}, dimensions={0} | all-to-all | bytes 262144 | tf_op jit(solution)/shard_map/all_to_all | solution.py:17
  144.0 1.0 reduce.7
  145.1 1.6 fusion.3
  146.8 18.2 %all_to_all.33 = bf16[16,4,1024]{2,1,0:T(4,128)(2,1)S(1)} all-to-all(bf16[16,4,1024]{2,1,0:T(4,128)(2,1)S(1)} %reshape.266), channel_id=1, replica_groups=mesh['y'=4,'z'=16,'tensor'=8] {'z'}, dimensions={0} | all-to-all | bytes 262144 | tf_op jit(solution)/shard_map/all_to_all | solution.py:17
  165.0 0.7 reduce_sum.112
  (68 shorter events, 4.8 us)
Async XLA Ops:
  7.2 91.4 %copy-start = (bf16[32,128,128]{2,1,0:T(8,128)(2,1)S(1)}, bf16[32,128,128]{2,1,0:T(8,128)(2,1)}, u32[]{:S(2)}) copy-start(bf16[32,128,128]{2,1,0:T(8,128)(2,1)} %param.20) | copy-start | bytes 3145732
  7.2 46.9 %copy-start.1 = (bf16[2,1024,192]{1,2,0:T(8,128)(2,1)S(1)}, bf16[2,1024,192]{1,2,0:T(8,128)(2,1)}, u32[]{:S(2)}) copy-start(bf16[2,1024,192]{1,2,0:T(8,128)(2,1)} %param.26) | copy-start | bytes 2359300
  7.2 70.5 %all-gather.4.cloned.1.call-start = ((), (), s32[]{:S(2)}) async-start(), calls=%async_computation.6 | async-start | bytes 1638400 | tf_op jit(solution)/shard_map/all_gather | solution.py:79
  9.1 45.3 %collective-permute-start = (bf16[2,1024,192]{1,2,0:T(8,128)(2,1)}, bf16[2,1024,192]{1,2,0:T(8,128)(2,1)}, u32[]{:S(2)}, u32[]{:S(2)}) collective-permute-start(bf16[2,1024,192]{1,2,0:T(8,128)(2,1)} %param.26), channel_id=1, source_target_pairs={{0,128},{128,256},{256,384},{384,0},{1,129},{129,257},{257,385},{3... | collective-permute-start | bytes 2359304 | tf_op jit(solution)/shard_map/ppermute | solution.py:74
  12.6 43.4 %collective-permute-start.1 = (bf16[2,1024,192]{1,2,0:T(8,128)(2,1)}, bf16[2,1024,192]{1,2,0:T(8,128)(2,1)S(1)}, u32[]{:S(2)}, u32[]{:S(2)}) collective-permute-start(bf16[2,1024,192]{1,2,0:T(8,128)(2,1)} %param.26), channel_id=1, source_target_pairs={{0,256},{128,384},{256,0},{384,128},{1,257},{129,385},{257,1},{385... | collective-permute-start | bytes 2359304 | tf_op jit(solution)/shard_map/ppermute | solution.py:74
  20.8 41.8 %collective-permute-start.2 = (bf16[2,1024,192]{1,2,0:T(8,128)(2,1)}, bf16[2,1024,192]{1,2,0:T(8,128)(2,1)S(1)}, u32[]{:S(2)}, u32[]{:S(2)}) collective-permute-start(bf16[2,1024,192]{1,2,0:T(8,128)(2,1)} %param.26), channel_id=1, source_target_pairs={{0,384},{128,0},{256,128},{384,256},{1,385},{129,1},{257,129},{385... | collective-permute-start | bytes 2359304 | tf_op jit(solution)/shard_map/ppermute | solution.py:74
  25.1 26.6 %all-to-all-start = ((bf16[16,4,1152]{2,1,0:T(4,128)(2,1)}), bf16[16,4,1152]{2,1,0:T(4,128)(2,1)}, u32[]{:S(2)}, u32[]{:S(2)}) async-start(bf16[16,4,1152]{2,1,0:T(4,128)(2,1)} %broadcast_in_dim.42), calls=%async_computation | async-start | bytes 294912 | tf_op jit(solution)/shard_map/all_to_all | solution.py:17
  37.4 95.4 %all-gather.6.cloned.1.call-start = ((), (), s32[]{:S(2)}) async-start(), calls=%async_computation.7 | async-start | bytes 1310720 | tf_op jit(solution)/shard_map/all_gather | solution.py:79
  63.0 14.7 %copy-start.6 = (bf16[64,8]{0,1:T(8,128)(2,1)S(1)}, bf16[64,8]{0,1:T(8,128)(2,1)}, u32[]{:S(2)}) copy-start(bf16[64,8]{0,1:T(8,128)(2,1)} %get-tuple-element.14) | copy-start | bytes 3076
  80.1 18.3 %copy-start.5 = (s32[4,8]{1,0:T(4,128)S(1)}, s32[4,8]{1,0:T(4,128)}, u32[]{:S(2)}) copy-start(s32[4,8]{1,0:T(4,128)} %param.22) | copy-start | bytes 388
  82.5 30.5 %all-to-all-start.2 = ((bf16[16,4,1280]{2,1,0:T(4,128)(2,1)}), bf16[16,4,1280]{2,1,0:T(4,128)(2,1)S(1)}, u32[]{:S(2)}, u32[]{:S(2)}) async-start(bf16[16,4,1280]{2,1,0:T(4,128)(2,1)} %reshape.261), calls=%async_computation.2 | async-start | bytes 327680 | tf_op jit(solution)/shard_map/all_to_all | solution.py:17
  97.7 47.4 %all-gather.8.cloned.1.call-start = ((), (), s32[]{:S(2)}) async-start(), calls=%async_computation.8 | async-start | bytes 1310720 | tf_op jit(solution)/shard_map/all_gather | solution.py:79
  99.3 2.0 %copy-start.9 = (s32[4]{0:T(128)S(1)}, s32[4]{0:T(128)}, u32[]{:S(2)}) copy-start(s32[4]{0:T(128)} %param.23) | copy-start | bytes 52
  99.3 13.8 %copy-start.4 = (bf16[4,1024]{1,0:T(4,128)(2,1)S(1)}, bf16[4,1024]{1,0:T(4,128)(2,1)}, u32[]{:S(2)}) copy-start(bf16[4,1024]{1,0:T(4,128)(2,1)} %param.17) | copy-start | bytes 24580
  99.3 13.8 %copy-start.7 = (bf16[4,128]{1,0:T(4,128)(2,1)S(1)}, bf16[4,128]{1,0:T(4,128)(2,1)}, u32[]{:S(2)}) copy-start(bf16[4,128]{1,0:T(4,128)(2,1)} %param.19) | copy-start | bytes 3076
  99.3 13.8 %copy-start.8 = (bf16[4,128]{1,0:T(4,128)(2,1)S(1)}, bf16[4,128]{1,0:T(4,128)(2,1)}, u32[]{:S(2)}) copy-start(bf16[4,128]{1,0:T(4,128)(2,1)} %param.18) | copy-start | bytes 3076
  113.7 19.1 %copy-start.3 = (f32[64,8]{0,1:T(8,128)S(1)}, f32[64,8]{0,1:T(8,128)}, u32[]{:S(2)}) copy-start(f32[64,8]{0,1:T(8,128)} %get-tuple-element.13) | copy-start | bytes 6148
  114.3 29.2 %copy-start.2 = (bf16[1,4,8,128]{3,1,2,0:T(4,128)(2,1)}, bf16[1,4,8,128]{3,1,2,0:T(4,128)(2,1)S(1)}, u32[]{:S(2)}) copy-start(bf16[1,4,8,128]{3,1,2,0:T(4,128)(2,1)S(1)} %copy.37) | copy-start | bytes 24580
Sparse Core Ops, SparseCore 0:
  10.1 48.4 all-gather.3
  60.7 34.7 all-gather.5
  100.6 29.1 all-gather.7

commit v3 on v1

--- a/solution.py
+++ b/solution.py
@@ -2,6 +2,8 @@
 import jax.numpy as jnp
 import numpy as np
 from jax import lax
+from jax.experimental import pallas as pl
+from jax.experimental.pallas import tpu as pltpu
 from jax.sharding import Mesh, PartitionSpec as P
 
 HEAD_SIZE = 128
@@ -22,22 +24,103 @@
     return exchange(copies, axis)
 
 
-def partial_ranks(rows, weight_pages, mask):
-    product = jnp.einsum("nd,jdr->njr", rows, weight_pages, preferred_element_type=jnp.float32)
-    return jnp.sum(product * mask[:, :, None], axis=1)
-
-
 def summed(parts):
     return jnp.sum(parts.astype(jnp.float32), axis=0)
 
 
-def up(ranks, weight_pages, mask):
-    count, rank, width = weight_pages.shape
-    picked = (ranks[:, None, :] * mask.astype(jnp.bfloat16)[:, :, None]).reshape(-1, count * rank)
-    product = jnp.dot(
-        picked, weight_pages.reshape(count * rank, width), preferred_element_type=jnp.float32
-    )
-    return (adapter_scale * product).astype(jnp.bfloat16)
+NT = (((1,), (1,)), ((), ()))
+VMEM = pl.BlockSpec(memory_space=pltpu.VMEM)
+SMEM = pl.BlockSpec(memory_space=pltpu.SMEM)
+
+
+def call(kernel, shape, dtype, *operands):
+    return pl.pallas_call(
+        kernel,
+        out_shape=jax.ShapeDtypeStruct(shape, dtype),
+        in_specs=[SMEM] + [VMEM] * (len(operands) - 1),
+        out_specs=VMEM,
+        compiler_params=pltpu.CompilerParams(vmem_limit_bytes=40 * 2**20),
+    )(*operands)
+
+
+def pack(slots_ref, *refs):
+    out_ref, at = refs[-1], 0
+    for ref in refs[:-1]:
+        out_ref[:, :, at : at + ref.shape[2]] = ref[...]
+        at += ref.shape[2]
+
+
+def picked(slots_ref, tags, values, number):
+    return jnp.where(tags == slots_ref[number].astype(jnp.float32), values, jnp.zeros_like(values))
+
+
+def tags_of(rows_ref, at, width):
+    return rows_ref[:, at : at + width].astype(jnp.float32)
+
+
+def grown(slots_ref, tags, ranks, pages, at, width):
+    total = None
+    for k, page in enumerate(pages):
+        count, rank, _ = page.shape
+        mine = [picked(slots_ref, tags, ranks, k * count + j) for j in range(count)]
+        product = jnp.dot(
+            jnp.concatenate(mine, axis=1).astype(jnp.bfloat16),
+            page[:, :, at : at + width].reshape(count * rank, width),
+            preferred_element_type=jnp.float32,
+        )
+        total = product if total is None else total + product
+    return (adapter_scale * total).astype(jnp.bfloat16)
+
+
+def make_up_first(cuts):
+    def up_first(slots_ref, ranks_ref, rows_ref, *refs):
+        pages, out_ref = refs[:-1], refs[-1]
+        rank = pages[0].shape[1]
+        tags = tags_of(rows_ref, rows_ref.shape[1] - 128, rank)
+        ranks = ranks_ref[...].astype(jnp.float32)
+        for i in range(3):
+            out_ref[:, cuts[i] : cuts[i + 1]] = grown(
+                slots_ref,
+                tags,
+                ranks[:, i * rank : (i + 1) * rank],
+                pages,
+                cuts[i],
+                cuts[i + 1] - cuts[i],
+            )
+
+    return up_first
+
+
+def make_down_second(at):
+    def down_second(slots_ref, out_rows_ref, rows_ref, *refs):
+        pages, out_ref = refs[:-1], refs[-1]
+        count, rank, _ = pages[0].shape
+        rows = out_rows_ref[...]
+        tags = tags_of(rows_ref, rows_ref.shape[1] - 128, rank)
+        total = jnp.zeros((rows.shape[0], rank), jnp.float32)
+        for k, page in enumerate(pages):
+            for j in range(count):
+                weight = page[j, :, at : at + rows.shape[1]]
+                product = lax.dot_general(rows, weight, NT, preferred_element_type=jnp.float32)
+                total = total + picked(slots_ref, tags, product, k * count + j)
+        half = rows.shape[0] // 2
+        side = jnp.concatenate([total[:half], total[half:]], axis=1)
+        for t in range(out_ref.shape[0]):
+            out_ref[t] = side
+
+    return down_second
+
+
+def make_up_second(at):
+    def up_second(slots_ref, parts_ref, rows_ref, *refs):
+        pages, out_ref = refs[:-1], refs[-1]
+        rank = pages[0].shape[1]
+        side = jnp.sum(parts_ref[...], axis=0).astype(jnp.bfloat16).astype(jnp.float32)
+        ranks = jnp.concatenate([side[:, :rank], side[:, rank:]], axis=0)
+        tags = tags_of(rows_ref, rows_ref.shape[1] - 128, rank)
+        out_ref[...] = grown(slots_ref, tags, ranks, pages, at, out_ref.shape[1])
+
+    return up_second
 
 
 def to_requests(rows):
@@ -69,33 +152,54 @@
         jnp.where(adapter_id[:, None] == lookup[None, :], adapter_slot[None, :], 0), axis=1
     )
     tags = jnp.broadcast_to(own_slots.astype(jnp.bfloat16)[:, None], (local_rows, 128))
-    column = [
-        lax.all_gather(weight, Y, axis=0, tiled=True)
-        for weight in (query_up_weight, key_up_weight, value_up_weight, output_down_weight, output_up_weight)
+    y_size, z_size, t_size = lax.axis_size(Y), lax.axis_size(Z), lax.axis_size(T)
+    rank, width_q, width_k = query_up_weight.shape[1], q_base.shape[1], base_key.shape[1]
+    cuts = (0, width_q, width_q + width_k, width_q + 2 * width_k)
+    own_y = lax.axis_index(Y)
+    places = jnp.arange(y_size, dtype=jnp.int32)
+    numbers = jnp.arange(local_count, dtype=jnp.int32)
+    column_slots = (
+        ((own_y - places[:, None]) % y_size * z_size + lax.axis_index(Z)) * local_count + numbers
+    ).reshape(-1)
+    packed_width = cuts[3] + local_width + output_up_weight.shape[2]
+    packed = call(
+        pack,
+        (local_count, rank, packed_width),
+        jnp.bfloat16,
+        column_slots,
+        query_up_weight,
+        key_up_weight,
+        value_up_weight,
+        jnp.swapaxes(output_down_weight, 1, 2),
+        output_up_weight,
+    )
+    pages = [packed] + [
+        lax.ppermute(packed, Y, [(i, (i + k) % y_size) for i in range(y_size)])
+        for k in range(1, y_size)
     ]
-    y_size, z_size, t_size = lax.axis_size(Y), lax.axis_size(Z), lax.axis_size(T)
     z_rows = spread(jnp.concatenate([hidden, tags], axis=1), Z).reshape(z_size * local_rows, -1)
     all_rows = spread(z_rows, Y).reshape(y_size * z_size * local_rows, -1)
 
-    numbers = jnp.arange(local_count, dtype=jnp.int32)
-    first = lax.axis_index(Z) * local_count
-    owned_slots = lax.axis_index(Y) * z_size * local_count + first + numbers
-    column_slots = (
-        jnp.arange(y_size, dtype=jnp.int32)[:, None] * (z_size * local_count) + first + numbers[None, :]
-    ).reshape(-1)
     all_slots = all_rows[:, local_width].astype(jnp.int32)
-    owned_mask = (all_slots[:, None] == owned_slots[None, :]).astype(jnp.float32)
-    z_slots = z_rows[:, local_width].astype(jnp.int32)
-    column_mask = (z_slots[:, None] == column_slots[None, :]).astype(jnp.float32)
-
-    part = partial_ranks(all_rows[:, :local_width], query_key_value_down, owned_mask)
+    owned_mask = (all_slots[:, None] == column_slots[None, :local_count]).astype(jnp.float32)
+    product = jnp.einsum(
+        "nd,jdr->njr",
+        all_rows[:, :local_width],
+        query_key_value_down,
+        preferred_element_type=jnp.float32,
+    )
+    part = jnp.sum(product * owned_mask[:, :, None], axis=1)
     share = z_size * local_rows // t_size
     shares = exchange(part.reshape(y_size * t_size, share, -1), (Y, T))
     ranks = spread(summed(shares).astype(jnp.bfloat16), T).reshape(z_size * local_rows, -1)
-    width = query_up_weight.shape[1]
-    delta = jnp.concatenate(
-        [up(ranks[:, i * width : (i + 1) * width], column[i], column_mask) for i in range(3)],
-        axis=1,
+    delta = call(
+        make_up_first(cuts),
+        (z_size * local_rows, cuts[3]),
+        jnp.bfloat16,
+        column_slots,
+        ranks,
+        z_rows,
+        *pages,
     )
     adapter_delta = to_requests(delta)
     width_q = q_base.shape[1]
@@ -145,8 +249,25 @@
     mixed = mixed + rounded_values(own_weight)[..., None] * fresh_wide
     attention = (mixed / total[..., None]).reshape(local_rows, width_q).astype(jnp.bfloat16)
     out_rows = spread(attention, Z).reshape(z_size * local_rows, -1)
-    out_ranks = summed(spread(partial_ranks(out_rows, column[3], column_mask), T))
-    output_adapter_term = to_requests(up(out_ranks.astype(jnp.bfloat16), column[4], column_mask))
+    sides = call(
+        make_down_second(cuts[3]),
+        (t_size, z_size * local_rows // 2, 2 * rank),
+        jnp.float32,
+        column_slots,
+        out_rows,
+        z_rows,
+        *pages,
+    )
+    term = call(
+        make_up_second(cuts[3] + local_width),
+        (z_size * local_rows, output_up_weight.shape[2]),
+        jnp.bfloat16,
+        column_slots,
+        exchange(sides, T),
+        z_rows,
+        *pages,
+    )
+    output_adapter_term = to_requests(term)
     return (attention, output_adapter_term.astype(jnp.bfloat16))
 
 

time: 186 us -> 174 us (0.935)
  between operations: 14.1 us -> 0.91 us
  waiting for transfers between devices: 40 us -> 29.2 us
  blocking collectives: 70.7 us -> 77 us
  Pallas kernels: 0 us -> 6.18 us
  matrix products: 6.99 us -> 3.71 us
  starting transfers between devices: 40.8 us -> 43.6 us
    all_to_all x3 -> x4, blocking collectives: 45.2 us -> 77 us  [exchange(): return lax.all_to_all(blocks, axis, 0, 0)]
    all_gather x2 -> x0, blocking collectives: 25.5 us -> none  [body(): lax.all_gather(weight, Y, axis=0, tiled=True)]
    ppermute x0 -> x3, starting transfers between devices: none -> 11.9 us  [body(): lax.ppermute(packed, Y, [(i, (i + k) % y_size) for i in range(y_size)])]
    all_to_all x5 -> x4, starting transfers between devices: 40.7 us -> 31.7 us  [exchange(): return lax.all_to_all(blocks, axis, 0, 0)]
    all_to_all x5 -> x4, waiting for transfers between devices: 37.9 us -> 29.2 us  [exchange(): return lax.all_to_all(blocks, axis, 0, 0)]
    pallas_call x0 -> x4, Pallas kernels: none -> 6.18 us  [call(): pl.pallas_call(kernel, out_shape=jax.ShapeDtypeStruct(shape, dtype), in_s...]
    dot_general x5 -> x0, matrix products: 5.7 us -> none  [the longest x4 3.84 us: up(): jnp.dot(picked, weight_pages.reshape(count * rank, width), preferred_elem...]
    unnamed x3 -> x0, waiting for transfers between devices: 2.05 us -> none
  transfers between devices with their start and end apart: 8 -> 7, of which waited for: 4 -> 3; matrix products, arithmetic and copies ran while one was open for 8% -> 4% of each run, Pallas kernels for 0% -> 0%
where the time goes in v3:
time: 174 us; the launch traced here: 172 us
  blocking collectives  77 us (44%)
  starting transfers between devices  43.6 us (25%)
  waiting for transfers between devices  29.2 us (17%)
  local copies, waits for them, and re-layouts  8.62 us (5%)
  Pallas kernels  6.18 us (4%)
  matrix products  3.71 us (2%)
  other arithmetic  3.06 us (2%)
    all_to_all x4, blocking collectives, exchange(): return lax.all_to_all(blocks, axis, 0, 0)  77 us
    all_to_all x4, starting transfers between devices, exchange(): return lax.all_to_all(blocks, axis, 0, 0)  31.7 us
    all_to_all x4, waiting for transfers between devices, exchange(): return lax.all_to_all(blocks, axis, 0, 0)  29.2 us
    ppermute x3, starting transfers between devices, body(): lax.ppermute(packed, Y, [(i, (i + k) % y_size) for i in range(y_size)])  11.9 us
    pallas_call x4, Pallas kernels, call(): pl.pallas_call(kernel, out_shape=jax.ShapeDtypeStruct(shape, dtype), in_s...  6.18 us
  transfers between devices with their start and end apart: 7, of which 3 were waited for; matrix products, arithmetic and copies ran while one was open for 4% of the time, Pallas kernels for 0%

profile of v3, /device:TPU:6, one launch (start us, length us, event | category | flops | bytes accessed | tf_op | source)
XLA Modules:
  0.0 172.3 jit_solution(14301332800212321512)
XLA Ops:
  0.6 0.9 select_reduce_fusion
  1.7 0.7 pad_maximum_fusion
  2.4 0.7 broadcast_in_dim.48
  3.1 15.2 %all-to-all-start = ((bf16[16,4,1152]{2,1,0:T(4,128)(2,1)}), bf16[16,4,1152]{2,1,0:T(4,128)(2,1)S(1)}, u32[]{:S(2)}, u32[]{:S(2)}) async-start(bf16[16,4,1152]{2,1,0:T(4,128)(2,1)} %broadcast_in_dim.48), calls=%async_computation | async-start | bytes 294912 | tf_op jit(solution)/shard_map/all_to_all | solution.py:19
  18.3 15.1 %all-to-all-done = bf16[16,4,1152]{2,1,0:T(4,128)(2,1)S(1)} async-done(((bf16[16,4,1152]{2,1,0:T(4,128)(2,1)}), bf16[16,4,1152]{2,1,0:T(4,128)(2,1)S(1)}, u32[]{:S(2)}, u32[]{:S(2)}) %all-to-all-start) | async-done | bytes 147488 | tf_op jit(solution)/shard_map/all_to_all | solution.py:19
  33.4 0.9 broadcast_in_dim.50
  34.3 4.6 %all-to-all-start.1 = ((bf16[4,64,1152]{2,1,0:T(8,128)(2,1)}), bf16[4,64,1152]{2,1,0:T(8,128)(2,1)S(1)}, u32[]{:S(2)}, u32[]{:S(2)}) async-start(bf16[4,64,1152]{2,1,0:T(8,128)(2,1)} %broadcast_in_dim.50), calls=%async_computation.1 | async-start | bytes 1179648 | tf_op jit(solution)/shard_map/all_to_all | solution.py:19
  39.1 0.6 shard_map.167.refs_0_
  39.7 3.9 %collective-permute-start = (bf16[2,64,3328]{2,1,0:T(8,128)(2,1)S(1)}, bf16[2,64,3328]{2,1,0:T(8,128)(2,1)S(1)}, u32[]{:S(2)}, u32[]{:S(2)}) collective-permute-start(bf16[2,64,3328]{2,1,0:T(8,128)(2,1)S(1)} %shard_map.167.refs_0_), channel_id=1, source_target_pairs={{0,128},{128,256},{256,384},{384,0},{1,129},{129,257},{257,385},{3... | collective-permute-start | bytes 2555912 | tf_op jit(solution)/shard_map/ppermute | solution.py:177
  43.7 4.6 %collective-permute-start.1 = (bf16[2,64,3328]{2,1,0:T(8,128)(2,1)S(1)}, bf16[2,64,3328]{2,1,0:T(8,128)(2,1)}, u32[]{:S(2)}, u32[]{:S(2)}) collective-permute-start(bf16[2,64,3328]{2,1,0:T(8,128)(2,1)S(1)} %shard_map.167.refs_0_), channel_id=1, source_target_pairs={{0,256},{128,384},{256,0},{384,128},{1,257},{129,385},{257,1},{385... | collective-permute-start | bytes 2555912 | tf_op jit(solution)/shard_map/ppermute | solution.py:177
  48.3 3.4 %collective-permute-start.2 = (bf16[2,64,3328]{2,1,0:T(8,128)(2,1)S(1)}, bf16[2,64,3328]{2,1,0:T(8,128)(2,1)}, u32[]{:S(2)}, u32[]{:S(2)}) collective-permute-start(bf16[2,64,3328]{2,1,0:T(8,128)(2,1)S(1)} %shard_map.167.refs_0_), channel_id=1, source_target_pairs={{0,384},{128,0},{256,128},{384,256},{1,385},{129,1},{257,129},{385... | collective-permute-start | bytes 2555912 | tf_op jit(solution)/shard_map/ppermute | solution.py:177
  51.9 1.5 fusion.4
  53.6 31.8 %all_to_all.40 = f32[32,8,192]{2,1,0:T(8,128)S(1)} all-to-all(f32[32,8,192]{2,1,0:T(8,128)S(1)} %bitcast.45), channel_id=1, replica_groups=mesh['y'=4,'z'=16,'tensor'=8] {'y','tensor'}, dimensions={0} | all-to-all | bytes 393216 | tf_op jit(solution)/shard_map/all_to_all | solution.py:19
  85.4 0.6 broadcast_in_dim.86
  86.0 4.8 %all-to-all-start.3 = ((bf16[8,8,192]{2,1,0:T(8,128)(2,1)}), bf16[8,8,192]{2,1,0:T(8,128)(2,1)S(1)}, u32[]{:S(2)}, u32[]{:S(2)}) async-start(bf16[8,8,192]{2,1,0:T(8,128)(2,1)} %broadcast_in_dim.86), calls=%async_computation.3 | async-start | bytes 65536 | tf_op jit(solution)/shard_map/all_to_all | solution.py:19
  90.8 3.4 %all-to-all-done.3 = bf16[8,8,192]{2,1,0:T(8,128)(2,1)S(1)} async-done(((bf16[8,8,192]{2,1,0:T(8,128)(2,1)}), bf16[8,8,192]{2,1,0:T(8,128)(2,1)S(1)}, u32[]{:S(2)}, u32[]{:S(2)}) %all-to-all-start.3) | async-done | bytes 24608 | tf_op jit(solution)/shard_map/all_to_all | solution.py:19
  94.1 1.8 %shard_map.168 = bf16[64,1280]{1,0:T(8,128)(2,1)S(1)} custom-call(s32[8]{0:T(128)S(1)} %add.66.slots_ref, bf16[64,192]{1,0:T(8,128)(2,1)S(1)} %bitcast.39, bf16[64,1152]{1,0:T(8,128)(2,1)S(1)} %broadcast_in_dim.49.rows_ref, bf16[2,64,3328]{2,1,0:T(8,128)(2,1)S(1)} %shard_map.167.refs_0_, bf16[2,64,3328]{2,1,0:T(8,128)(2,1)S(1)} %collective-permute-done.refs_1_, ...), custom_call_target="tpu_custom_call" | custom-call | tf_op jit(solution)/shard_map/pallas_call | solution.py:37
  96.0 0.7 reshape.193
  96.7 7.2 %all-to-all-start.4 = ((bf16[16,4,1280]{2,1,0:T(4,128)(2,1)}), bf16[16,4,1280]{2,1,0:T(4,128)(2,1)S(1)}, u32[]{:S(2)}, u32[]{:S(2)}) async-start(bf16[16,4,1280]{2,1,0:T(4,128)(2,1)} %reshape.193), calls=%async_computation.4 | async-start | bytes 327680 | tf_op jit(solution)/shard_map/all_to_all | solution.py:19
  104.0 1.7 gather_fusion
  105.7 2.9 %gather_fusion.1 = bf16[32,128,128]{2,1,0:T(8,128)(2,1)} fusion(bf16[32,128,128]{2,1,0:T(8,128)(2,1)} %param.21, s32[1024]{0:T(1024)S(1)} %pad_clamp_fusion), kind=kCustom, calls=%fused_computation.1 | custom fusion | bytes 2097280 | tf_op jit(solution)/shard_map/gather | solution.py:217
  108.7 10.7 %all-to-all-done.4 = bf16[16,4,1280]{2,1,0:T(4,128)(2,1)S(1)} async-done(((bf16[16,4,1280]{2,1,0:T(4,128)(2,1)}), bf16[16,4,1280]{2,1,0:T(4,128)(2,1)S(1)}, u32[]{:S(2)}, u32[]{:S(2)}) %all-to-all-start.4) | async-done | bytes 163872 | tf_op jit(solution)/shard_map/all_to_all | solution.py:19
  119.7 1.7 %fusion.30 = (f32[4,8]{1,0:T(4,128)S(1)}, f32[4,8,1024]{2,1,0:T(8,128)S(1)}) fusion(bf16[4,1024,128]{2,1,0:T(8,128)(2,1)} %bitcast.41, bf16[1,4,8,128]{3,1,2,0:T(4,128)(2,1)S(1)} %fusion.13, pred[4,1024]{1,0:T(4,128)(4,1)S(1)} %iota_compare_fusion), kind=kOutput, calls=%fused_computation.57 | convolution fusion | flops 8486880 | bytes 1192064 | tf_op jit(solution)/shard_map/bkgd,btkd->bkgt/dot_general | solution.py:221
  121.4 0.2 fusion.6
  121.6 0.3 fusion.3
  122.0 0.5 copy-done.7
  122.6 18.5 %all_to_all.41 = bf16[16,4,1024]{2,1,0:T(4,128)(2,1)S(1)} all-to-all(bf16[16,4,1024]{2,1,0:T(4,128)(2,1)S(1)} %broadcast_in_dim.90), channel_id=1, replica_groups=mesh['y'=4,'z'=16,'tensor'=8] {'z'}, dimensions={0} | all-to-all | bytes 262144 | tf_op jit(solution)/shard_map/all_to_all | solution.py:19
  141.2 1.9 %shard_map.169 = f32[8,32,128]{2,1,0:T(8,128)S(1)} custom-call(s32[8]{0:T(128)S(1)} %add.66.slots_ref, bf16[64,1024]{1,0:T(8,128)(2,1)S(1)} %reshape.197.out_rows_ref, bf16[64,1152]{1,0:T(8,128)(2,1)S(1)} %broadcast_in_dim.49.rows_ref, bf16[2,64,3328]{2,1,0:T(8,128)(2,1)S(1)} %shard_map.167.refs_0_, bf16[2,64,3328]{2,1,0:T(8,128)(2,1)S(1)} %collective-permute-done.refs_1_, ...), custom_call_target="tpu_custom_call" | custom-call | tf_op jit(solution)/shard_map/pallas_call | solution.py:37
  143.1 8.5 %all_to_all.42.parts_ref = f32[8,32,128]{2,1,0:T(8,128)S(1)} all-to-all(f32[8,32,128]{2,1,0:T(8,128)S(1)} %shard_map.169), channel_id=1, replica_groups=mesh['y'=4,'z'=16,'tensor'=8] {'tensor'}, dimensions={0} | all-to-all | bytes 262144 | tf_op jit(solution)/shard_map/all_to_all | solution.py:19
  151.6 1.8 %shard_map.170 = bf16[64,1024]{1,0:T(8,128)(2,1)S(1)} custom-call(s32[8]{0:T(128)S(1)} %add.66.slots_ref, f32[8,32,128]{2,1,0:T(8,128)S(1)} %all_to_all.42.parts_ref, bf16[64,1152]{1,0:T(8,128)(2,1)S(1)} %broadcast_in_dim.49.rows_ref, bf16[2,64,3328]{2,1,0:T(8,128)(2,1)S(1)} %shard_map.167.refs_0_, bf16[2,64,3328]{2,1,0:T(8,128)(2,1)S(1)} %collective-permute-done.refs_1_, ...), custom_call_target="tpu_custom_call" | custom-call | tf_op jit(solution)/shard_map/pallas_call | solution.py:37
  153.5 18.1 %all_to_all.43 = bf16[16,4,1024]{2,1,0:T(4,128)(2,1)S(1)} all-to-all(bf16[16,4,1024]{2,1,0:T(4,128)(2,1)S(1)} %reshape.198), channel_id=1, replica_groups=mesh['y'=4,'z'=16,'tensor'=8] {'z'}, dimensions={0} | all-to-all | bytes 262144 | tf_op jit(solution)/shard_map/all_to_all | solution.py:19
  171.6 0.7 reduce_sum.62
  (56 shorter events, 1.3 us)
Async XLA Ops:
  0.6 103.3 %copy-start = (bf16[32,128,128]{2,1,0:T(8,128)(2,1)S(1)}, bf16[32,128,128]{2,1,0:T(8,128)(2,1)}, u32[]{:S(2)}) copy-start(bf16[32,128,128]{2,1,0:T(8,128)(2,1)} %param.20) | copy-start | bytes 3145732
  3.1 30.3 %all-to-all-start = ((bf16[16,4,1152]{2,1,0:T(4,128)(2,1)}), bf16[16,4,1152]{2,1,0:T(4,128)(2,1)S(1)}, u32[]{:S(2)}, u32[]{:S(2)}) async-start(bf16[16,4,1152]{2,1,0:T(4,128)(2,1)} %broadcast_in_dim.48), calls=%async_computation | async-start | bytes 294912 | tf_op jit(solution)/shard_map/all_to_all | solution.py:19
  34.3 4.8 %copy-start.1 = (bf16[2,64,1024]{2,1,0:T(8,128)(2,1)S(1)}, bf16[2,64,1024]{2,1,0:T(8,128)(2,1)}, u32[]{:S(2)}) copy-start(bf16[2,64,1024]{2,1,0:T(8,128)(2,1)} %refs_0_.1) | copy-start | bytes 786436
  34.3 4.8 %copy-start.2 = (bf16[2,1024,64]{1,2,0:T(8,128)(2,1)S(1)}, bf16[2,1024,64]{1,2,0:T(8,128)(2,1)}, u32[]{:S(2)}) copy-start(bf16[2,1024,64]{1,2,0:T(8,128)(2,1)} %param.30) | copy-start | bytes 786436
  34.3 4.8 %copy-start.3 = (bf16[2,64,1024]{2,1,0:T(8,128)(2,1)S(1)}, bf16[2,64,1024]{2,1,0:T(8,128)(2,1)}, u32[]{:S(2)}) copy-start(bf16[2,64,1024]{2,1,0:T(8,128)(2,1)} %refs_4_.1) | copy-start | bytes 786436
  34.3 4.8 %copy-start.4 = (bf16[2,64,128]{2,1,0:T(8,128)(2,1)S(1)}, bf16[2,64,128]{2,1,0:T(8,128)(2,1)}, u32[]{:S(2)}) copy-start(bf16[2,64,128]{2,1,0:T(8,128)(2,1)} %refs_1_.1) | copy-start | bytes 98308
  34.3 4.8 %copy-start.5 = (bf16[2,64,128]{2,1,0:T(8,128)(2,1)S(1)}, bf16[2,64,128]{2,1,0:T(8,128)(2,1)}, u32[]{:S(2)}) copy-start(bf16[2,64,128]{2,1,0:T(8,128)(2,1)} %refs_2_.1) | copy-start | bytes 98308
  34.3 17.3 %all-to-all-start.1 = ((bf16[4,64,1152]{2,1,0:T(8,128)(2,1)}), bf16[4,64,1152]{2,1,0:T(8,128)(2,1)S(1)}, u32[]{:S(2)}, u32[]{:S(2)}) async-start(bf16[4,64,1152]{2,1,0:T(8,128)(2,1)} %broadcast_in_dim.50), calls=%async_computation.1 | async-start | bytes 1179648 | tf_op jit(solution)/shard_map/all_to_all | solution.py:19
  39.7 51.0 %collective-permute-start = (bf16[2,64,3328]{2,1,0:T(8,128)(2,1)S(1)}, bf16[2,64,3328]{2,1,0:T(8,128)(2,1)S(1)}, u32[]{:S(2)}, u32[]{:S(2)}) collective-permute-start(bf16[2,64,3328]{2,1,0:T(8,128)(2,1)S(1)} %shard_map.167.refs_0_), channel_id=1, source_target_pairs={{0,128},{128,256},{256,384},{384,0},{1,129},{129,257},{257,385},{3... | collective-permute-start | bytes 2555912 | tf_op jit(solution)/shard_map/ppermute | solution.py:177
  43.7 47.1 %collective-permute-start.1 = (bf16[2,64,3328]{2,1,0:T(8,128)(2,1)S(1)}, bf16[2,64,3328]{2,1,0:T(8,128)(2,1)}, u32[]{:S(2)}, u32[]{:S(2)}) collective-permute-start(bf16[2,64,3328]{2,1,0:T(8,128)(2,1)S(1)} %shard_map.167.refs_0_), channel_id=1, source_target_pairs={{0,256},{128,384},{256,0},{384,128},{1,257},{129,385},{257,1},{385... | collective-permute-start | bytes 2555912 | tf_op jit(solution)/shard_map/ppermute | solution.py:177
  48.3 42.5 %collective-permute-start.2 = (bf16[2,64,3328]{2,1,0:T(8,128)(2,1)S(1)}, bf16[2,64,3328]{2,1,0:T(8,128)(2,1)}, u32[]{:S(2)}, u32[]{:S(2)}) collective-permute-start(bf16[2,64,3328]{2,1,0:T(8,128)(2,1)S(1)} %shard_map.167.refs_0_), channel_id=1, source_target_pairs={{0,384},{128,0},{256,128},{384,256},{1,385},{129,1},{257,129},{385... | collective-permute-start | bytes 2555912 | tf_op jit(solution)/shard_map/ppermute | solution.py:177
  86.0 8.2 %all-to-all-start.3 = ((bf16[8,8,192]{2,1,0:T(8,128)(2,1)}), bf16[8,8,192]{2,1,0:T(8,128)(2,1)S(1)}, u32[]{:S(2)}, u32[]{:S(2)}) async-start(bf16[8,8,192]{2,1,0:T(8,128)(2,1)} %broadcast_in_dim.86), calls=%async_computation.3 | async-start | bytes 65536 | tf_op jit(solution)/shard_map/all_to_all | solution.py:19
  96.7 7.2 %copy-start.9 = (s32[4,8]{1,0:T(4,128)S(1)}, s32[4,8]{1,0:T(4,128)}, u32[]{:S(2)}) copy-start(s32[4,8]{1,0:T(4,128)} %param.22) | copy-start | bytes 388
  96.7 22.7 %all-to-all-start.4 = ((bf16[16,4,1280]{2,1,0:T(4,128)(2,1)}), bf16[16,4,1280]{2,1,0:T(4,128)(2,1)S(1)}, u32[]{:S(2)}, u32[]{:S(2)}) async-start(bf16[16,4,1280]{2,1,0:T(4,128)(2,1)} %reshape.193), calls=%async_computation.4 | async-start | bytes 327680 | tf_op jit(solution)/shard_map/all_to_all | solution.py:19
  105.7 2.9 %copy-start.12 = (s32[4]{0:T(128)S(1)}, s32[4]{0:T(128)}, u32[]{:S(2)}) copy-start(s32[4]{0:T(128)} %param.23) | copy-start | bytes 52
  105.7 13.8 %copy-start.10 = (bf16[4,128]{1,0:T(4,128)(2,1)S(1)}, bf16[4,128]{1,0:T(4,128)(2,1)}, u32[]{:S(2)}) copy-start(bf16[4,128]{1,0:T(4,128)(2,1)} %param.19) | copy-start | bytes 3076
  105.7 13.9 %copy-start.11 = (bf16[4,128]{1,0:T(4,128)(2,1)S(1)}, bf16[4,128]{1,0:T(4,128)(2,1)}, u32[]{:S(2)}) copy-start(bf16[4,128]{1,0:T(4,128)(2,1)} %param.18) | copy-start | bytes 3076
  108.7 10.8 %copy-start.8 = (bf16[4,1024]{1,0:T(4,128)(2,1)S(1)}, bf16[4,1024]{1,0:T(4,128)(2,1)}, u32[]{:S(2)}) copy-start(bf16[4,1024]{1,0:T(4,128)(2,1)} %param.17) | copy-start | bytes 24580
  119.4 2.2 %copy-start.6 = (bf16[32,128,128]{2,1,0:T(8,128)(2,1)S(1)}, bf16[32,128,128]{2,1,0:T(8,128)(2,1)}, u32[]{:S(2)}) copy-start(bf16[32,128,128]{2,1,0:T(8,128)(2,1)} %gather_fusion.1) | copy-start | bytes 3145732
  122.0 0.6 copy-start.7

commit v4 on v3

--- a/solution.py
+++ b/solution.py
@@ -33,17 +33,42 @@
 SMEM = pl.BlockSpec(memory_space=pltpu.SMEM)
 
 
-def call(kernel, shape, dtype, *operands):
+def call(kernel, shape, dtype, *operands, scalars=1, after=()):
+    count = len(operands)
+
+    def body(*refs):
+        kernel(*refs[:count], *refs[count + len(after) :])
+
     return pl.pallas_call(
-        kernel,
+        body,
         out_shape=jax.ShapeDtypeStruct(shape, dtype),
-        in_specs=[SMEM] + [VMEM] * (len(operands) - 1),
+        in_specs=[SMEM] * scalars
+        + [VMEM] * (count - scalars)
+        + [pl.BlockSpec(memory_space=pl.ANY)] * len(after),
         out_specs=VMEM,
-        compiler_params=pltpu.CompilerParams(vmem_limit_bytes=40 * 2**20),
-    )(*operands)
-
-
-def pack(slots_ref, *refs):
+        compiler_params=pltpu.CompilerParams(vmem_limit_bytes=32 * 2**20),
+    )(*operands, *after)
+
+
+def first_blocks(id_ref, slot_ref, hidden_ref, out_ref):
+    rows, width = hidden_ref.shape
+    tags = [
+        jnp.full((1, 128), slot_ref[id_ref[r]].astype(jnp.float32), jnp.float32) for r in range(rows)
+    ]
+    block = jnp.concatenate(
+        [hidden_ref[...], jnp.concatenate(tags, axis=0).astype(jnp.bfloat16)], axis=1
+    )
+    for z in range(out_ref.shape[0]):
+        out_ref[z] = block
+
+
+def second_blocks(from_z_ref, out_ref):
+    rows = from_z_ref[...].reshape(out_ref.shape[1:])
+    for y in range(out_ref.shape[0]):
+        out_ref[y] = rows
+
+
+def pack(*refs):
     out_ref, at = refs[-1], 0
     for ref in refs[:-1]:
         out_ref[:, :, at : at + ref.shape[2]] = ref[...]
@@ -147,11 +172,6 @@
 ):
     local_rows, local_width = hidden.shape
     local_count = query_key_value_down.shape[0]
-    lookup = jnp.arange(adapter_slot.shape[0], dtype=jnp.int32)
-    own_slots = jnp.sum(
-        jnp.where(adapter_id[:, None] == lookup[None, :], adapter_slot[None, :], 0), axis=1
-    )
-    tags = jnp.broadcast_to(own_slots.astype(jnp.bfloat16)[:, None], (local_rows, 128))
     y_size, z_size, t_size = lax.axis_size(Y), lax.axis_size(Z), lax.axis_size(T)
     rank, width_q, width_k = query_up_weight.shape[1], q_base.shape[1], base_key.shape[1]
     cuts = (0, width_q, width_q + width_k, width_q + 2 * width_k)
@@ -161,24 +181,36 @@
     column_slots = (
         ((own_y - places[:, None]) % y_size * z_size + lax.axis_index(Z)) * local_count + numbers
     ).reshape(-1)
-    packed_width = cuts[3] + local_width + output_up_weight.shape[2]
-    packed = call(
-        pack,
-        (local_count, rank, packed_width),
+
+    def packed(*weights, after=()):
+        width = sum(weight.shape[2] for weight in weights)
+        shape = (local_count, rank, width)
+        mine = call(pack, shape, jnp.bfloat16, *weights, scalars=0, after=after)
+        return [mine] + [
+            lax.ppermute(mine, Y, [(i, (i + k) % y_size) for i in range(y_size)])
+            for k in range(1, y_size)
+        ]
+
+    up_pages = packed(query_up_weight, key_up_weight, value_up_weight)
+    z_blocks = call(
+        first_blocks,
+        (z_size, local_rows, local_width + 128),
         jnp.bfloat16,
-        column_slots,
-        query_up_weight,
-        key_up_weight,
-        value_up_weight,
-        jnp.swapaxes(output_down_weight, 1, 2),
-        output_up_weight,
-    )
-    pages = [packed] + [
-        lax.ppermute(packed, Y, [(i, (i + k) % y_size) for i in range(y_size)])
-        for k in range(1, y_size)
-    ]
-    z_rows = spread(jnp.concatenate([hidden, tags], axis=1), Z).reshape(z_size * local_rows, -1)
-    all_rows = spread(z_rows, Y).reshape(y_size * z_size * local_rows, -1)
+        adapter_id,
+        adapter_slot,
+        hidden,
+        scalars=2,
+    )
+    y_blocks = call(
+        second_blocks,
+        (y_size, z_size * local_rows, local_width + 128),
+        jnp.bfloat16,
+        exchange(z_blocks, Z),
+        scalars=0,
+        after=up_pages[1:],
+    )
+    z_rows = y_blocks[0]
+    all_rows = exchange(y_blocks, Y).reshape(y_size * z_size * local_rows, -1)
 
     all_slots = all_rows[:, local_width].astype(jnp.int32)
     owned_mask = (all_slots[:, None] == column_slots[None, :local_count]).astype(jnp.float32)
@@ -199,7 +231,10 @@
         column_slots,
         ranks,
         z_rows,
-        *pages,
+        *up_pages,
+    )
+    out_pages = packed(
+        jnp.swapaxes(output_down_weight, 1, 2), output_up_weight, after=(shares,)
     )
     adapter_delta = to_requests(delta)
     width_q = q_base.shape[1]
@@ -250,22 +285,22 @@
     attention = (mixed / total[..., None]).reshape(local_rows, width_q).astype(jnp.bfloat16)
     out_rows = spread(attention, Z).reshape(z_size * local_rows, -1)
     sides = call(
-        make_down_second(cuts[3]),
+        make_down_second(0),
         (t_size, z_size * local_rows // 2, 2 * rank),
         jnp.float32,
         column_slots,
         out_rows,
         z_rows,
-        *pages,
+        *out_pages,
     )
     term = call(
-        make_up_second(cuts[3] + local_width),
+        make_up_second(local_width),
         (z_size * local_rows, output_up_weight.shape[2]),
         jnp.bfloat16,
         column_slots,
         exchange(sides, T),
         z_rows,
-        *pages,
+        *out_pages,
     )
     output_adapter_term = to_requests(term)
     return (attention, output_adapter_term.astype(jnp.bfloat16))

time: 174 us -> 170 us (0.977)
  blocking collectives: 77 us -> 50.8 us
  starting transfers between devices: 43.6 us -> 64.3 us
  local copies, waits for them, and re-layouts: 8.62 us -> 11.4 us
    all_to_all x4 -> x3, blocking collectives: 77 us -> 50.8 us  [exchange(): return lax.all_to_all(blocks, axis, 0, 0)]
    all_to_all x4 -> x5, starting transfers between devices: 31.7 us -> 43.3 us  [exchange(): return lax.all_to_all(blocks, axis, 0, 0)]
    ppermute x3 -> x6, waiting for transfers between devices: 0.01 us -> 10.3 us  [packed(): lax.ppermute(mine, Y, [(i, (i + k) % y_size) for i in range(y_size)])]
    ppermute x3 -> x6, starting transfers between devices: 11.9 us -> 21 us  [packed(): lax.ppermute(mine, Y, [(i, (i + k) % y_size) for i in range(y_size)])]
    all_to_all x4 -> x5, waiting for transfers between devices: 29.2 us -> 20.2 us  [exchange(): return lax.all_to_all(blocks, axis, 0, 0)]
    unnamed x27 -> x37, local copies, waits for them, and re-layouts: 0.61 us -> 3.37 us
    pallas_call x4 -> x7, Pallas kernels: 6.18 us -> 5.11 us  [call(): pl.pallas_call(body, out_shape=jax.ShapeDtypeStruct(shape, dtype), in_spe...]
  transfers between devices with their start and end apart: 7 -> 11, of which waited for: 3 -> 7; matrix products, arithmetic and copies ran while one was open for 4% -> 5% of each run, Pallas kernels for 0% -> 0%
where the time goes in v4:
time: 170 us; the launch traced here: 168 us
  starting transfers between devices  64.3 us (38%)
  blocking collectives  50.8 us (30%)
  waiting for transfers between devices  30.5 us (18%)
  local copies, waits for them, and re-layouts  11.4 us (7%)
  Pallas kernels  5.11 us (3%)
  matrix products  3.7 us (2%)
    all_to_all x3, blocking collectives, exchange(): return lax.all_to_all(blocks, axis, 0, 0)  50.8 us
    all_to_all x5, starting transfers between devices, exchange(): return lax.all_to_all(blocks, axis, 0, 0)  43.3 us
    ppermute x6, starting transfers between devices, packed(): lax.ppermute(mine, Y, [(i, (i + k) % y_size) for i in range(y_size)])  21 us
    all_to_all x5, waiting for transfers between devices, exchange(): return lax.all_to_all(blocks, axis, 0, 0)  20.2 us
    ppermute x6, waiting for transfers between devices, packed(): lax.ppermute(mine, Y, [(i, (i + k) % y_size) for i in range(y_size)])  10.3 us
    pallas_call x7, Pallas kernels, call(): pl.pallas_call(body, out_shape=jax.ShapeDtypeStruct(shape, dtype), in_spe...  5.11 us
  transfers between devices with their start and end apart: 11, of which 7 were waited for; matrix products, arithmetic and copies ran while one was open for 5% of the time, Pallas kernels for 0%

profile of v4, /device:TPU:6, one launch (start us, length us, event | category | flops | bytes accessed | tf_op | source)
XLA Modules:
  0.0 168.1 jit_solution(9148979764917129489)
XLA Ops:
  2.8 1.2 shard_map.167
  4.0 15.3 %all-to-all-start = ((bf16[16,4,1152]{2,1,0:T(4,128)(2,1)}), bf16[16,4,1152]{2,1,0:T(4,128)(2,1)S(1)}, u32[]{:S(2)}, u32[]{:S(2)}) async-start(bf16[16,4,1152]{2,1,0:T(4,128)(2,1)} %shard_map.167), calls=%async_computation | async-start | bytes 294912 | tf_op jit(solution)/shard_map/all_to_all | solution.py:19
  19.4 3.5 %collective-permute-start = (bf16[2,64,1280]{2,1,0:T(8,128)(2,1)S(1)}, bf16[2,64,1280]{2,1,0:T(8,128)(2,1)S(1)}, u32[]{:S(2)}, u32[]{:S(2)}) collective-permute-start(bf16[2,64,1280]{2,1,0:T(8,128)(2,1)S(1)} %shard_map.168.refs_3_), channel_id=1, source_target_pairs={{0,128},{128,256},{256,384},{384,0},{1,129},{129,257},{257,385},{3... | collective-permute-start | bytes 983048 | tf_op jit(solution)/shard_map/ppermute | solution.py:190
  22.9 4.8 %collective-permute-start.1 = (bf16[2,64,1280]{2,1,0:T(8,128)(2,1)S(1)}, bf16[2,64,1280]{2,1,0:T(8,128)(2,1)S(1)}, u32[]{:S(2)}, u32[]{:S(2)}) collective-permute-start(bf16[2,64,1280]{2,1,0:T(8,128)(2,1)S(1)} %shard_map.168.refs_3_), channel_id=1, source_target_pairs={{0,256},{128,384},{256,0},{384,128},{1,257},{129,385},{257,1},{385... | collective-permute-start | bytes 983048 | tf_op jit(solution)/shard_map/ppermute | solution.py:190
  27.7 3.3 %collective-permute-start.2 = (bf16[2,64,1280]{2,1,0:T(8,128)(2,1)S(1)}, bf16[2,64,1280]{2,1,0:T(8,128)(2,1)S(1)}, u32[]{:S(2)}, u32[]{:S(2)}) collective-permute-start(bf16[2,64,1280]{2,1,0:T(8,128)(2,1)S(1)} %shard_map.168.refs_3_), channel_id=1, source_target_pairs={{0,384},{128,0},{256,128},{384,256},{1,385},{129,1},{257,129},{385... | collective-permute-start | bytes 983048 | tf_op jit(solution)/shard_map/ppermute | solution.py:190
  31.0 1.0 collective-permute-done.refs_1_.refs_4_
  32.0 7.9 %collective-permute-done.1.refs_2_.refs_5_ = bf16[2,64,1280]{2,1,0:T(8,128)(2,1)S(1)} collective-permute-done((bf16[2,64,1280]{2,1,0:T(8,128)(2,1)S(1)}, bf16[2,64,1280]{2,1,0:T(8,128)(2,1)S(1)}, u32[]{:S(2)}, u32[]{:S(2)}) %collective-permute-start.1) | collective-permute-done | bytes 327712 | tf_op jit(solution)/shard_map/ppermute | solution.py:190
  39.9 1.3 collective-permute-done.2.refs_3_.refs_6_
  41.3 0.9 shard_map.169
  42.1 4.4 %all-to-all-start.1 = ((bf16[4,64,1152]{2,1,0:T(8,128)(2,1)}), bf16[4,64,1152]{2,1,0:T(8,128)(2,1)S(1)}, u32[]{:S(2)}, u32[]{:S(2)}) async-start(bf16[4,64,1152]{2,1,0:T(8,128)(2,1)} %shard_map.169), calls=%async_computation.1 | async-start | bytes 1179648 | tf_op jit(solution)/shard_map/all_to_all | solution.py:19
  46.6 9.6 %all-to-all-done.1 = bf16[4,64,1152]{2,1,0:T(8,128)(2,1)S(1)} async-done(((bf16[4,64,1152]{2,1,0:T(8,128)(2,1)}), bf16[4,64,1152]{2,1,0:T(8,128)(2,1)S(1)}, u32[]{:S(2)}, u32[]{:S(2)}) %all-to-all-start.1) | async-done | bytes 589856 | tf_op jit(solution)/shard_map/all_to_all | solution.py:19
  56.4 1.5 fusion.4
  58.1 0.8 copy.18
  58.9 6.3 %all-to-all-start.2 = ((f32[32,8,192]{2,1,0:T(8,128)}), f32[32,8,192]{2,1,0:T(8,128)S(1)}, u32[]{:S(2)}, u32[]{:S(2)}) async-start(f32[32,8,192]{2,1,0:T(8,128)} %bitcast.5), calls=%async_computation.2 | async-start | bytes 524288 | tf_op jit(solution)/shard_map/all_to_all | solution.py:19
  65.3 6.9 %all-to-all-done.2.refs_2_ = f32[32,8,192]{2,1,0:T(8,128)S(1)} async-done(((f32[32,8,192]{2,1,0:T(8,128)}), f32[32,8,192]{2,1,0:T(8,128)S(1)}, u32[]{:S(2)}, u32[]{:S(2)}) %all-to-all-start.2) | async-done | bytes 196640 | tf_op jit(solution)/shard_map/all_to_all | solution.py:19
  72.8 5.4 %all-to-all-start.3 = ((bf16[8,8,192]{2,1,0:T(8,128)(2,1)}), bf16[8,8,192]{2,1,0:T(8,128)(2,1)S(1)}, u32[]{:S(2)}, u32[]{:S(2)}) async-start(bf16[8,8,192]{2,1,0:T(8,128)(2,1)} %broadcast_in_dim.25), calls=%async_computation.3 | async-start | bytes 65536 | tf_op jit(solution)/shard_map/all_to_all | solution.py:19
  78.2 0.9 slice_bitcast_fusion.refs_2_
  79.2 2.4 %all-to-all-done.3 = bf16[8,8,192]{2,1,0:T(8,128)(2,1)S(1)} async-done(((bf16[8,8,192]{2,1,0:T(8,128)(2,1)}), bf16[8,8,192]{2,1,0:T(8,128)(2,1)S(1)}, u32[]{:S(2)}, u32[]{:S(2)}) %all-to-all-start.3) | async-done | bytes 24608 | tf_op jit(solution)/shard_map/all_to_all | solution.py:19
  81.6 1.0 shard_map.170
  83.3 11.9 %all-to-all-start.4 = ((bf16[16,4,1280]{2,1,0:T(4,128)(2,1)}), bf16[16,4,1280]{2,1,0:T(4,128)(2,1)S(1)}, u32[]{:S(2)}, u32[]{:S(2)}) async-start(bf16[16,4,1280]{2,1,0:T(4,128)(2,1)} %reshape.185), calls=%async_computation.4 | async-start | bytes 327680 | tf_op jit(solution)/shard_map/all_to_all | solution.py:19
  95.3 1.7 gather_fusion
  96.9 2.9 %gather_fusion.1 = bf16[32,128,128]{2,1,0:T(8,128)(2,1)} fusion(bf16[32,128,128]{2,1,0:T(8,128)(2,1)} %param.21, s32[1024]{0:T(1024)S(1)} %pad_clamp_fusion), kind=kCustom, calls=%fused_computation.1 | custom fusion | bytes 2097280 | tf_op jit(solution)/shard_map/gather | solution.py:252
  100.0 2.3 %collective-permute-start.3 = (bf16[2,64,2048]{2,1,0:T(8,128)(2,1)S(1)}, bf16[2,64,2048]{2,1,0:T(8,128)(2,1)S(1)}, u32[]{:S(2)}, u32[]{:S(2)}) collective-permute-start(bf16[2,64,2048]{2,1,0:T(8,128)(2,1)S(1)} %shard_map.171.refs_3_), channel_id=1, source_target_pairs={{0,128},{128,256},{256,384},{384,0},{1,129},{129,257},{257,385},{3... | collective-permute-start | bytes 1572872 | tf_op jit(solution)/shard_map/ppermute | solution.py:190
  102.3 4.0 %collective-permute-start.4 = (bf16[2,64,2048]{2,1,0:T(8,128)(2,1)S(1)}, bf16[2,64,2048]{2,1,0:T(8,128)(2,1)S(1)}, u32[]{:S(2)}, u32[]{:S(2)}) collective-permute-start(bf16[2,64,2048]{2,1,0:T(8,128)(2,1)S(1)} %shard_map.171.refs_3_), channel_id=1, source_target_pairs={{0,256},{128,384},{256,0},{384,128},{1,257},{129,385},{257,1},{385... | collective-permute-start | bytes 1572872 | tf_op jit(solution)/shard_map/ppermute | solution.py:190
  106.3 3.2 %collective-permute-start.5 = (bf16[2,64,2048]{2,1,0:T(8,128)(2,1)S(1)}, bf16[2,64,2048]{2,1,0:T(8,128)(2,1)S(1)}, u32[]{:S(2)}, u32[]{:S(2)}) collective-permute-start(bf16[2,64,2048]{2,1,0:T(8,128)(2,1)S(1)} %shard_map.171.refs_3_), channel_id=1, source_target_pairs={{0,384},{128,0},{256,128},{384,256},{1,385},{129,1},{257,129},{385... | collective-permute-start | bytes 1572872 | tf_op jit(solution)/shard_map/ppermute | solution.py:190
  109.5 1.2 all-to-all-done.4
  110.9 1.7 %fusion.30 = (f32[4,8]{1,0:T(4,128)S(1)}, f32[4,8,1024]{2,1,0:T(8,128)S(1)}) fusion(bf16[4,1024,128]{2,1,0:T(8,128)(2,1)} %bitcast.43, bf16[1,4,8,128]{3,1,2,0:T(4,128)(2,1)S(1)} %fusion.13, pred[4,1024]{1,0:T(4,128)(4,1)S(1)} %iota_compare_fusion), kind=kOutput, calls=%fused_computation.55 | convolution fusion | flops 8486880 | bytes 1192064 | tf_op jit(solution)/shard_map/bkgd,btkd->bkgt/dot_general | solution.py:256
  113.8 24.0 %all_to_all.40 = bf16[16,4,1024]{2,1,0:T(4,128)(2,1)S(1)} all-to-all(bf16[16,4,1024]{2,1,0:T(4,128)(2,1)S(1)} %broadcast_in_dim.50), channel_id=1, replica_groups=mesh['y'=4,'z'=16,'tensor'=8] {'z'}, dimensions={0} | all-to-all | bytes 262144 | tf_op jit(solution)/shard_map/all_to_all | solution.py:19
  138.6 1.0 shard_map.172
  139.6 8.5 %all_to_all.41.refs_1_ = f32[8,32,128]{2,1,0:T(8,128)S(1)} all-to-all(f32[8,32,128]{2,1,0:T(8,128)S(1)} %shard_map.172), channel_id=1, replica_groups=mesh['y'=4,'z'=16,'tensor'=8] {'tensor'}, dimensions={0} | all-to-all | bytes 262144 | tf_op jit(solution)/shard_map/all_to_all | solution.py:19
  148.1 1.0 shard_map.173
  149.2 18.3 %all_to_all.42 = bf16[16,4,1024]{2,1,0:T(4,128)(2,1)S(1)} all-to-all(bf16[16,4,1024]{2,1,0:T(4,128)(2,1)S(1)} %reshape.190), channel_id=1, replica_groups=mesh['y'=4,'z'=16,'tensor'=8] {'z'}, dimensions={0} | all-to-all | bytes 262144 | tf_op jit(solution)/shard_map/all_to_all | solution.py:19
  (70 shorter events, 6.9 us)
Async XLA Ops:
  0.6 94.6 %copy-start = (bf16[32,128,128]{2,1,0:T(8,128)(2,1)S(1)}, bf16[32,128,128]{2,1,0:T(8,128)(2,1)}, u32[]{:S(2)}) copy-start(bf16[32,128,128]{2,1,0:T(8,128)(2,1)} %param.20) | copy-start | bytes 3145732
  0.6 18.7 %copy-start.3 = (bf16[2,64,1024]{2,1,0:T(8,128)(2,1)S(1)}, bf16[2,64,1024]{2,1,0:T(8,128)(2,1)}, u32[]{:S(2)}) copy-start(bf16[2,64,1024]{2,1,0:T(8,128)(2,1)} %refs_0_.3) | copy-start | bytes 786436
  0.7 0.8 copy-start.6
  1.5 0.7 copy-start.9
  2.1 0.7 copy-start.10
  4.0 15.4 %copy-start.4 = (bf16[2,64,128]{2,1,0:T(8,128)(2,1)S(1)}, bf16[2,64,128]{2,1,0:T(8,128)(2,1)}, u32[]{:S(2)}) copy-start(bf16[2,64,128]{2,1,0:T(8,128)(2,1)} %refs_1_.4) | copy-start | bytes 98308
  4.0 15.4 %copy-start.5 = (bf16[2,64,128]{2,1,0:T(8,128)(2,1)S(1)}, bf16[2,64,128]{2,1,0:T(8,128)(2,1)}, u32[]{:S(2)}) copy-start(bf16[2,64,128]{2,1,0:T(8,128)(2,1)} %refs_2_.3) | copy-start | bytes 98308
  4.0 37.3 %all-to-all-start = ((bf16[16,4,1152]{2,1,0:T(4,128)(2,1)}), bf16[16,4,1152]{2,1,0:T(4,128)(2,1)S(1)}, u32[]{:S(2)}, u32[]{:S(2)}) async-start(bf16[16,4,1152]{2,1,0:T(4,128)(2,1)} %shard_map.167), calls=%async_computation | async-start | bytes 294912 | tf_op jit(solution)/shard_map/all_to_all | solution.py:19
  19.4 12.6 %collective-permute-start = (bf16[2,64,1280]{2,1,0:T(8,128)(2,1)S(1)}, bf16[2,64,1280]{2,1,0:T(8,128)(2,1)S(1)}, u32[]{:S(2)}, u32[]{:S(2)}) collective-permute-start(bf16[2,64,1280]{2,1,0:T(8,128)(2,1)S(1)} %shard_map.168.refs_3_), channel_id=1, source_target_pairs={{0,128},{128,256},{256,384},{384,0},{1,129},{129,257},{257,385},{3... | collective-permute-start | bytes 983048 | tf_op jit(solution)/shard_map/ppermute | solution.py:190
  22.9 17.0 %collective-permute-start.1 = (bf16[2,64,1280]{2,1,0:T(8,128)(2,1)S(1)}, bf16[2,64,1280]{2,1,0:T(8,128)(2,1)S(1)}, u32[]{:S(2)}, u32[]{:S(2)}) collective-permute-start(bf16[2,64,1280]{2,1,0:T(8,128)(2,1)S(1)} %shard_map.168.refs_3_), channel_id=1, source_target_pairs={{0,256},{128,384},{256,0},{384,128},{1,257},{129,385},{257,1},{385... | collective-permute-start | bytes 983048 | tf_op jit(solution)/shard_map/ppermute | solution.py:190
  27.7 13.6 %collective-permute-start.2 = (bf16[2,64,1280]{2,1,0:T(8,128)(2,1)S(1)}, bf16[2,64,1280]{2,1,0:T(8,128)(2,1)S(1)}, u32[]{:S(2)}, u32[]{:S(2)}) collective-permute-start(bf16[2,64,1280]{2,1,0:T(8,128)(2,1)S(1)} %shard_map.168.refs_3_), channel_id=1, source_target_pairs={{0,384},{128,0},{256,128},{384,256},{1,385},{129,1},{257,129},{385... | collective-permute-start | bytes 983048 | tf_op jit(solution)/shard_map/ppermute | solution.py:190
  42.1 14.1 %all-to-all-start.1 = ((bf16[4,64,1152]{2,1,0:T(8,128)(2,1)}), bf16[4,64,1152]{2,1,0:T(8,128)(2,1)S(1)}, u32[]{:S(2)}, u32[]{:S(2)}) async-start(bf16[4,64,1152]{2,1,0:T(8,128)(2,1)} %shard_map.169), calls=%async_computation.1 | async-start | bytes 1179648 | tf_op jit(solution)/shard_map/all_to_all | solution.py:19
  58.9 13.3 %all-to-all-start.2 = ((f32[32,8,192]{2,1,0:T(8,128)}), f32[32,8,192]{2,1,0:T(8,128)S(1)}, u32[]{:S(2)}, u32[]{:S(2)}) async-start(f32[32,8,192]{2,1,0:T(8,128)} %bitcast.5), calls=%async_computation.2 | async-start | bytes 524288 | tf_op jit(solution)/shard_map/all_to_all | solution.py:19
  65.3 16.3 %copy-start.7 = (s32[8]{0:T(128)}, s32[8]{0:T(128)S(1)}, u32[]{:S(2)}) copy-start(s32[8]{0:T(128)S(1)} %add.66.refs_0_) | copy-start | bytes 100
  72.8 8.7 %all-to-all-start.3 = ((bf16[8,8,192]{2,1,0:T(8,128)(2,1)}), bf16[8,8,192]{2,1,0:T(8,128)(2,1)S(1)}, u32[]{:S(2)}, u32[]{:S(2)}) async-start(bf16[8,8,192]{2,1,0:T(8,128)(2,1)} %broadcast_in_dim.25), calls=%async_computation.3 | async-start | bytes 65536 | tf_op jit(solution)/shard_map/all_to_all | solution.py:19
  83.3 11.9 %copy-start.14 = (s32[4,8]{1,0:T(4,128)S(1)}, s32[4,8]{1,0:T(4,128)}, u32[]{:S(2)}) copy-start(s32[4,8]{1,0:T(4,128)} %param.22) | copy-start | bytes 388
  83.3 27.4 %all-to-all-start.4 = ((bf16[16,4,1280]{2,1,0:T(4,128)(2,1)}), bf16[16,4,1280]{2,1,0:T(4,128)(2,1)S(1)}, u32[]{:S(2)}, u32[]{:S(2)}) async-start(bf16[16,4,1280]{2,1,0:T(4,128)(2,1)} %reshape.185), calls=%async_computation.4 | async-start | bytes 327680 | tf_op jit(solution)/shard_map/all_to_all | solution.py:19
  96.9 2.9 %copy-start.17 = (s32[4]{0:T(128)S(1)}, s32[4]{0:T(128)}, u32[]{:S(2)}) copy-start(s32[4]{0:T(128)} %param.23) | copy-start | bytes 52
  96.9 3.0 %copy-start.1 = (bf16[2,1024,64]{1,2,0:T(8,128)(2,1)S(1)}, bf16[2,1024,64]{1,2,0:T(8,128)(2,1)}, u32[]{:S(2)}) copy-start(bf16[2,1024,64]{1,2,0:T(8,128)(2,1)} %param.30) | copy-start | bytes 786436
  96.9 3.0 %copy-start.2 = (bf16[2,64,1024]{2,1,0:T(8,128)(2,1)S(1)}, bf16[2,64,1024]{2,1,0:T(8,128)(2,1)}, u32[]{:S(2)}) copy-start(bf16[2,64,1024]{2,1,0:T(8,128)(2,1)} %refs_1_.5) | copy-start | bytes 786436
  100.0 10.8 %copy-start.15 = (bf16[4,128]{1,0:T(4,128)(2,1)S(1)}, bf16[4,128]{1,0:T(4,128)(2,1)}, u32[]{:S(2)}) copy-start(bf16[4,128]{1,0:T(4,128)(2,1)} %param.19) | copy-start | bytes 3076
  100.0 10.8 %copy-start.16 = (bf16[4,128]{1,0:T(4,128)(2,1)S(1)}, bf16[4,128]{1,0:T(4,128)(2,1)}, u32[]{:S(2)}) copy-start(bf16[4,128]{1,0:T(4,128)(2,1)} %param.18) | copy-start | bytes 3076
  100.0 10.8 %copy-start.13 = (bf16[4,1024]{1,0:T(4,128)(2,1)S(1)}, bf16[4,1024]{1,0:T(4,128)(2,1)}, u32[]{:S(2)}) copy-start(bf16[4,1024]{1,0:T(4,128)(2,1)} %param.17) | copy-start | bytes 24580
  100.0 37.9 %collective-permute-start.3 = (bf16[2,64,2048]{2,1,0:T(8,128)(2,1)S(1)}, bf16[2,64,2048]{2,1,0:T(8,128)(2,1)S(1)}, u32[]{:S(2)}, u32[]{:S(2)}) collective-permute-start(bf16[2,64,2048]{2,1,0:T(8,128)(2,1)S(1)} %shard_map.171.refs_3_), channel_id=1, source_target_pairs={{0,128},{128,256},{256,384},{384,0},{1,129},{129,257},{257,385},{3... | collective-permute-start | bytes 1572872 | tf_op jit(solution)/shard_map/ppermute | solution.py:190
  102.3 35.6 %collective-permute-start.4 = (bf16[2,64,2048]{2,1,0:T(8,128)(2,1)S(1)}, bf16[2,64,2048]{2,1,0:T(8,128)(2,1)S(1)}, u32[]{:S(2)}, u32[]{:S(2)}) collective-permute-start(bf16[2,64,2048]{2,1,0:T(8,128)(2,1)S(1)} %shard_map.171.refs_3_), channel_id=1, source_target_pairs={{0,256},{128,384},{256,0},{384,128},{1,257},{129,385},{257,1},{385... | collective-permute-start | bytes 1572872 | tf_op jit(solution)/shard_map/ppermute | solution.py:190
  106.3 31.7 %collective-permute-start.5 = (bf16[2,64,2048]{2,1,0:T(8,128)(2,1)S(1)}, bf16[2,64,2048]{2,1,0:T(8,128)(2,1)S(1)}, u32[]{:S(2)}, u32[]{:S(2)}) collective-permute-start(bf16[2,64,2048]{2,1,0:T(8,128)(2,1)S(1)} %shard_map.171.refs_3_), channel_id=1, source_target_pairs={{0,384},{128,0},{256,128},{384,256},{1,385},{129,1},{257,129},{385... | collective-permute-start | bytes 1572872 | tf_op jit(solution)/shard_map/ppermute | solution.py:190
  110.7 2.2 %copy-start.11 = (bf16[32,128,128]{2,1,0:T(8,128)(2,1)S(1)}, bf16[32,128,128]{2,1,0:T(8,128)(2,1)}, u32[]{:S(2)}) copy-start(bf16[32,128,128]{2,1,0:T(8,128)(2,1)} %gather_fusion.1) | copy-start | bytes 3145732
  113.2 0.6 copy-start.12
  137.9 0.7 copy-start.8

commit v5 on v4

--- a/solution.py
+++ b/solution.py
@@ -33,21 +33,14 @@
 SMEM = pl.BlockSpec(memory_space=pltpu.SMEM)
 
 
-def call(kernel, shape, dtype, *operands, scalars=1, after=()):
-    count = len(operands)
-
-    def body(*refs):
-        kernel(*refs[:count], *refs[count + len(after) :])
-
+def call(kernel, shape, dtype, *operands, scalars=1):
     return pl.pallas_call(
-        body,
+        kernel,
         out_shape=jax.ShapeDtypeStruct(shape, dtype),
-        in_specs=[SMEM] * scalars
-        + [VMEM] * (count - scalars)
-        + [pl.BlockSpec(memory_space=pl.ANY)] * len(after),
+        in_specs=[SMEM] * scalars + [VMEM] * (len(operands) - scalars),
         out_specs=VMEM,
         compiler_params=pltpu.CompilerParams(vmem_limit_bytes=32 * 2**20),
-    )(*operands, *after)
+    )(*operands)
 
 
 def first_blocks(id_ref, slot_ref, hidden_ref, out_ref):
@@ -84,68 +77,49 @@
 
 
 def grown(slots_ref, tags, ranks, pages, at, width):
-    total = None
-    for k, page in enumerate(pages):
-        count, rank, _ = page.shape
-        mine = [picked(slots_ref, tags, ranks, k * count + j) for j in range(count)]
-        product = jnp.dot(
-            jnp.concatenate(mine, axis=1).astype(jnp.bfloat16),
-            page[:, :, at : at + width].reshape(count * rank, width),
-            preferred_element_type=jnp.float32,
-        )
-        total = product if total is None else total + product
-    return (adapter_scale * total).astype(jnp.bfloat16)
+    count, rank, _ = pages.shape
+    mine = [picked(slots_ref, tags, ranks, k) for k in range(count)]
+    product = jnp.dot(
+        jnp.concatenate(mine, axis=1).astype(jnp.bfloat16),
+        pages[:, :, at : at + width].reshape(count * rank, width),
+        preferred_element_type=jnp.float32,
+    )
+    return (adapter_scale * product).astype(jnp.bfloat16)
 
 
 def make_up_first(cuts):
-    def up_first(slots_ref, ranks_ref, rows_ref, *refs):
-        pages, out_ref = refs[:-1], refs[-1]
-        rank = pages[0].shape[1]
+    def up_first(slots_ref, ranks_ref, rows_ref, pages, out_ref):
+        rank = pages.shape[1]
         tags = tags_of(rows_ref, rows_ref.shape[1] - 128, rank)
         ranks = ranks_ref[...].astype(jnp.float32)
         for i in range(3):
-            out_ref[:, cuts[i] : cuts[i + 1]] = grown(
-                slots_ref,
-                tags,
-                ranks[:, i * rank : (i + 1) * rank],
-                pages,
-                cuts[i],
-                cuts[i + 1] - cuts[i],
-            )
+            mine, width = ranks[:, i * rank : (i + 1) * rank], cuts[i + 1] - cuts[i]
+            out_ref[:, cuts[i] : cuts[i + 1]] = grown(slots_ref, tags, mine, pages, cuts[i], width)
 
     return up_first
 
 
-def make_down_second(at):
-    def down_second(slots_ref, out_rows_ref, rows_ref, *refs):
-        pages, out_ref = refs[:-1], refs[-1]
-        count, rank, _ = pages[0].shape
-        rows = out_rows_ref[...]
-        tags = tags_of(rows_ref, rows_ref.shape[1] - 128, rank)
-        total = jnp.zeros((rows.shape[0], rank), jnp.float32)
-        for k, page in enumerate(pages):
-            for j in range(count):
-                weight = page[j, :, at : at + rows.shape[1]]
-                product = lax.dot_general(rows, weight, NT, preferred_element_type=jnp.float32)
-                total = total + picked(slots_ref, tags, product, k * count + j)
-        half = rows.shape[0] // 2
-        side = jnp.concatenate([total[:half], total[half:]], axis=1)
-        for t in range(out_ref.shape[0]):
-            out_ref[t] = side
-
-    return down_second
-
-
-def make_up_second(at):
-    def up_second(slots_ref, parts_ref, rows_ref, *refs):
-        pages, out_ref = refs[:-1], refs[-1]
-        rank = pages[0].shape[1]
-        side = jnp.sum(parts_ref[...], axis=0).astype(jnp.bfloat16).astype(jnp.float32)
-        ranks = jnp.concatenate([side[:, :rank], side[:, rank:]], axis=0)
-        tags = tags_of(rows_ref, rows_ref.shape[1] - 128, rank)
-        out_ref[...] = grown(slots_ref, tags, ranks, pages, at, out_ref.shape[1])
-
-    return up_second
+def down_second(slots_ref, out_rows_ref, rows_ref, pages, out_ref):
+    count, rank, width = pages.shape
+    rows = out_rows_ref[...]
+    tags = tags_of(rows_ref, rows_ref.shape[1] - 128, rank)
+    weights = pages[...].reshape(count * rank, width)
+    product = lax.dot_general(rows, weights, NT, preferred_element_type=jnp.float32)
+    total = jnp.zeros((rows.shape[0], rank), jnp.float32)
+    for k in range(count):
+        total = total + picked(slots_ref, tags, product[:, k * rank : (k + 1) * rank], k)
+    half = rows.shape[0] // 2
+    side = jnp.concatenate([total[:half], total[half:]], axis=1)
+    for t in range(out_ref.shape[0]):
+        out_ref[t] = side
+
+
+def up_second(slots_ref, parts_ref, rows_ref, pages, out_ref):
+    rank = pages.shape[1]
+    side = jnp.sum(parts_ref[...], axis=0).astype(jnp.bfloat16).astype(jnp.float32)
+    ranks = jnp.concatenate([side[:, :rank], side[:, rank:]], axis=0)
+    tags = tags_of(rows_ref, rows_ref.shape[1] - 128, rank)
+    out_ref[...] = grown(slots_ref, tags, ranks, pages, 0, out_ref.shape[1])
 
 
 def to_requests(rows):
@@ -175,23 +149,21 @@
     y_size, z_size, t_size = lax.axis_size(Y), lax.axis_size(Z), lax.axis_size(T)
     rank, width_q, width_k = query_up_weight.shape[1], q_base.shape[1], base_key.shape[1]
     cuts = (0, width_q, width_q + width_k, width_q + 2 * width_k)
-    own_y = lax.axis_index(Y)
-    places = jnp.arange(y_size, dtype=jnp.int32)
     numbers = jnp.arange(local_count, dtype=jnp.int32)
-    column_slots = (
-        ((own_y - places[:, None]) % y_size * z_size + lax.axis_index(Z)) * local_count + numbers
-    ).reshape(-1)
-
-    def packed(*weights, after=()):
-        width = sum(weight.shape[2] for weight in weights)
-        shape = (local_count, rank, width)
-        mine = call(pack, shape, jnp.bfloat16, *weights, scalars=0, after=after)
-        return [mine] + [
-            lax.ppermute(mine, Y, [(i, (i + k) % y_size) for i in range(y_size)])
-            for k in range(1, y_size)
-        ]
-
-    up_pages = packed(query_up_weight, key_up_weight, value_up_weight)
+
+    def slots_of(y):
+        return (y * z_size + lax.axis_index(Z)) * local_count + numbers
+
+    owned_slots = slots_of(lax.axis_index(Y))
+    column_slots = slots_of(jnp.arange(y_size, dtype=jnp.int32)[:, None]).reshape(-1)
+    up_shape = (local_count, rank, cuts[3])
+    up_weights = call(
+        pack, up_shape, jnp.bfloat16, query_up_weight, key_up_weight, value_up_weight, scalars=0
+    )
+    up_pages, down_pages, out_pages = [
+        lax.all_gather(weight, Y, axis=0, tiled=True)
+        for weight in (up_weights, jnp.swapaxes(output_down_weight, 1, 2), output_up_weight)
+    ]
     z_blocks = call(
         first_blocks,
         (z_size, local_rows, local_width + 128),
@@ -207,13 +179,12 @@
         jnp.bfloat16,
         exchange(z_blocks, Z),
         scalars=0,
-        after=up_pages[1:],
     )
     z_rows = y_blocks[0]
     all_rows = exchange(y_blocks, Y).reshape(y_size * z_size * local_rows, -1)
 
     all_slots = all_rows[:, local_width].astype(jnp.int32)
-    owned_mask = (all_slots[:, None] == column_slots[None, :local_count]).astype(jnp.float32)
+    owned_mask = (all_slots[:, None] == owned_slots[None, :]).astype(jnp.float32)
     product = jnp.einsum(
         "nd,jdr->njr",
         all_rows[:, :local_width],
@@ -231,10 +202,7 @@
         column_slots,
         ranks,
         z_rows,
-        *up_pages,
-    )
-    out_pages = packed(
-        jnp.swapaxes(output_down_weight, 1, 2), output_up_weight, after=(shares,)
+        up_pages,
     )
     adapter_delta = to_requests(delta)
     width_q = q_base.shape[1]
@@ -285,22 +253,22 @@
     attention = (mixed / total[..., None]).reshape(local_rows, width_q).astype(jnp.bfloat16)
     out_rows = spread(attention, Z).reshape(z_size * local_rows, -1)
     sides = call(
-        make_down_second(0),
+        down_second,
         (t_size, z_size * local_rows // 2, 2 * rank),
         jnp.float32,
         column_slots,
         out_rows,
         z_rows,
-        *out_pages,
+        down_pages,
     )
     term = call(
-        make_up_second(local_width),
+        up_second,
         (z_size * local_rows, output_up_weight.shape[2]),
         jnp.bfloat16,
         column_slots,
         exchange(sides, T),
         z_rows,
-        *out_pages,
+        out_pages,
     )
     output_adapter_term = to_requests(term)
     return (attention, output_adapter_term.astype(jnp.bfloat16))

time: 170 us -> 171 us (level)
  starting transfers between devices: 64.3 us -> 30.4 us
  blocking collectives: 50.8 us -> 67 us
  between operations: 0.99 us -> 14 us
  waiting for transfers between devices: 30.5 us -> 34.2 us
  local copies, waits for them, and re-layouts: 11.4 us -> 14.5 us
  matrix products: 3.7 us -> 1.29 us
    ppermute x6 -> x0, starting transfers between devices: 21 us -> none  [packed(): lax.ppermute(mine, Y, [(i, (i + k) % y_size) for i in range(y_size)])]
    all_to_all x3, blocking collectives: 50.8 us -> 67 us  [exchange(): return lax.all_to_all(blocks, axis, 0, 0)]
    all_to_all x5, starting transfers between devices: 43.3 us -> 30.3 us  [exchange(): return lax.all_to_all(blocks, axis, 0, 0)]
    all_to_all x5, waiting for transfers between devices: 20.2 us -> 32.8 us  [exchange(): return lax.all_to_all(blocks, axis, 0, 0)]
    ppermute x6 -> x0, waiting for transfers between devices: 10.3 us -> none  [packed(): lax.ppermute(mine, Y, [(i, (i + k) % y_size) for i in range(y_size)])]
    unnamed x37 -> x35, local copies, waits for them, and re-layouts: 3.37 us -> 8.38 us
    pallas_call x7 -> x6, Pallas kernels: 5.11 us -> 5.86 us  [call(): pl.pallas_call(kernel, out_shape=jax.ShapeDtypeStruct(shape, dtype), in_s...]
  transfers between devices with their start and end apart: 11 -> 8, of which waited for: 7 -> 5; matrix products, arithmetic and copies ran while one was open for 5% -> 5% of each run, Pallas kernels for 0% -> 2%
where the time goes in v5:
time: 171 us; the launch traced here: 169 us
  blocking collectives  67 us (39%)
  waiting for transfers between devices  34.2 us (20%)
  starting transfers between devices  30.4 us (18%)
  local copies, waits for them, and re-layouts  14.5 us (8%)
  between operations  14 us (8%)
  Pallas kernels  5.86 us (3%)
    all_to_all x3, blocking collectives, exchange(): return lax.all_to_all(blocks, axis, 0, 0)  67 us
    all_to_all x5, waiting for transfers between devices, exchange(): return lax.all_to_all(blocks, axis, 0, 0)  32.8 us
    all_to_all x5, starting transfers between devices, exchange(): return lax.all_to_all(blocks, axis, 0, 0)  30.3 us
    unnamed x35, local copies, waits for them, and re-layouts  8.38 us
    pallas_call x6, Pallas kernels, call(): pl.pallas_call(kernel, out_shape=jax.ShapeDtypeStruct(shape, dtype), in_s...  5.86 us
  transfers between devices with their start and end apart: 8, of which 5 were waited for; matrix products, arithmetic and copies ran while one was open for 5% of the time, Pallas kernels for 2%

profile of v5, /device:TPU:6, one launch (start us, length us, event | category | flops | bytes accessed | tf_op | source)
XLA Modules:
  0.0 168.7 jit_solution(366317905187727354)
XLA Ops:
  7.2 1.0 copy-done.4
  8.3 0.8 copy-done.5
  9.0 0.8 copy-done.6
  9.8 0.7 shard_map.169
  10.6 0.7 copy-done.7
  13.1 30.3 %all_to_all.40.from_z_ref = bf16[16,4,1152]{2,1,0:T(4,128)(2,1)S(1)} all-to-all(bf16[16,4,1152]{2,1,0:T(4,128)(2,1)S(1)} %shard_map.167), channel_id=1, replica_groups=mesh['y'=4,'z'=16,'tensor'=8] {'z'}, dimensions={0} | all-to-all | bytes 294912 | tf_op jit(solution)/shard_map/all_to_all | solution.py:19
  43.4 0.9 shard_map.168
  44.3 4.5 %all-to-all-start.1 = ((bf16[4,64,1152]{2,1,0:T(8,128)(2,1)}), bf16[4,64,1152]{2,1,0:T(8,128)(2,1)S(1)}, u32[]{:S(2)}, u32[]{:S(2)}) async-start(bf16[4,64,1152]{2,1,0:T(8,128)(2,1)} %shard_map.168), calls=%async_computation.1 | async-start | bytes 1179648 | tf_op jit(solution)/shard_map/all_to_all | solution.py:19
  48.8 0.7 all-gather.6.cloned.1.call-update
  49.5 7.7 %all-to-all-done.1 = bf16[4,64,1152]{2,1,0:T(8,128)(2,1)S(1)} async-done(((bf16[4,64,1152]{2,1,0:T(8,128)(2,1)}), bf16[4,64,1152]{2,1,0:T(8,128)(2,1)S(1)}, u32[]{:S(2)}, u32[]{:S(2)}) %all-to-all-start.1) | async-done | bytes 589856 | tf_op jit(solution)/shard_map/all_to_all | solution.py:19
  57.8 0.8 copy.18
  58.7 5.5 %all-to-all-start.2 = ((f32[32,8,192]{2,1,0:T(8,128)}), f32[32,8,192]{2,1,0:T(8,128)S(1)}, u32[]{:S(2)}, u32[]{:S(2)}) async-start(f32[32,8,192]{2,1,0:T(8,128)} %bitcast.4), calls=%async_computation.2 | async-start | bytes 524288 | tf_op jit(solution)/shard_map/all_to_all | solution.py:19
  64.4 6.9 %all-to-all-done.2 = f32[32,8,192]{2,1,0:T(8,128)S(1)} async-done(((f32[32,8,192]{2,1,0:T(8,128)}), f32[32,8,192]{2,1,0:T(8,128)S(1)}, u32[]{:S(2)}, u32[]{:S(2)}) %all-to-all-start.2) | async-done | bytes 196640 | tf_op jit(solution)/shard_map/all_to_all | solution.py:19
  71.9 5.4 %all-to-all-start.3 = ((bf16[8,8,192]{2,1,0:T(8,128)(2,1)}), bf16[8,8,192]{2,1,0:T(8,128)(2,1)S(1)}, u32[]{:S(2)}, u32[]{:S(2)}) async-start(bf16[8,8,192]{2,1,0:T(8,128)(2,1)} %broadcast_in_dim.25), calls=%async_computation.3 | async-start | bytes 65536 | tf_op jit(solution)/shard_map/all_to_all | solution.py:19
  77.3 0.9 slice_bitcast_fusion.rows_ref
  78.2 2.4 %all-to-all-done.3 = bf16[8,8,192]{2,1,0:T(8,128)(2,1)S(1)} async-done(((bf16[8,8,192]{2,1,0:T(8,128)(2,1)}), bf16[8,8,192]{2,1,0:T(8,128)(2,1)S(1)}, u32[]{:S(2)}, u32[]{:S(2)}) %all-to-all-start.3) | async-done | bytes 24608 | tf_op jit(solution)/shard_map/all_to_all | solution.py:19
  80.6 1.3 copy-done.1
  82.0 0.9 shard_map.170
  82.9 0.7 reshape.167
  83.6 9.5 %all-to-all-start.4 = ((bf16[16,4,1280]{2,1,0:T(4,128)(2,1)}), bf16[16,4,1280]{2,1,0:T(4,128)(2,1)S(1)}, u32[]{:S(2)}, u32[]{:S(2)}) async-start(bf16[16,4,1280]{2,1,0:T(4,128)(2,1)} %reshape.167), calls=%async_computation.4 | async-start | bytes 327680 | tf_op jit(solution)/shard_map/all_to_all | solution.py:19
  93.2 0.7 all-gather.8.cloned.1.call-update
  94.0 0.7 gather_fusion
  94.8 2.0 %gather_fusion.1 = bf16[32,128,128]{2,1,0:T(8,128)(2,1)S(1)} fusion(bf16[32,128,128]{2,1,0:T(8,128)(2,1)} %param.21, s32[1024]{0:T(1024)S(1)} %pad_clamp_fusion), kind=kCustom, calls=%fused_computation.1 | custom fusion | bytes 2097280 | tf_op jit(solution)/shard_map/gather | solution.py:220
  96.9 11.8 %all-to-all-done.4 = bf16[16,4,1280]{2,1,0:T(4,128)(2,1)S(1)} async-done(((bf16[16,4,1280]{2,1,0:T(4,128)(2,1)}), bf16[16,4,1280]{2,1,0:T(4,128)(2,1)S(1)}, u32[]{:S(2)}, u32[]{:S(2)}) %all-to-all-start.4) | async-done | bytes 163872 | tf_op jit(solution)/shard_map/all_to_all | solution.py:19
  110.0 18.6 %all_to_all.41 = bf16[16,4,1024]{2,1,0:T(4,128)(2,1)S(1)} all-to-all(bf16[16,4,1024]{2,1,0:T(4,128)(2,1)S(1)} %broadcast_in_dim.50), channel_id=1, replica_groups=mesh['y'=4,'z'=16,'tensor'=8] {'z'}, dimensions={0} | all-to-all | bytes 262144 | tf_op jit(solution)/shard_map/all_to_all | solution.py:19
  128.7 1.2 copy-done.2
  129.9 1.8 %shard_map.171 = f32[8,32,128]{2,1,0:T(8,128)} custom-call(s32[8]{0:T(128)S(1)} %add.67.slots_ref, bf16[64,1024]{1,0:T(8,128)(2,1)S(1)} %reshape.171.out_rows_ref, bf16[64,1152]{1,0:T(8,128)(2,1)S(1)} %slice_bitcast_fusion.rows_ref, bf16[8,64,1024]{2,1,0:T(8,128)(2,1)S(1)} %copy-done.2), custom_call_target="tpu_custom_call" | custom-call | tf_op jit(solution)/shard_map/pallas_call | solution.py:37
  131.7 5.4 %all-to-all-start.6 = ((f32[8,32,128]{2,1,0:T(8,128)}), f32[8,32,128]{2,1,0:T(8,128)S(1)}, u32[]{:S(2)}, u32[]{:S(2)}) async-start(f32[8,32,128]{2,1,0:T(8,128)} %shard_map.171), calls=%async_computation.6 | async-start | bytes 262144 | tf_op jit(solution)/shard_map/all_to_all | solution.py:19
  137.1 4.0 %all-to-all-done.6.parts_ref = f32[8,32,128]{2,1,0:T(8,128)S(1)} async-done(((f32[8,32,128]{2,1,0:T(8,128)}), f32[8,32,128]{2,1,0:T(8,128)S(1)}, u32[]{:S(2)}, u32[]{:S(2)}) %all-to-all-start.6) | async-done | bytes 131104 | tf_op jit(solution)/shard_map/all_to_all | solution.py:19
  141.1 1.2 copy-done.3
  142.3 0.9 shard_map.172
  143.3 18.2 %all_to_all.42 = bf16[16,4,1024]{2,1,0:T(4,128)(2,1)S(1)} all-to-all(bf16[16,4,1024]{2,1,0:T(4,128)(2,1)S(1)} %reshape.172), channel_id=1, replica_groups=mesh['y'=4,'z'=16,'tensor'=8] {'z'}, dimensions={0} | all-to-all | bytes 262144 | tf_op jit(solution)/shard_map/all_to_all | solution.py:19
  (64 shorter events, 5.7 us)
Async XLA Ops:
  7.2 86.8 %copy-start = (bf16[32,128,128]{2,1,0:T(8,128)(2,1)S(1)}, bf16[32,128,128]{2,1,0:T(8,128)(2,1)}, u32[]{:S(2)}) copy-start(bf16[32,128,128]{2,1,0:T(8,128)(2,1)} %param.20) | copy-start | bytes 3145732
  7.2 73.5 %all-gather.4.cloned.1.call-start = ((), (), s32[]{:S(2)}) async-start(), calls=%async_computation.8 | async-start | bytes 1638400 | tf_op jit(solution)/shard_map/all_gather | solution.py:164
  7.2 1.0 copy-start.4
  8.3 0.8 copy-start.5
  9.0 0.8 copy-start.6
  10.5 0.7 copy-start.7
  11.2 0.7 copy-start.8
  11.9 0.7 copy-start.9
  13.1 44.2 %copy-start.10 = (bf16[2,1024,192]{1,2,0:T(8,128)(2,1)S(1)}, bf16[2,1024,192]{1,2,0:T(8,128)(2,1)}, u32[]{:S(2)}) copy-start(bf16[2,1024,192]{1,2,0:T(8,128)(2,1)} %param.26) | copy-start | bytes 2359300
  44.3 12.9 %all-to-all-start.1 = ((bf16[4,64,1152]{2,1,0:T(8,128)(2,1)}), bf16[4,64,1152]{2,1,0:T(8,128)(2,1)S(1)}, u32[]{:S(2)}, u32[]{:S(2)}) async-start(bf16[4,64,1152]{2,1,0:T(8,128)(2,1)} %shard_map.168), calls=%async_computation.1 | async-start | bytes 1179648 | tf_op jit(solution)/shard_map/all_to_all | solution.py:19
  48.8 79.9 %all-gather.6.cloned.1.call-start = ((), (), s32[]{:S(2)}) async-start(), calls=%async_computation.9 | async-start | bytes 1310720 | tf_op jit(solution)/shard_map/all_gather | solution.py:164
  58.7 12.6 %all-to-all-start.2 = ((f32[32,8,192]{2,1,0:T(8,128)}), f32[32,8,192]{2,1,0:T(8,128)S(1)}, u32[]{:S(2)}, u32[]{:S(2)}) async-start(f32[32,8,192]{2,1,0:T(8,128)} %bitcast.4), calls=%async_computation.2 | async-start | bytes 524288 | tf_op jit(solution)/shard_map/all_to_all | solution.py:19
  71.9 8.7 %all-to-all-start.3 = ((bf16[8,8,192]{2,1,0:T(8,128)(2,1)}), bf16[8,8,192]{2,1,0:T(8,128)(2,1)S(1)}, u32[]{:S(2)}, u32[]{:S(2)}) async-start(bf16[8,8,192]{2,1,0:T(8,128)(2,1)} %broadcast_in_dim.25), calls=%async_computation.3 | async-start | bytes 65536 | tf_op jit(solution)/shard_map/all_to_all | solution.py:19
  77.3 16.6 %copy-start.13 = (s32[4,8]{1,0:T(4,128)S(1)}, s32[4,8]{1,0:T(4,128)}, u32[]{:S(2)}) copy-start(s32[4,8]{1,0:T(4,128)} %param.22) | copy-start | bytes 388
  80.6 1.3 copy-start.1
  83.6 25.0 %all-to-all-start.4 = ((bf16[16,4,1280]{2,1,0:T(4,128)(2,1)}), bf16[16,4,1280]{2,1,0:T(4,128)(2,1)S(1)}, u32[]{:S(2)}, u32[]{:S(2)}) async-start(bf16[16,4,1280]{2,1,0:T(4,128)(2,1)} %reshape.167), calls=%async_computation.4 | async-start | bytes 327680 | tf_op jit(solution)/shard_map/all_to_all | solution.py:19
  93.1 44.0 %all-gather.8.cloned.1.call-start = ((), (), s32[]{:S(2)}) async-start(), calls=%async_computation.10 | async-start | bytes 1310720 | tf_op jit(solution)/shard_map/all_gather | solution.py:164
  94.7 2.0 %copy-start.16 = (s32[4]{0:T(128)S(1)}, s32[4]{0:T(128)}, u32[]{:S(2)}) copy-start(s32[4]{0:T(128)} %param.23) | copy-start | bytes 52
  94.8 14.0 %copy-start.12 = (bf16[4,1024]{1,0:T(4,128)(2,1)S(1)}, bf16[4,1024]{1,0:T(4,128)(2,1)}, u32[]{:S(2)}) copy-start(bf16[4,1024]{1,0:T(4,128)(2,1)} %param.17) | copy-start | bytes 24580
  94.8 14.0 %copy-start.14 = (bf16[4,128]{1,0:T(4,128)(2,1)S(1)}, bf16[4,128]{1,0:T(4,128)(2,1)}, u32[]{:S(2)}) copy-start(bf16[4,128]{1,0:T(4,128)(2,1)} %param.19) | copy-start | bytes 3076
  94.8 14.0 %copy-start.15 = (bf16[4,128]{1,0:T(4,128)(2,1)S(1)}, bf16[4,128]{1,0:T(4,128)(2,1)}, u32[]{:S(2)}) copy-start(bf16[4,128]{1,0:T(4,128)(2,1)} %param.18) | copy-start | bytes 3076
  110.0 33.3 %copy-start.11 = (bf16[1,4,8,128]{3,1,2,0:T(4,128)(2,1)}, bf16[1,4,8,128]{3,1,2,0:T(4,128)(2,1)S(1)}, u32[]{:S(2)}) copy-start(bf16[1,4,8,128]{3,1,2,0:T(4,128)(2,1)S(1)} %copy.36) | copy-start | bytes 24580
  128.6 1.2 copy-start.2
  131.7 9.5 %all-to-all-start.6 = ((f32[8,32,128]{2,1,0:T(8,128)}), f32[8,32,128]{2,1,0:T(8,128)S(1)}, u32[]{:S(2)}, u32[]{:S(2)}) async-start(f32[8,32,128]{2,1,0:T(8,128)} %shard_map.171), calls=%async_computation.6 | async-start | bytes 262144 | tf_op jit(solution)/shard_map/all_to_all | solution.py:19
  141.1 1.2 copy-start.3
Sparse Core Ops, SparseCore 0:
  10.7 37.0 all-gather.3
  51.7 36.0 all-gather.5
  96.1 30.5 all-gather.7

commit v6 on v4

--- a/solution.py
+++ b/solution.py
@@ -6,13 +6,8 @@
 from jax.experimental.pallas import tpu as pltpu
 from jax.sharding import Mesh, PartitionSpec as P
 
-HEAD_SIZE = 128
 adapter_scale = 2.0
 Y, Z, T = "y", "z", "tensor"
-
-
-def rounded_values(values):
-    return lax.optimization_barrier(values.astype(jnp.bfloat16)).astype(jnp.float32)
 
 
 def exchange(blocks, axis):
@@ -33,24 +28,35 @@
 SMEM = pl.BlockSpec(memory_space=pltpu.SMEM)
 
 
+ANY = pl.BlockSpec(memory_space=pl.ANY)
+
+
 def call(kernel, shape, dtype, *operands, scalars=1, after=()):
     count = len(operands)
 
-    def body(*refs):
+    def run(*refs):
         kernel(*refs[:count], *refs[count + len(after) :])
 
     return pl.pallas_call(
-        body,
+        run,
         out_shape=jax.ShapeDtypeStruct(shape, dtype),
-        in_specs=[SMEM] * scalars
-        + [VMEM] * (count - scalars)
-        + [pl.BlockSpec(memory_space=pl.ANY)] * len(after),
+        in_specs=[SMEM] * scalars + [VMEM] * (count - scalars) + [ANY] * len(after),
         out_specs=VMEM,
         compiler_params=pltpu.CompilerParams(vmem_limit_bytes=32 * 2**20),
     )(*operands, *after)
 
 
-def first_blocks(id_ref, slot_ref, hidden_ref, out_ref):
+def first_blocks(id_hbm, slot_hbm, hidden_hbm, out_ref, id_ref, slot_ref, hidden_ref, sems):
+    copies = [
+        pltpu.make_async_copy(source, target, sems.at[i])
+        for i, (source, target) in enumerate(
+            ((id_hbm, id_ref), (slot_hbm, slot_ref), (hidden_hbm, hidden_ref))
+        )
+    ]
+    for copy in copies:
+        copy.start()
+    for copy in copies:
+        copy.wait()
     rows, width = hidden_ref.shape
     tags = [
         jnp.full((1, 128), slot_ref[id_ref[r]].astype(jnp.float32), jnp.float32) for r in range(rows)
@@ -62,6 +68,48 @@
         out_ref[z] = block
 
 
+def attend(
+    table_ref, length_ref, terms_ref, q_ref, k_ref, v_ref, keys_ref, values_ref, out_ref, block_ref
+):
+    rows, width_q = q_ref.shape
+    size = k_ref.shape[1]
+    heads = width_q // size
+    delta = summed(terms_ref[...])
+    parts = (
+        q_ref[...].astype(jnp.float32) + delta[:, :width_q],
+        k_ref[...].astype(jnp.float32) + delta[:, width_q : width_q + size],
+        v_ref[...].astype(jnp.float32) + delta[:, width_q + size :],
+    )
+    query, key, value = [part.astype(jnp.bfloat16).astype(jnp.float32) for part in parts]
+    inverse = 1.0 / size**0.5
+    done = []
+    for r in range(rows):
+        pages = [table_ref[r, i] for i in range(table_ref.shape[1])]
+        q = jnp.concatenate(
+            [query[r : r + 1, h * size : (h + 1) * size] for h in range(heads)], axis=0
+        )
+        keys = jnp.concatenate([keys_ref[page] for page in pages], axis=0)
+        scores = lax.dot_general(
+            q.astype(jnp.bfloat16), keys, NT, preferred_element_type=jnp.float32
+        )
+        live = lax.broadcasted_iota(jnp.int32, scores.shape, 1) < length_ref[r]
+        scores = jnp.where(live, scores * inverse, jnp.float32(-1e30))
+        own = jnp.sum(q * key[r : r + 1], axis=1, keepdims=True) * inverse
+        top = jnp.maximum(jnp.max(scores, axis=1, keepdims=True), own)
+        weights = jnp.where(live, jnp.exp(scores - top), 0.0)
+        own_weight = jnp.exp(own - top)
+        total = jnp.sum(weights, axis=1, keepdims=True) + own_weight
+        values = jnp.concatenate([values_ref[page] for page in pages], axis=0)
+        mixed = jnp.dot(weights.astype(jnp.bfloat16), values, preferred_element_type=jnp.float32)
+        own_rounded = own_weight.astype(jnp.bfloat16).astype(jnp.float32)
+        mixed = (mixed + own_rounded * value[r : r + 1]) / total
+        done.append(jnp.concatenate([mixed[h : h + 1] for h in range(heads)], axis=1))
+    attention = jnp.concatenate(done, axis=0).astype(jnp.bfloat16)
+    out_ref[...] = attention
+    for z in range(block_ref.shape[0]):
+        block_ref[z] = attention
+
+
 def second_blocks(from_z_ref, out_ref):
     rows = from_z_ref[...].reshape(out_ref.shape[1:])
     for y in range(out_ref.shape[0]):
@@ -77,6 +125,17 @@
 
 def picked(slots_ref, tags, values, number):
     return jnp.where(tags == slots_ref[number].astype(jnp.float32), values, jnp.zeros_like(values))
+
+
+def down_first(slots_ref, rows_ref, weight_ref, out_ref):
+    width = weight_ref.shape[2]
+    rows, tags = rows_ref[:, :width], rows_ref[:, width : width + 1].astype(jnp.float32)
+    total = None
+    for j in range(weight_ref.shape[0]):
+        product = lax.dot_general(rows, weight_ref[j], NT, preferred_element_type=jnp.float32)
+        mine = picked(slots_ref, tags, product, j)
+        total = mine if total is None else total + mine
+    out_ref[...] = total
 
 
 def tags_of(rows_ref, at, width):
@@ -192,35 +251,38 @@
         ]
 
     up_pages = packed(query_up_weight, key_up_weight, value_up_weight)
-    z_blocks = call(
+    z_blocks = pl.pallas_call(
         first_blocks,
-        (z_size, local_rows, local_width + 128),
-        jnp.bfloat16,
-        adapter_id,
-        adapter_slot,
-        hidden,
-        scalars=2,
-    )
+        out_shape=jax.ShapeDtypeStruct((z_size, local_rows, local_width + 128), jnp.bfloat16),
+        in_specs=[ANY] * 3,
+        out_specs=VMEM,
+        scratch_shapes=[
+            pltpu.SMEM(adapter_id.shape, jnp.int32),
+            pltpu.SMEM(adapter_slot.shape, jnp.int32),
+            pltpu.VMEM(hidden.shape, jnp.bfloat16),
+            pltpu.SemaphoreType.DMA((3,)),
+        ],
+    )(adapter_id, adapter_slot, hidden)
     y_blocks = call(
         second_blocks,
         (y_size, z_size * local_rows, local_width + 128),
         jnp.bfloat16,
         exchange(z_blocks, Z),
         scalars=0,
-        after=up_pages[1:],
+        after=up_pages[1:2],
     )
     z_rows = y_blocks[0]
     all_rows = exchange(y_blocks, Y).reshape(y_size * z_size * local_rows, -1)
 
-    all_slots = all_rows[:, local_width].astype(jnp.int32)
-    owned_mask = (all_slots[:, None] == column_slots[None, :local_count]).astype(jnp.float32)
-    product = jnp.einsum(
-        "nd,jdr->njr",
-        all_rows[:, :local_width],
-        query_key_value_down,
-        preferred_element_type=jnp.float32,
-    )
-    part = jnp.sum(product * owned_mask[:, :, None], axis=1)
+    part = call(
+        down_first,
+        (y_size * z_size * local_rows, query_key_value_down.shape[2]),
+        jnp.float32,
+        column_slots,
+        all_rows,
+        jnp.swapaxes(query_key_value_down, 1, 2),
+        after=up_pages[2:],
+    )
     share = z_size * local_rows // t_size
     shares = exchange(part.reshape(y_size * t_size, share, -1), (Y, T))
     ranks = spread(summed(shares).astype(jnp.bfloat16), T).reshape(z_size * local_rows, -1)
@@ -236,54 +298,27 @@
     out_pages = packed(
         jnp.swapaxes(output_down_weight, 1, 2), output_up_weight, after=(shares,)
     )
-    adapter_delta = to_requests(delta)
-    width_q = q_base.shape[1]
-    width_k = base_key.shape[1]
-    query_vector = (q_base.astype(jnp.float32) + adapter_delta[:, 0:width_q]).astype(jnp.bfloat16)
-    new_token_key = (
-        base_key.astype(jnp.float32) + adapter_delta[:, width_q : width_q + width_k]
-    ).astype(jnp.bfloat16)
-    new_token_value = (
-        base_value.astype(jnp.float32) + adapter_delta[:, width_q + width_k : width_q + 2 * width_k]
-    ).astype(jnp.bfloat16)
-    kv_local = width_k // HEAD_SIZE
-    head_group = width_q // width_k
-    gathered_keys = paged_key_cache[page_table].reshape(local_rows, -1, kv_local, HEAD_SIZE)
-    gathered_values = paged_value_cache[page_table].reshape(local_rows, -1, kv_local, HEAD_SIZE)
-    query_heads = query_vector.reshape(local_rows, kv_local, head_group, HEAD_SIZE)
-    inverse = 1.0 / HEAD_SIZE**0.5
-    scores = (
-        jnp.einsum(
-            "bkgd,btkd->bkgt", query_heads, gathered_keys, preferred_element_type=jnp.float32
-        )
-        * inverse
-    )
-    own_score = (
-        jnp.einsum(
-            "txvc,txc->txv",
-            query_heads,
-            new_token_key.reshape(local_rows, kv_local, HEAD_SIZE),
-            preferred_element_type=jnp.float32,
-        )
-        * inverse
-    )
-    positions = jnp.arange(gathered_keys.shape[1], dtype=jnp.int32)
-    live = (positions[None, :] < context_len[:, None])[:, None, None, :]
-    scores = jnp.where(live, scores, jnp.float32(-1e30))
-    top = jnp.maximum(jnp.max(scores, axis=-1), own_score)
-    weights = jnp.where(live, jnp.exp(scores - top[..., None]), jnp.float32(0.0))
-    own_weight = jnp.exp(own_score - top)
-    total = jnp.sum(weights, axis=-1) + own_weight
-    mixed = jnp.einsum(
-        "bkgt,btkd->bkgd",
-        weights.astype(jnp.bfloat16),
-        gathered_values,
-        preferred_element_type=jnp.float32,
-    )
-    fresh_wide = new_token_value.reshape(local_rows, kv_local, 1, HEAD_SIZE).astype(jnp.float32)
-    mixed = mixed + rounded_values(own_weight)[..., None] * fresh_wide
-    attention = (mixed / total[..., None]).reshape(local_rows, width_q).astype(jnp.bfloat16)
-    out_rows = spread(attention, Z).reshape(z_size * local_rows, -1)
+    terms = exchange(delta.reshape(z_size, local_rows, cuts[3]), Z)
+    attention, out_blocks = pl.pallas_call(
+        attend,
+        out_shape=[
+            jax.ShapeDtypeStruct(q_base.shape, jnp.bfloat16),
+            jax.ShapeDtypeStruct((z_size,) + q_base.shape, jnp.bfloat16),
+        ],
+        in_specs=[SMEM] * 2 + [VMEM] * 6,
+        out_specs=[VMEM] * 2,
+        compiler_params=pltpu.CompilerParams(vmem_limit_bytes=32 * 2**20),
+    )(
+        page_table,
+        context_len,
+        terms,
+        q_base,
+        base_key,
+        base_value,
+        paged_key_cache,
+        paged_value_cache,
+    )
+    out_rows = exchange(out_blocks, Z).reshape(z_size * local_rows, -1)
     sides = call(
         make_down_second(0),
         (t_size, z_size * local_rows // 2, 2 * rank),

time: 170 us -> 169 us (level)
  blocking collectives: 50.8 us -> 63.8 us
  starting transfers between devices: 64.3 us -> 55 us
  Pallas kernels: 5.11 us -> 9.24 us
  matrix products: 3.7 us -> 0 us
  waiting for transfers between devices: 30.5 us -> 27.3 us
  local copies, waits for them, and re-layouts: 11.4 us -> 9.55 us
    all_to_all x3 -> x4, blocking collectives: 50.8 us -> 63.8 us  [exchange(): return lax.all_to_all(blocks, axis, 0, 0)]
    all_to_all x5 -> x4, waiting for transfers between devices: 20.2 us -> 10.6 us  [exchange(): return lax.all_to_all(blocks, axis, 0, 0)]
    all_to_all x5 -> x4, starting transfers between devices: 43.3 us -> 35.4 us  [exchange(): return lax.all_to_all(blocks, axis, 0, 0)]
    ppermute x6, waiting for transfers between devices: 10.3 us -> 16.7 us  [packed(): lax.ppermute(mine, Y, [(i, (i + k) % y_size) for i in range(y_size)])]
    gather x2 -> x0, local copies, waits for them, and re-layouts: 4.61 us -> none  [the longest x1 2.94 us: body(): paged_value_cache[page_table].reshape(local_rows, -1, kv_local, HEAD_SIZE)]
    pallas_call x7 -> x9, Pallas kernels: 5.11 us -> 9.24 us  [the longest x7 4.88 us: call(): pl.pallas_call(run, out_shape=jax.ShapeDtypeStruct(shape, dtype), in_spec...]
    unnamed x37 -> x30, local copies, waits for them, and re-layouts: 3.37 us -> 7.13 us
    dot_general x3 -> x0, matrix products: 2.17 us -> none  [the longest x1 1.74 us: body(): jnp.einsum('bkgd,btkd->bkgt', query_heads, gathered_keys, preferred_eleme...]
  transfers between devices with their start and end apart: 11 -> 10, of which waited for: 7 -> 5; matrix products, arithmetic and copies ran while one was open for 5% -> 1% of each run, Pallas kernels for 0% -> 2%
where the time goes in v6:
time: 169 us; the launch traced here: 167 us
  blocking collectives  63.8 us (38%)
  starting transfers between devices  55 us (33%)
  waiting for transfers between devices  27.3 us (16%)
  local copies, waits for them, and re-layouts  9.55 us (6%)
  Pallas kernels  9.24 us (5%)
    all_to_all x4, blocking collectives, exchange(): return lax.all_to_all(blocks, axis, 0, 0)  63.8 us
    all_to_all x4, starting transfers between devices, exchange(): return lax.all_to_all(blocks, axis, 0, 0)  35.4 us
    ppermute x6, starting transfers between devices, packed(): lax.ppermute(mine, Y, [(i, (i + k) % y_size) for i in range(y_size)])  19.6 us
    ppermute x6, waiting for transfers between devices, packed(): lax.ppermute(mine, Y, [(i, (i + k) % y_size) for i in range(y_size)])  16.7 us
    all_to_all x4, waiting for transfers between devices, exchange(): return lax.all_to_all(blocks, axis, 0, 0)  10.6 us
    unnamed x30, local copies, waits for them, and re-layouts  7.13 us
    pallas_call x7, Pallas kernels, call(): pl.pallas_call(run, out_shape=jax.ShapeDtypeStruct(shape, dtype), in_spec...  4.88 us
  transfers between devices with their start and end apart: 10, of which 5 were waited for; matrix products, arithmetic and copies ran while one was open for 1% of the time, Pallas kernels for 2%

profile of v6, /device:TPU:6, one launch (start us, length us, event | category | flops | bytes accessed | tf_op | source)
XLA Modules:
  0.0 166.5 jit_solution(18074008774599255362)
XLA Ops:
  0.6 1.5 shard_map.167
  2.2 15.2 %all-to-all-start = ((bf16[16,4,1152]{2,1,0:T(4,128)(2,1)}), bf16[16,4,1152]{2,1,0:T(4,128)(2,1)S(1)}, u32[]{:S(2)}, u32[]{:S(2)}) async-start(bf16[16,4,1152]{2,1,0:T(4,128)(2,1)} %shard_map.167), calls=%async_computation | async-start | bytes 294912 | tf_op jit(solution)/shard_map/all_to_all | solution.py:14
  17.5 3.5 %collective-permute-start = (bf16[2,64,1280]{2,1,0:T(8,128)(2,1)S(1)}, bf16[2,64,1280]{2,1,0:T(8,128)(2,1)S(1)}, u32[]{:S(2)}, u32[]{:S(2)}) collective-permute-start(bf16[2,64,1280]{2,1,0:T(8,128)(2,1)S(1)} %shard_map.168.refs_3_), channel_id=1, source_target_pairs={{0,128},{128,256},{256,384},{384,0},{1,129},{129,257},{257,385},{3... | collective-permute-start | bytes 983048 | tf_op jit(solution)/shard_map/ppermute | solution.py:249
  20.9 8.9 %collective-permute-done.refs_1_.refs_4_ = bf16[2,64,1280]{2,1,0:T(8,128)(2,1)S(1)} collective-permute-done((bf16[2,64,1280]{2,1,0:T(8,128)(2,1)S(1)}, bf16[2,64,1280]{2,1,0:T(8,128)(2,1)S(1)}, u32[]{:S(2)}, u32[]{:S(2)}) %collective-permute-start) | collective-permute-done | bytes 327712 | tf_op jit(solution)/shard_map/ppermute | solution.py:249
  29.8 2.7 %all-to-all-done.refs_0_ = bf16[16,4,1152]{2,1,0:T(4,128)(2,1)S(1)} async-done(((bf16[16,4,1152]{2,1,0:T(4,128)(2,1)}), bf16[16,4,1152]{2,1,0:T(4,128)(2,1)S(1)}, u32[]{:S(2)}, u32[]{:S(2)}) %all-to-all-start) | async-done | bytes 147488 | tf_op jit(solution)/shard_map/all_to_all | solution.py:14
  32.5 0.9 shard_map.169
  33.4 4.6 %all-to-all-start.1 = ((bf16[4,64,1152]{2,1,0:T(8,128)(2,1)}), bf16[4,64,1152]{2,1,0:T(8,128)(2,1)S(1)}, u32[]{:S(2)}, u32[]{:S(2)}) async-start(bf16[4,64,1152]{2,1,0:T(8,128)(2,1)} %shard_map.169), calls=%async_computation.1 | async-start | bytes 1179648 | tf_op jit(solution)/shard_map/all_to_all | solution.py:14
  38.0 5.1 %collective-permute-start.2 = (bf16[2,64,1280]{2,1,0:T(8,128)(2,1)S(1)}, bf16[2,64,1280]{2,1,0:T(8,128)(2,1)S(1)}, u32[]{:S(2)}, u32[]{:S(2)}) collective-permute-start(bf16[2,64,1280]{2,1,0:T(8,128)(2,1)S(1)} %shard_map.168.refs_3_), channel_id=1, source_target_pairs={{0,384},{128,0},{256,128},{384,256},{1,385},{129,1},{257,129},{385... | collective-permute-start | bytes 983048 | tf_op jit(solution)/shard_map/ppermute | solution.py:249
  43.1 2.8 %collective-permute-start.1 = (bf16[2,64,1280]{2,1,0:T(8,128)(2,1)S(1)}, bf16[2,64,1280]{2,1,0:T(8,128)(2,1)S(1)}, u32[]{:S(2)}, u32[]{:S(2)}) collective-permute-start(bf16[2,64,1280]{2,1,0:T(8,128)(2,1)S(1)} %shard_map.168.refs_3_), channel_id=1, source_target_pairs={{0,256},{128,384},{256,0},{384,128},{1,257},{129,385},{257,1},{385... | collective-permute-start | bytes 983048 | tf_op jit(solution)/shard_map/ppermute | solution.py:249
  46.1 7.9 %collective-permute-done.2.refs_4_.refs_6_ = bf16[2,64,1280]{2,1,0:T(8,128)(2,1)S(1)} collective-permute-done((bf16[2,64,1280]{2,1,0:T(8,128)(2,1)S(1)}, bf16[2,64,1280]{2,1,0:T(8,128)(2,1)S(1)}, u32[]{:S(2)}, u32[]{:S(2)}) %collective-permute-start.2) | collective-permute-done | bytes 327712 | tf_op jit(solution)/shard_map/ppermute | solution.py:249
  54.0 1.0 shard_map.170
  55.0 17.4 %all_to_all.40.refs_2_ = f32[32,8,192]{2,1,0:T(8,128)S(1)} all-to-all(f32[32,8,192]{2,1,0:T(8,128)S(1)} %bitcast.8), channel_id=1, replica_groups=mesh['y'=4,'z'=16,'tensor'=8] {'y','tensor'}, dimensions={0} | all-to-all | bytes 393216 | tf_op jit(solution)/shard_map/all_to_all | solution.py:14
  73.0 5.4 %all-to-all-start.3 = ((bf16[8,8,192]{2,1,0:T(8,128)(2,1)}), bf16[8,8,192]{2,1,0:T(8,128)(2,1)S(1)}, u32[]{:S(2)}, u32[]{:S(2)}) async-start(bf16[8,8,192]{2,1,0:T(8,128)(2,1)} %broadcast_in_dim.2), calls=%async_computation.3 | async-start | bytes 65536 | tf_op jit(solution)/shard_map/all_to_all | solution.py:14
  78.4 0.9 slice_bitcast_fusion.refs_2_
  79.3 2.4 %all-to-all-done.3 = bf16[8,8,192]{2,1,0:T(8,128)(2,1)S(1)} async-done(((bf16[8,8,192]{2,1,0:T(8,128)(2,1)}), bf16[8,8,192]{2,1,0:T(8,128)(2,1)S(1)}, u32[]{:S(2)}, u32[]{:S(2)}) %all-to-all-start.3) | async-done | bytes 24608 | tf_op jit(solution)/shard_map/all_to_all | solution.py:14
  81.7 0.9 shard_map.171
  82.7 0.7 reshape.60
  83.4 10.2 %all-to-all-start.4 = ((bf16[16,4,1280]{2,1,0:T(4,128)(2,1)}), bf16[16,4,1280]{2,1,0:T(4,128)(2,1)}, u32[]{:S(2)}, u32[]{:S(2)}) async-start(bf16[16,4,1280]{2,1,0:T(4,128)(2,1)} %reshape.60), calls=%async_computation.4 | async-start | bytes 327680 | tf_op jit(solution)/shard_map/all_to_all | solution.py:14
  93.6 0.9 copy-done.3
  94.6 0.9 copy-done.4
  95.6 2.9 %collective-permute-start.5 = (bf16[2,64,2048]{2,1,0:T(8,128)(2,1)S(1)}, bf16[2,64,2048]{2,1,0:T(8,128)(2,1)S(1)}, u32[]{:S(2)}, u32[]{:S(2)}) collective-permute-start(bf16[2,64,2048]{2,1,0:T(8,128)(2,1)S(1)} %shard_map.173.refs_3_), channel_id=1, source_target_pairs={{0,384},{128,0},{256,128},{384,256},{1,385},{129,1},{257,129},{385... | collective-permute-start | bytes 1572872 | tf_op jit(solution)/shard_map/ppermute | solution.py:249
  98.4 3.4 %collective-permute-start.4 = (bf16[2,64,2048]{2,1,0:T(8,128)(2,1)S(1)}, bf16[2,64,2048]{2,1,0:T(8,128)(2,1)S(1)}, u32[]{:S(2)}, u32[]{:S(2)}) collective-permute-start(bf16[2,64,2048]{2,1,0:T(8,128)(2,1)S(1)} %shard_map.173.refs_3_), channel_id=1, source_target_pairs={{0,256},{128,384},{256,0},{384,128},{1,257},{129,385},{257,1},{385... | collective-permute-start | bytes 1572872 | tf_op jit(solution)/shard_map/ppermute | solution.py:249
  101.8 2.0 %collective-permute-start.3 = (bf16[2,64,2048]{2,1,0:T(8,128)(2,1)S(1)}, bf16[2,64,2048]{2,1,0:T(8,128)(2,1)S(1)}, u32[]{:S(2)}, u32[]{:S(2)}) collective-permute-start(bf16[2,64,2048]{2,1,0:T(8,128)(2,1)S(1)} %shard_map.173.refs_3_), channel_id=1, source_target_pairs={{0,128},{128,256},{256,384},{384,0},{1,129},{129,257},{257,385},{3... | collective-permute-start | bytes 1572872 | tf_op jit(solution)/shard_map/ppermute | solution.py:249
  103.8 5.4 %all-to-all-done.4.terms_ref = bf16[16,4,1280]{2,1,0:T(4,128)(2,1)} async-done(((bf16[16,4,1280]{2,1,0:T(4,128)(2,1)}), bf16[16,4,1280]{2,1,0:T(4,128)(2,1)}, u32[]{:S(2)}, u32[]{:S(2)}) %all-to-all-start.4) | async-done | bytes 163872 | tf_op jit(solution)/shard_map/all_to_all | solution.py:14
  109.2 1.2 copy-done.1
  110.5 0.7 copy-done.10
  113.9 2.9 %shard_map.172 = (bf16[4,1024]{1,0:T(4,128)(2,1)}, bf16[16,4,1024]{2,1,0:T(4,128)(2,1)S(1)}) custom-call(s32[4,8]{1,0:T(4,128)S(1)} %copy-done.11, s32[4]{0:T(128)S(1)} %copy-done.14, bf16[16,4,1280]{2,1,0:T(4,128)(2,1)} %all-to-all-done.4.terms_ref, bf16[4,1024]{1,0:T(4,128)(2,1)S(1)} %copy-done.10, bf16[4,128]{1,0:T(4,128)(2,1)S(1)} %copy-done.12, ...), custom_call_target="tpu_custom_call" | custom-call | tf_op jit(solution)/shard_map/pallas_call | solution.py:302
  116.7 20.3 %all_to_all.41 = bf16[16,4,1024]{2,1,0:T(4,128)(2,1)S(1)} all-to-all(bf16[16,4,1024]{2,1,0:T(4,128)(2,1)S(1)} %get-tuple-element.5), channel_id=1, replica_groups=mesh['y'=4,'z'=16,'tensor'=8] {'z'}, dimensions={0} | all-to-all | bytes 262144 | tf_op jit(solution)/shard_map/all_to_all | solution.py:14
  137.7 1.0 shard_map.174
  138.7 8.5 %all_to_all.42.refs_1_ = f32[8,32,128]{2,1,0:T(8,128)S(1)} all-to-all(f32[8,32,128]{2,1,0:T(8,128)S(1)} %shard_map.174), channel_id=1, replica_groups=mesh['y'=4,'z'=16,'tensor'=8] {'tensor'}, dimensions={0} | all-to-all | bytes 262144 | tf_op jit(solution)/shard_map/all_to_all | solution.py:14
  147.2 1.0 shard_map.175
  148.3 17.6 %all_to_all.43 = bf16[16,4,1024]{2,1,0:T(4,128)(2,1)S(1)} all-to-all(bf16[16,4,1024]{2,1,0:T(4,128)(2,1)S(1)} %reshape.62), channel_id=1, replica_groups=mesh['y'=4,'z'=16,'tensor'=8] {'z'}, dimensions={0} | all-to-all | bytes 262144 | tf_op jit(solution)/shard_map/all_to_all | solution.py:14
  (41 shorter events, 5.0 us)
Async XLA Ops:
  0.6 16.8 %copy-start.5 = (bf16[2,64,1024]{2,1,0:T(8,128)(2,1)S(1)}, bf16[2,64,1024]{2,1,0:T(8,128)(2,1)}, u32[]{:S(2)}) copy-start(bf16[2,64,1024]{2,1,0:T(8,128)(2,1)} %refs_0_.1) | copy-start | bytes 786436
  2.1 15.3 %copy-start.6 = (bf16[2,64,128]{2,1,0:T(8,128)(2,1)S(1)}, bf16[2,64,128]{2,1,0:T(8,128)(2,1)}, u32[]{:S(2)}) copy-start(bf16[2,64,128]{2,1,0:T(8,128)(2,1)} %refs_1_.2) | copy-start | bytes 98308
  2.2 15.2 %copy-start.7 = (bf16[2,64,128]{2,1,0:T(8,128)(2,1)S(1)}, bf16[2,64,128]{2,1,0:T(8,128)(2,1)}, u32[]{:S(2)}) copy-start(bf16[2,64,128]{2,1,0:T(8,128)(2,1)} %refs_2_.1) | copy-start | bytes 98308
  2.2 30.3 %all-to-all-start = ((bf16[16,4,1152]{2,1,0:T(4,128)(2,1)}), bf16[16,4,1152]{2,1,0:T(4,128)(2,1)S(1)}, u32[]{:S(2)}, u32[]{:S(2)}) async-start(bf16[16,4,1152]{2,1,0:T(4,128)(2,1)} %shard_map.167), calls=%async_computation | async-start | bytes 294912 | tf_op jit(solution)/shard_map/all_to_all | solution.py:14
  17.5 12.3 %collective-permute-start = (bf16[2,64,1280]{2,1,0:T(8,128)(2,1)S(1)}, bf16[2,64,1280]{2,1,0:T(8,128)(2,1)S(1)}, u32[]{:S(2)}, u32[]{:S(2)}) collective-permute-start(bf16[2,64,1280]{2,1,0:T(8,128)(2,1)S(1)} %shard_map.168.refs_3_), channel_id=1, source_target_pairs={{0,128},{128,256},{256,384},{384,0},{1,129},{129,257},{257,385},{3... | collective-permute-start | bytes 983048 | tf_op jit(solution)/shard_map/ppermute | solution.py:249
  33.4 20.6 %copy-start.2 = (bf16[2,1024,192]{1,2,0:T(8,128)(2,1)S(1)}, bf16[2,1024,192]{1,2,0:T(8,128)(2,1)}, u32[]{:S(2)}) copy-start(bf16[2,1024,192]{1,2,0:T(8,128)(2,1)} %param.26) | copy-start | bytes 2359300
  33.4 20.5 %all-to-all-start.1 = ((bf16[4,64,1152]{2,1,0:T(8,128)(2,1)}), bf16[4,64,1152]{2,1,0:T(8,128)(2,1)S(1)}, u32[]{:S(2)}, u32[]{:S(2)}) async-start(bf16[4,64,1152]{2,1,0:T(8,128)(2,1)} %shard_map.169), calls=%async_computation.1 | async-start | bytes 1179648 | tf_op jit(solution)/shard_map/all_to_all | solution.py:14
  38.0 15.9 %collective-permute-start.2 = (bf16[2,64,1280]{2,1,0:T(8,128)(2,1)S(1)}, bf16[2,64,1280]{2,1,0:T(8,128)(2,1)S(1)}, u32[]{:S(2)}, u32[]{:S(2)}) collective-permute-start(bf16[2,64,1280]{2,1,0:T(8,128)(2,1)S(1)} %shard_map.168.refs_3_), channel_id=1, source_target_pairs={{0,384},{128,0},{256,128},{384,256},{1,385},{129,1},{257,129},{385... | collective-permute-start | bytes 983048 | tf_op jit(solution)/shard_map/ppermute | solution.py:249
  43.1 10.8 %collective-permute-start.1 = (bf16[2,64,1280]{2,1,0:T(8,128)(2,1)S(1)}, bf16[2,64,1280]{2,1,0:T(8,128)(2,1)S(1)}, u32[]{:S(2)}, u32[]{:S(2)}) collective-permute-start(bf16[2,64,1280]{2,1,0:T(8,128)(2,1)S(1)} %shard_map.168.refs_3_), channel_id=1, source_target_pairs={{0,256},{128,384},{256,0},{384,128},{1,257},{129,385},{257,1},{385... | collective-permute-start | bytes 983048 | tf_op jit(solution)/shard_map/ppermute | solution.py:249
  46.1 35.6 %copy-start.8 = (s32[8]{0:T(128)}, s32[8]{0:T(128)S(1)}, u32[]{:S(2)}) copy-start(s32[8]{0:T(128)S(1)} %add.45.refs_0_) | copy-start | bytes 100
  73.0 8.7 %all-to-all-start.3 = ((bf16[8,8,192]{2,1,0:T(8,128)(2,1)}), bf16[8,8,192]{2,1,0:T(8,128)(2,1)S(1)}, u32[]{:S(2)}, u32[]{:S(2)}) async-start(bf16[8,8,192]{2,1,0:T(8,128)(2,1)} %broadcast_in_dim.2), calls=%async_computation.3 | async-start | bytes 65536 | tf_op jit(solution)/shard_map/all_to_all | solution.py:14
  82.7 26.6 %copy-start = (bf16[32,128,128]{2,1,0:T(8,128)(2,1)S(1)}, bf16[32,128,128]{2,1,0:T(8,128)(2,1)}, u32[]{:S(2)}) copy-start(bf16[32,128,128]{2,1,0:T(8,128)(2,1)} %keys_ref.1) | copy-start | bytes 3145732
  83.4 25.8 %all-to-all-start.4 = ((bf16[16,4,1280]{2,1,0:T(4,128)(2,1)}), bf16[16,4,1280]{2,1,0:T(4,128)(2,1)}, u32[]{:S(2)}, u32[]{:S(2)}) async-start(bf16[16,4,1280]{2,1,0:T(4,128)(2,1)} %reshape.60), calls=%async_computation.4 | async-start | bytes 327680 | tf_op jit(solution)/shard_map/all_to_all | solution.py:14
  93.6 1.0 copy-start.3
  94.6 0.9 copy-start.4
  95.6 41.5 %collective-permute-start.5 = (bf16[2,64,2048]{2,1,0:T(8,128)(2,1)S(1)}, bf16[2,64,2048]{2,1,0:T(8,128)(2,1)S(1)}, u32[]{:S(2)}, u32[]{:S(2)}) collective-permute-start(bf16[2,64,2048]{2,1,0:T(8,128)(2,1)S(1)} %shard_map.173.refs_3_), channel_id=1, source_target_pairs={{0,384},{128,0},{256,128},{384,256},{1,385},{129,1},{257,129},{385... | collective-permute-start | bytes 1572872 | tf_op jit(solution)/shard_map/ppermute | solution.py:249
  98.4 38.6 %collective-permute-start.4 = (bf16[2,64,2048]{2,1,0:T(8,128)(2,1)S(1)}, bf16[2,64,2048]{2,1,0:T(8,128)(2,1)S(1)}, u32[]{:S(2)}, u32[]{:S(2)}) collective-permute-start(bf16[2,64,2048]{2,1,0:T(8,128)(2,1)S(1)} %shard_map.173.refs_3_), channel_id=1, source_target_pairs={{0,256},{128,384},{256,0},{384,128},{1,257},{129,385},{257,1},{385... | collective-permute-start | bytes 1572872 | tf_op jit(solution)/shard_map/ppermute | solution.py:249
  101.8 35.3 %collective-permute-start.3 = (bf16[2,64,2048]{2,1,0:T(8,128)(2,1)S(1)}, bf16[2,64,2048]{2,1,0:T(8,128)(2,1)S(1)}, u32[]{:S(2)}, u32[]{:S(2)}) collective-permute-start(bf16[2,64,2048]{2,1,0:T(8,128)(2,1)S(1)} %shard_map.173.refs_3_), channel_id=1, source_target_pairs={{0,128},{128,256},{256,384},{384,0},{1,129},{129,257},{257,385},{3... | collective-permute-start | bytes 1572872 | tf_op jit(solution)/shard_map/ppermute | solution.py:249
  109.2 1.2 copy-start.1
  110.5 0.7 copy-start.10
  111.2 0.7 copy-start.11
  111.8 0.7 copy-start.12
  112.5 0.7 copy-start.13
  113.2 0.7 copy-start.14
  137.0 0.7 copy-start.9

commit v7 on v6

--- a/solution.py
+++ b/solution.py
@@ -46,16 +46,18 @@
     )(*operands, *after)
 
 
-def first_blocks(id_hbm, slot_hbm, hidden_hbm, out_ref, id_ref, slot_ref, hidden_ref, sems):
+def fetch(sources, targets, sems):
     copies = [
         pltpu.make_async_copy(source, target, sems.at[i])
-        for i, (source, target) in enumerate(
-            ((id_hbm, id_ref), (slot_hbm, slot_ref), (hidden_hbm, hidden_ref))
-        )
+        for i, (source, target) in enumerate(zip(sources, targets))
     ]
     for copy in copies:
         copy.start()
-    for copy in copies:
+    return copies
+
+
+def first_blocks(id_hbm, slot_hbm, hidden_hbm, out_ref, id_ref, slot_ref, hidden_ref, sems):
+    for copy in fetch((id_hbm, slot_hbm, hidden_hbm), (id_ref, slot_ref, hidden_ref), sems):
         copy.wait()
     rows, width = hidden_ref.shape
     tags = [
@@ -68,9 +70,11 @@
         out_ref[z] = block
 
 
-def attend(
-    table_ref, length_ref, terms_ref, q_ref, k_ref, v_ref, keys_ref, values_ref, out_ref, block_ref
-):
+def attend(*refs):
+    sources, (out_ref, block_ref), held, sems = refs[:8], refs[8:10], refs[10:18], refs[18]
+    table_ref, length_ref, terms_ref, q_ref, k_ref, v_ref, keys_ref, values_ref = held
+    for copy in fetch(sources, held, sems):
+        copy.wait()
     rows, width_q = q_ref.shape
     size = k_ref.shape[1]
     heads = width_q // size
@@ -156,23 +160,20 @@
     return (adapter_scale * total).astype(jnp.bfloat16)
 
 
-def make_up_first(cuts):
-    def up_first(slots_ref, ranks_ref, rows_ref, *refs):
-        pages, out_ref = refs[:-1], refs[-1]
-        rank = pages[0].shape[1]
-        tags = tags_of(rows_ref, rows_ref.shape[1] - 128, rank)
-        ranks = ranks_ref[...].astype(jnp.float32)
-        for i in range(3):
-            out_ref[:, cuts[i] : cuts[i + 1]] = grown(
-                slots_ref,
-                tags,
-                ranks[:, i * rank : (i + 1) * rank],
-                pages,
-                cuts[i],
-                cuts[i + 1] - cuts[i],
-            )
-
-    return up_first
+def up_first(slots_ref, ranks_ref, rows_ref, q_up, k_up, v_up, out_ref):
+    rank = q_up.shape[1]
+    tags = tags_of(rows_ref, rows_ref.shape[1] - 128, rank)
+    ranks = ranks_ref[...].astype(jnp.float32)
+    at = 0
+    for i, page in enumerate((q_up, k_up, v_up)):
+        width = page.shape[2]
+        mine = ranks[:, i * rank : (i + 1) * rank]
+        out_ref[:, at : at + width] = grown(slots_ref, tags, mine, [page], 0, width)
+        at += width
+
+
+def term_blocks(from_y_ref, out_ref):
+    out_ref[...] = summed(from_y_ref[...]).reshape(out_ref.shape).astype(jnp.bfloat16)
 
 
 def make_down_second(at):
@@ -250,7 +251,6 @@
             for k in range(1, y_size)
         ]
 
-    up_pages = packed(query_up_weight, key_up_weight, value_up_weight)
     z_blocks = pl.pallas_call(
         first_blocks,
         out_shape=jax.ShapeDtypeStruct((z_size, local_rows, local_width + 128), jnp.bfloat16),
@@ -269,7 +269,6 @@
         jnp.bfloat16,
         exchange(z_blocks, Z),
         scalars=0,
-        after=up_pages[1:2],
     )
     z_rows = y_blocks[0]
     all_rows = exchange(y_blocks, Y).reshape(y_size * z_size * local_rows, -1)
@@ -281,32 +280,46 @@
         column_slots,
         all_rows,
         jnp.swapaxes(query_key_value_down, 1, 2),
-        after=up_pages[2:],
-    )
-    share = z_size * local_rows // t_size
-    shares = exchange(part.reshape(y_size * t_size, share, -1), (Y, T))
-    ranks = spread(summed(shares).astype(jnp.bfloat16), T).reshape(z_size * local_rows, -1)
+    )
+    shares = exchange(part.reshape(t_size, -1, part.shape[1]), T)
+    ranks = spread(summed(shares).astype(jnp.bfloat16), T).reshape(part.shape)
     delta = call(
-        make_up_first(cuts),
-        (z_size * local_rows, cuts[3]),
+        up_first,
+        (all_rows.shape[0], cuts[3]),
         jnp.bfloat16,
         column_slots,
         ranks,
-        z_rows,
-        *up_pages,
+        all_rows,
+        query_up_weight,
+        key_up_weight,
+        value_up_weight,
+    )
+    from_y = exchange(delta.reshape(y_size, z_size * local_rows, cuts[3]), Y)
+    terms = exchange(
+        call(term_blocks, (z_size, local_rows, cuts[3]), jnp.bfloat16, from_y, scalars=0), Z
     )
     out_pages = packed(
-        jnp.swapaxes(output_down_weight, 1, 2), output_up_weight, after=(shares,)
-    )
-    terms = exchange(delta.reshape(z_size, local_rows, cuts[3]), Z)
+        jnp.swapaxes(output_down_weight, 1, 2), output_up_weight, after=(from_y,)
+    )
     attention, out_blocks = pl.pallas_call(
         attend,
         out_shape=[
             jax.ShapeDtypeStruct(q_base.shape, jnp.bfloat16),
             jax.ShapeDtypeStruct((z_size,) + q_base.shape, jnp.bfloat16),
         ],
-        in_specs=[SMEM] * 2 + [VMEM] * 6,
+        in_specs=[ANY] * 8,
         out_specs=[VMEM] * 2,
+        scratch_shapes=[
+            pltpu.SMEM(page_table.shape, jnp.int32),
+            pltpu.SMEM(context_len.shape, jnp.int32),
+            pltpu.VMEM(terms.shape, jnp.bfloat16),
+            pltpu.VMEM(q_base.shape, jnp.bfloat16),
+            pltpu.VMEM(base_key.shape, jnp.bfloat16),
+            pltpu.VMEM(base_value.shape, jnp.bfloat16),
+            pltpu.VMEM(paged_key_cache.shape, jnp.bfloat16),
+            pltpu.VMEM(paged_value_cache.shape, jnp.bfloat16),
+            pltpu.SemaphoreType.DMA((8,)),
+        ],
         compiler_params=pltpu.CompilerParams(vmem_limit_bytes=32 * 2**20),
     )(
         page_table,

time: 169 us -> 157 us (0.929)
  starting transfers between devices: 55 us -> 24.6 us
  blocking collectives: 63.8 us -> 89.1 us
  local copies, waits for them, and re-layouts: 9.55 us -> 2.4 us
    all_to_all x4 -> x6, blocking collectives: 63.8 us -> 89.1 us  [exchange(): return lax.all_to_all(blocks, axis, 0, 0)]
    all_to_all x4 -> x3, starting transfers between devices: 35.4 us -> 16.2 us  [exchange(): return lax.all_to_all(blocks, axis, 0, 0)]
    ppermute x6 -> x3, waiting for transfers between devices: 16.7 us -> 0.01 us  [packed(): lax.ppermute(mine, Y, [(i, (i + k) % y_size) for i in range(y_size)])]
    all_to_all x4 -> x3, waiting for transfers between devices: 10.6 us -> 26.7 us  [exchange(): return lax.all_to_all(blocks, axis, 0, 0)]
    ppermute x6 -> x3, starting transfers between devices: 19.6 us -> 8.37 us  [packed(): lax.ppermute(mine, Y, [(i, (i + k) % y_size) for i in range(y_size)])]
    unnamed x30 -> x26, local copies, waits for them, and re-layouts: 7.13 us -> 1.29 us
  transfers between devices with their start and end apart: 10 -> 6, of which waited for: 5 -> 3; matrix products, arithmetic and copies ran while one was open for 1% -> 1% of each run, Pallas kernels for 2% -> 2%
where the time goes in v7:
time: 157 us; the launch traced here: 154 us
  blocking collectives  89.1 us (57%)
  waiting for transfers between devices  26.7 us (17%)
  starting transfers between devices  24.6 us (16%)
  Pallas kernels  9.7 us (6%)
  local copies, waits for them, and re-layouts  2.4 us (2%)
    all_to_all x6, blocking collectives, exchange(): return lax.all_to_all(blocks, axis, 0, 0)  89.1 us
    all_to_all x3, waiting for transfers between devices, exchange(): return lax.all_to_all(blocks, axis, 0, 0)  26.7 us
    all_to_all x3, starting transfers between devices, exchange(): return lax.all_to_all(blocks, axis, 0, 0)  16.2 us
    ppermute x3, starting transfers between devices, packed(): lax.ppermute(mine, Y, [(i, (i + k) % y_size) for i in range(y_size)])  8.37 us
    pallas_call x7, Pallas kernels, call(): pl.pallas_call(run, out_shape=jax.ShapeDtypeStruct(shape, dtype), in_spec...  5.62 us
  transfers between devices with their start and end apart: 6, of which 3 were waited for; matrix products, arithmetic and copies ran while one was open for 1% of the time, Pallas kernels for 2%

profile of v7, /device:TPU:6, one launch (start us, length us, event | category | flops | bytes accessed | tf_op | source)
XLA Modules:
  0.0 154.1 jit_solution(15081674734073449576)
XLA Ops:
  0.6 1.4 shard_map.167
  2.1 30.3 %all_to_all.45.refs_0_ = bf16[16,4,1152]{2,1,0:T(4,128)(2,1)S(1)} all-to-all(bf16[16,4,1152]{2,1,0:T(4,128)(2,1)} %shard_map.167), channel_id=1, replica_groups=mesh['y'=4,'z'=16,'tensor'=8] {'z'}, dimensions={0} | all-to-all | bytes 294912 | tf_op jit(solution)/shard_map/all_to_all | solution.py:14
  32.4 0.9 shard_map.168
  33.3 4.5 %all-to-all-start.1 = ((bf16[4,64,1152]{2,1,0:T(8,128)(2,1)}), bf16[4,64,1152]{2,1,0:T(8,128)(2,1)S(1)}, u32[]{:S(2)}, u32[]{:S(2)}) async-start(bf16[4,64,1152]{2,1,0:T(8,128)(2,1)} %shard_map.168), calls=%async_computation.1 | async-start | bytes 1179648 | tf_op jit(solution)/shard_map/all_to_all | solution.py:14
  37.8 0.1 iota_add_fusion
  37.8 0.1 add.45.refs_0_
  37.9 8.3 %all-to-all-done.1 = bf16[4,64,1152]{2,1,0:T(8,128)(2,1)S(1)} async-done(((bf16[4,64,1152]{2,1,0:T(8,128)(2,1)}), bf16[4,64,1152]{2,1,0:T(8,128)(2,1)S(1)}, u32[]{:S(2)}, u32[]{:S(2)}) %all-to-all-start.1) | async-done | bytes 589856 | tf_op jit(solution)/shard_map/all_to_all | solution.py:14
  46.2 1.0 shard_map.169
  47.2 10.0 %all_to_all.46 = f32[8,32,192]{2,1,0:T(8,128)S(1)} all-to-all(f32[8,32,192]{2,1,0:T(8,128)S(1)} %bitcast.11), channel_id=1, replica_groups=mesh['y'=4,'z'=16,'tensor'=8] {'tensor'}, dimensions={0} | all-to-all | bytes 393216 | tf_op jit(solution)/shard_map/all_to_all | solution.py:14
  57.3 0.0 copy-start.3
  57.3 0.0 copy-start.6
  57.3 8.6 %all_to_all.47 = bf16[8,32,192]{2,1,0:T(8,128)(2,1)S(1)} all-to-all(bf16[8,32,192]{2,1,0:T(8,128)(2,1)S(1)} %broadcast_in_dim.2), channel_id=1, replica_groups=mesh['y'=4,'z'=16,'tensor'=8] {'tensor'}, dimensions={0} | all-to-all | bytes 196608 | tf_op jit(solution)/shard_map/all_to_all | solution.py:14
  66.0 0.9 shard_map.170
  66.9 13.4 %all_to_all.48.refs_0_.refs_2_ = bf16[4,64,1280]{2,1,0:T(8,128)(2,1)S(1)} all-to-all(bf16[4,64,1280]{2,1,0:T(8,128)(2,1)S(1)} %bitcast.10), channel_id=1, replica_groups=mesh['y'=4,'z'=16,'tensor'=8] {'y'}, dimensions={0} | all-to-all | bytes 1310720 | tf_op jit(solution)/shard_map/all_to_all | solution.py:14
  80.3 0.8 shard_map.171
  81.1 5.8 %all-to-all-start.5 = ((bf16[16,4,1280]{2,1,0:T(4,128)(2,1)}), bf16[16,4,1280]{2,1,0:T(4,128)(2,1)S(1)}, u32[]{:S(2)}, u32[]{:S(2)}) async-start(bf16[16,4,1280]{2,1,0:T(4,128)(2,1)} %shard_map.171), calls=%async_computation.5 | async-start | bytes 327680 | tf_op jit(solution)/shard_map/all_to_all | solution.py:14
  86.9 0.0 copy-start.10
  87.0 3.1 %collective-permute-start.2 = (bf16[2,64,2048]{2,1,0:T(8,128)(2,1)S(1)}, bf16[2,64,2048]{2,1,0:T(8,128)(2,1)S(1)}, u32[]{:S(2)}, u32[]{:S(2)}) collective-permute-start(bf16[2,64,2048]{2,1,0:T(8,128)(2,1)S(1)} %shard_map.173.refs_3_), channel_id=1, source_target_pairs={{0,384},{128,0},{256,128},{384,256},{1,385},{129,1},{257,129},{385... | collective-permute-start | bytes 1572872 | tf_op jit(solution)/shard_map/ppermute | solution.py:250
  90.1 3.4 %collective-permute-start.1 = (bf16[2,64,2048]{2,1,0:T(8,128)(2,1)S(1)}, bf16[2,64,2048]{2,1,0:T(8,128)(2,1)S(1)}, u32[]{:S(2)}, u32[]{:S(2)}) collective-permute-start(bf16[2,64,2048]{2,1,0:T(8,128)(2,1)S(1)} %shard_map.173.refs_3_), channel_id=1, source_target_pairs={{0,256},{128,384},{256,0},{384,128},{1,257},{129,385},{257,1},{385... | collective-permute-start | bytes 1572872 | tf_op jit(solution)/shard_map/ppermute | solution.py:250
  93.5 1.9 %collective-permute-start = (bf16[2,64,2048]{2,1,0:T(8,128)(2,1)S(1)}, bf16[2,64,2048]{2,1,0:T(8,128)(2,1)S(1)}, u32[]{:S(2)}, u32[]{:S(2)}) collective-permute-start(bf16[2,64,2048]{2,1,0:T(8,128)(2,1)S(1)} %shard_map.173.refs_3_), channel_id=1, source_target_pairs={{0,128},{128,256},{256,384},{384,0},{1,129},{129,257},{257,385},{3... | collective-permute-start | bytes 1572872 | tf_op jit(solution)/shard_map/ppermute | solution.py:250
  95.4 6.1 %all-to-all-done.5.refs_2_ = bf16[16,4,1280]{2,1,0:T(4,128)(2,1)S(1)} async-done(((bf16[16,4,1280]{2,1,0:T(4,128)(2,1)}), bf16[16,4,1280]{2,1,0:T(4,128)(2,1)S(1)}, u32[]{:S(2)}, u32[]{:S(2)}) %all-to-all-start.5) | async-done | bytes 163872 | tf_op jit(solution)/shard_map/all_to_all | solution.py:14
  101.6 1.2 copy-done.1
  102.8 2.7 %shard_map.172 = (bf16[4,1024]{1,0:T(4,128)(2,1)}, bf16[16,4,1024]{2,1,0:T(4,128)(2,1)}) custom-call(s32[4,8]{1,0:T(4,128)S(1)} %copy-done.9, s32[4]{0:T(128)S(1)} %copy-done.12, bf16[16,4,1280]{2,1,0:T(4,128)(2,1)S(1)} %all-to-all-done.5.refs_2_, bf16[4,1024]{1,0:T(4,128)(2,1)S(1)} %copy-done.8, bf16[4,128]{1,0:T(4,128)(2,1)S(1)} %copy-done.10, ...), custom_call_target="tpu_custom_call" | custom-call | tf_op jit(solution)/shard_map/pallas_call | solution.py:304
  105.4 5.9 %all-to-all-start.6 = ((bf16[16,4,1024]{2,1,0:T(4,128)(2,1)}), bf16[16,4,1024]{2,1,0:T(4,128)(2,1)S(1)}, u32[]{:S(2)}, u32[]{:S(2)}) async-start(bf16[16,4,1024]{2,1,0:T(4,128)(2,1)} %get-tuple-element.5), calls=%async_computation.6 | async-start | bytes 262144 | tf_op jit(solution)/shard_map/all_to_all | solution.py:14
  111.4 0.9 slice_bitcast_fusion.refs_2_
  112.3 12.3 %all-to-all-done.6 = bf16[16,4,1024]{2,1,0:T(4,128)(2,1)S(1)} async-done(((bf16[16,4,1024]{2,1,0:T(4,128)(2,1)}), bf16[16,4,1024]{2,1,0:T(4,128)(2,1)S(1)}, u32[]{:S(2)}, u32[]{:S(2)}) %all-to-all-start.6) | async-done | bytes 131104 | tf_op jit(solution)/shard_map/all_to_all | solution.py:14
  124.7 1.0 shard_map.174
  125.7 8.5 %all_to_all.49.refs_1_ = f32[8,32,128]{2,1,0:T(8,128)S(1)} all-to-all(f32[8,32,128]{2,1,0:T(8,128)S(1)} %shard_map.174), channel_id=1, replica_groups=mesh['y'=4,'z'=16,'tensor'=8] {'tensor'}, dimensions={0} | all-to-all | bytes 262144 | tf_op jit(solution)/shard_map/all_to_all | solution.py:14
  134.2 1.0 shard_map.175
  135.2 0.1 reshape.62
  135.3 18.1 %all_to_all.50 = bf16[16,4,1024]{2,1,0:T(4,128)(2,1)S(1)} all-to-all(bf16[16,4,1024]{2,1,0:T(4,128)(2,1)S(1)} %reshape.62), channel_id=1, replica_groups=mesh['y'=4,'z'=16,'tensor'=8] {'z'}, dimensions={0} | all-to-all | bytes 262144 | tf_op jit(solution)/shard_map/all_to_all | solution.py:14
  153.4 0.7 reduce_sum.22
  (30 shorter events, 0.2 us)
Async XLA Ops:
  32.4 13.8 %copy-start.2 = (bf16[2,1024,192]{1,2,0:T(8,128)(2,1)S(1)}, bf16[2,1024,192]{1,2,0:T(8,128)(2,1)}, u32[]{:S(2)}) copy-start(bf16[2,1024,192]{1,2,0:T(8,128)(2,1)} %param.26) | copy-start | bytes 2359300
  33.3 12.9 %all-to-all-start.1 = ((bf16[4,64,1152]{2,1,0:T(8,128)(2,1)}), bf16[4,64,1152]{2,1,0:T(8,128)(2,1)S(1)}, u32[]{:S(2)}, u32[]{:S(2)}) async-start(bf16[4,64,1152]{2,1,0:T(8,128)(2,1)} %shard_map.168), calls=%async_computation.1 | async-start | bytes 1179648 | tf_op jit(solution)/shard_map/all_to_all | solution.py:14
  57.3 8.7 %copy-start.3 = (bf16[2,64,1024]{2,1,0:T(8,128)(2,1)S(1)}, bf16[2,64,1024]{2,1,0:T(8,128)(2,1)}, u32[]{:S(2)}) copy-start(bf16[2,64,1024]{2,1,0:T(8,128)(2,1)} %refs_3_.2) | copy-start | bytes 786436
  57.3 8.7 %copy-start.6 = (bf16[2,64,128]{2,1,0:T(8,128)(2,1)S(1)}, bf16[2,64,128]{2,1,0:T(8,128)(2,1)}, u32[]{:S(2)}) copy-start(bf16[2,64,128]{2,1,0:T(8,128)(2,1)} %refs_4_.2) | copy-start | bytes 98308
  57.3 8.7 %copy-start.7 = (bf16[2,64,128]{2,1,0:T(8,128)(2,1)S(1)}, bf16[2,64,128]{2,1,0:T(8,128)(2,1)}, u32[]{:S(2)}) copy-start(bf16[2,64,128]{2,1,0:T(8,128)(2,1)} %refs_5_.2) | copy-start | bytes 98308
  80.3 6.6 %copy-start.4 = (bf16[2,1024,64]{1,2,0:T(8,128)(2,1)S(1)}, bf16[2,1024,64]{1,2,0:T(8,128)(2,1)}, u32[]{:S(2)}) copy-start(bf16[2,1024,64]{1,2,0:T(8,128)(2,1)} %param.30) | copy-start | bytes 786436
  80.3 6.6 %copy-start.5 = (bf16[2,64,1024]{2,1,0:T(8,128)(2,1)S(1)}, bf16[2,64,1024]{2,1,0:T(8,128)(2,1)}, u32[]{:S(2)}) copy-start(bf16[2,64,1024]{2,1,0:T(8,128)(2,1)} %refs_1_.3) | copy-start | bytes 786436
  81.1 20.4 %copy-start = (bf16[32,128,128]{2,1,0:T(8,128)(2,1)S(1)}, bf16[32,128,128]{2,1,0:T(8,128)(2,1)}, u32[]{:S(2)}) copy-start(bf16[32,128,128]{2,1,0:T(8,128)(2,1)} %refs_6_.1) | copy-start | bytes 3145732
  81.1 20.4 %all-to-all-start.5 = ((bf16[16,4,1280]{2,1,0:T(4,128)(2,1)}), bf16[16,4,1280]{2,1,0:T(4,128)(2,1)S(1)}, u32[]{:S(2)}, u32[]{:S(2)}) async-start(bf16[16,4,1280]{2,1,0:T(4,128)(2,1)} %shard_map.171), calls=%async_computation.5 | async-start | bytes 327680 | tf_op jit(solution)/shard_map/all_to_all | solution.py:14
  86.9 14.6 %copy-start.8 = (bf16[4,1024]{1,0:T(4,128)(2,1)S(1)}, bf16[4,1024]{1,0:T(4,128)(2,1)}, u32[]{:S(2)}) copy-start(bf16[4,1024]{1,0:T(4,128)(2,1)} %refs_3_.3) | copy-start | bytes 24580
  86.9 14.6 %copy-start.9 = (s32[4,8]{1,0:T(4,128)S(1)}, s32[4,8]{1,0:T(4,128)}, u32[]{:S(2)}) copy-start(s32[4,8]{1,0:T(4,128)} %refs_0_.1) | copy-start | bytes 388
  86.9 14.6 %copy-start.10 = (bf16[4,128]{1,0:T(4,128)(2,1)S(1)}, bf16[4,128]{1,0:T(4,128)(2,1)}, u32[]{:S(2)}) copy-start(bf16[4,128]{1,0:T(4,128)(2,1)} %refs_4_.3) | copy-start | bytes 3076
  86.9 14.6 %copy-start.11 = (bf16[4,128]{1,0:T(4,128)(2,1)S(1)}, bf16[4,128]{1,0:T(4,128)(2,1)}, u32[]{:S(2)}) copy-start(bf16[4,128]{1,0:T(4,128)(2,1)} %refs_5_.3) | copy-start | bytes 3076
  86.9 14.6 %copy-start.12 = (s32[4]{0:T(128)S(1)}, s32[4]{0:T(128)}, u32[]{:S(2)}) copy-start(s32[4]{0:T(128)} %refs_1_.2) | copy-start | bytes 52
  87.0 37.7 %collective-permute-start.2 = (bf16[2,64,2048]{2,1,0:T(8,128)(2,1)S(1)}, bf16[2,64,2048]{2,1,0:T(8,128)(2,1)S(1)}, u32[]{:S(2)}, u32[]{:S(2)}) collective-permute-start(bf16[2,64,2048]{2,1,0:T(8,128)(2,1)S(1)} %shard_map.173.refs_3_), channel_id=1, source_target_pairs={{0,384},{128,0},{256,128},{384,256},{1,385},{129,1},{257,129},{385... | collective-permute-start | bytes 1572872 | tf_op jit(solution)/shard_map/ppermute | solution.py:250
  90.1 34.6 %collective-permute-start.1 = (bf16[2,64,2048]{2,1,0:T(8,128)(2,1)S(1)}, bf16[2,64,2048]{2,1,0:T(8,128)(2,1)S(1)}, u32[]{:S(2)}, u32[]{:S(2)}) collective-permute-start(bf16[2,64,2048]{2,1,0:T(8,128)(2,1)S(1)} %shard_map.173.refs_3_), channel_id=1, source_target_pairs={{0,256},{128,384},{256,0},{384,128},{1,257},{129,385},{257,1},{385... | collective-permute-start | bytes 1572872 | tf_op jit(solution)/shard_map/ppermute | solution.py:250
  93.5 31.2 %collective-permute-start = (bf16[2,64,2048]{2,1,0:T(8,128)(2,1)S(1)}, bf16[2,64,2048]{2,1,0:T(8,128)(2,1)S(1)}, u32[]{:S(2)}, u32[]{:S(2)}) collective-permute-start(bf16[2,64,2048]{2,1,0:T(8,128)(2,1)S(1)} %shard_map.173.refs_3_), channel_id=1, source_target_pairs={{0,128},{128,256},{256,384},{384,0},{1,129},{129,257},{257,385},{3... | collective-permute-start | bytes 1572872 | tf_op jit(solution)/shard_map/ppermute | solution.py:250
  101.5 1.2 copy-start.1
  105.4 19.2 %all-to-all-start.6 = ((bf16[16,4,1024]{2,1,0:T(4,128)(2,1)}), bf16[16,4,1024]{2,1,0:T(4,128)(2,1)S(1)}, u32[]{:S(2)}, u32[]{:S(2)}) async-start(bf16[16,4,1024]{2,1,0:T(4,128)(2,1)} %get-tuple-element.5), calls=%async_computation.6 | async-start | bytes 262144 | tf_op jit(solution)/shard_map/all_to_all | solution.py:14

commit v8 on v7

--- a/solution.py
+++ b/solution.py
@@ -73,7 +73,8 @@
 def attend(*refs):
     sources, (out_ref, block_ref), held, sems = refs[:8], refs[8:10], refs[10:18], refs[18]
     table_ref, length_ref, terms_ref, q_ref, k_ref, v_ref, keys_ref, values_ref = held
-    for copy in fetch(sources, held, sems):
+    copies = fetch(sources, held, sems)
+    for copy in copies[:7]:
         copy.wait()
     rows, width_q = q_ref.shape
     size = k_ref.shape[1]
@@ -103,6 +104,8 @@
         weights = jnp.where(live, jnp.exp(scores - top), 0.0)
         own_weight = jnp.exp(own - top)
         total = jnp.sum(weights, axis=1, keepdims=True) + own_weight
+        if r == 0:
+            copies[7].wait()
         values = jnp.concatenate([values_ref[page] for page in pages], axis=0)
         mixed = jnp.dot(weights.astype(jnp.bfloat16), values, preferred_element_type=jnp.float32)
         own_rounded = own_weight.astype(jnp.bfloat16).astype(jnp.float32)
@@ -131,6 +134,35 @@
     return jnp.where(tags == slots_ref[number].astype(jnp.float32), values, jnp.zeros_like(values))
 
 
+def write_packed(ranks, out_ref):
+    shares, packed_rows, lanes = out_ref.shape
+    rows = ranks.shape[0] // shares
+    half = packed_rows - rows
+    for t in range(shares):
+        share = ranks[t * rows : (t + 1) * rows]
+        out_ref[t, :rows] = share[:, :lanes]
+        out_ref[t, rows:] = jnp.concatenate(
+            [share[:half, lanes:], share[half:, lanes:]], axis=1
+        )
+
+
+def read_packed(ref):
+    shares, packed_rows, lanes = ref.shape
+    rows = packed_rows * 2 // 3
+    first, last = [], []
+    for t in range(shares):
+        share = ref[t].astype(jnp.float32)
+        first.append(share[:rows])
+        last += [share[rows:, : lanes // 2], share[rows:, lanes // 2 :]]
+    return jnp.concatenate([jnp.concatenate(first, 0), jnp.concatenate(last, 0)], axis=1)
+
+
+def rank_blocks(shares_ref, out_ref):
+    ranks = jnp.sum(shares_ref[...], axis=0).astype(jnp.bfloat16)
+    for t in range(out_ref.shape[0]):
+        out_ref[t] = ranks
+
+
 def down_first(slots_ref, rows_ref, weight_ref, out_ref):
     width = weight_ref.shape[2]
     rows, tags = rows_ref[:, :width], rows_ref[:, width : width + 1].astype(jnp.float32)
@@ -139,7 +171,7 @@
         product = lax.dot_general(rows, weight_ref[j], NT, preferred_element_type=jnp.float32)
         mine = picked(slots_ref, tags, product, j)
         total = mine if total is None else total + mine
-    out_ref[...] = total
+    write_packed(total, out_ref)
 
 
 def tags_of(rows_ref, at, width):
@@ -163,7 +195,7 @@
 def up_first(slots_ref, ranks_ref, rows_ref, q_up, k_up, v_up, out_ref):
     rank = q_up.shape[1]
     tags = tags_of(rows_ref, rows_ref.shape[1] - 128, rank)
-    ranks = ranks_ref[...].astype(jnp.float32)
+    ranks = read_packed(ranks_ref)
     at = 0
     for i, page in enumerate((q_up, k_up, v_up)):
         width = page.shape[2]
@@ -273,16 +305,18 @@
     z_rows = y_blocks[0]
     all_rows = exchange(y_blocks, Y).reshape(y_size * z_size * local_rows, -1)
 
+    packed_shape = (t_size, all_rows.shape[0] // t_size * 3 // 2, 2 * rank)
     part = call(
         down_first,
-        (y_size * z_size * local_rows, query_key_value_down.shape[2]),
+        packed_shape,
         jnp.float32,
         column_slots,
         all_rows,
         jnp.swapaxes(query_key_value_down, 1, 2),
     )
-    shares = exchange(part.reshape(t_size, -1, part.shape[1]), T)
-    ranks = spread(summed(shares).astype(jnp.bfloat16), T).reshape(part.shape)
+    ranks = exchange(
+        call(rank_blocks, packed_shape, jnp.bfloat16, exchange(part, T), scalars=0), T
+    )
     delta = call(
         up_first,
         (all_rows.shape[0], cuts[3]),

time: 157 us -> 156 us (level)
    pallas_call x7 -> x8, Pallas kernels: 5.62 us -> 5.7 us  [call(): pl.pallas_call(run, out_shape=jax.ShapeDtypeStruct(shape, dtype), in_spec...]
where the time goes in v8:
time: 156 us; the launch traced here: 153 us
  blocking collectives  88.1 us (56%)
  waiting for transfers between devices  26.7 us (17%)
  starting transfers between devices  24.6 us (16%)
  Pallas kernels  9.86 us (6%)
  local copies, waits for them, and re-layouts  2.38 us (2%)
    all_to_all x6, blocking collectives, exchange(): return lax.all_to_all(blocks, axis, 0, 0)  88.1 us
    all_to_all x3, waiting for transfers between devices, exchange(): return lax.all_to_all(blocks, axis, 0, 0)  26.7 us
    all_to_all x3, starting transfers between devices, exchange(): return lax.all_to_all(blocks, axis, 0, 0)  16.2 us
    ppermute x3, starting transfers between devices, packed(): lax.ppermute(mine, Y, [(i, (i + k) % y_size) for i in range(y_size)])  8.37 us
    pallas_call x8, Pallas kernels, call(): pl.pallas_call(run, out_shape=jax.ShapeDtypeStruct(shape, dtype), in_spec...  5.7 us
  transfers between devices with their start and end apart: 6, of which 3 were waited for; matrix products, arithmetic and copies ran while one was open for 1% of the time, Pallas kernels for 2%

profile of v8, /device:TPU:6, one launch (start us, length us, event | category | flops | bytes accessed | tf_op | source)
XLA Modules:
  0.0 153.2 jit_solution(8893659397878913722)
XLA Ops:
  0.6 1.4 shard_map.167
  2.0 30.3 %all_to_all.45.refs_0_ = bf16[16,4,1152]{2,1,0:T(4,128)(2,1)S(1)} all-to-all(bf16[16,4,1152]{2,1,0:T(4,128)(2,1)} %shard_map.167), channel_id=1, replica_groups=mesh['y'=4,'z'=16,'tensor'=8] {'z'}, dimensions={0} | all-to-all | bytes 294912 | tf_op jit(solution)/shard_map/all_to_all | solution.py:14
  32.4 0.9 shard_map.168
  33.3 4.5 %all-to-all-start.1 = ((bf16[4,64,1152]{2,1,0:T(8,128)(2,1)}), bf16[4,64,1152]{2,1,0:T(8,128)(2,1)S(1)}, u32[]{:S(2)}, u32[]{:S(2)}) async-start(bf16[4,64,1152]{2,1,0:T(8,128)(2,1)} %shard_map.168), calls=%async_computation.1 | async-start | bytes 1179648 | tf_op jit(solution)/shard_map/all_to_all | solution.py:14
  37.7 0.1 iota_add_fusion
  37.8 0.1 add.45.refs_0_
  37.9 8.3 %all-to-all-done.1 = bf16[4,64,1152]{2,1,0:T(8,128)(2,1)S(1)} async-done(((bf16[4,64,1152]{2,1,0:T(8,128)(2,1)}), bf16[4,64,1152]{2,1,0:T(8,128)(2,1)S(1)}, u32[]{:S(2)}, u32[]{:S(2)}) %all-to-all-start.1) | async-done | bytes 589856 | tf_op jit(solution)/shard_map/all_to_all | solution.py:14
  46.2 1.1 shard_map.169
  47.2 9.3 %all_to_all.46.refs_0_ = f32[8,48,128]{2,1,0:T(8,128)S(1)} all-to-all(f32[8,48,128]{2,1,0:T(8,128)S(1)} %shard_map.169), channel_id=1, replica_groups=mesh['y'=4,'z'=16,'tensor'=8] {'tensor'}, dimensions={0} | all-to-all | bytes 393216 | tf_op jit(solution)/shard_map/all_to_all | solution.py:14
  56.6 0.0 copy-start.6
  56.6 0.0 copy-start.7
  56.6 8.3 %all_to_all.47.refs_1_ = bf16[8,48,128]{2,1,0:T(8,128)(2,1)S(1)} all-to-all(bf16[8,48,128]{2,1,0:T(8,128)(2,1)S(1)} %shard_map.170), channel_id=1, replica_groups=mesh['y'=4,'z'=16,'tensor'=8] {'tensor'}, dimensions={0} | all-to-all | bytes 196608 | tf_op jit(solution)/shard_map/all_to_all | solution.py:14
  64.9 0.9 shard_map.171
  65.9 13.4 %all_to_all.48.refs_0_.refs_2_ = bf16[4,64,1280]{2,1,0:T(8,128)(2,1)S(1)} all-to-all(bf16[4,64,1280]{2,1,0:T(8,128)(2,1)S(1)} %bitcast.8), channel_id=1, replica_groups=mesh['y'=4,'z'=16,'tensor'=8] {'y'}, dimensions={0} | all-to-all | bytes 1310720 | tf_op jit(solution)/shard_map/all_to_all | solution.py:14
  79.3 0.8 shard_map.172
  80.1 5.8 %all-to-all-start.5 = ((bf16[16,4,1280]{2,1,0:T(4,128)(2,1)}), bf16[16,4,1280]{2,1,0:T(4,128)(2,1)S(1)}, u32[]{:S(2)}, u32[]{:S(2)}) async-start(bf16[16,4,1280]{2,1,0:T(4,128)(2,1)} %shard_map.172), calls=%async_computation.5 | async-start | bytes 327680 | tf_op jit(solution)/shard_map/all_to_all | solution.py:14
  85.9 0.0 copy-start.10
  86.0 3.1 %collective-permute-start.2 = (bf16[2,64,2048]{2,1,0:T(8,128)(2,1)S(1)}, bf16[2,64,2048]{2,1,0:T(8,128)(2,1)S(1)}, u32[]{:S(2)}, u32[]{:S(2)}) collective-permute-start(bf16[2,64,2048]{2,1,0:T(8,128)(2,1)S(1)} %shard_map.174.refs_3_), channel_id=1, source_target_pairs={{0,384},{128,0},{256,128},{384,256},{1,385},{129,1},{257,129},{385... | collective-permute-start | bytes 1572872 | tf_op jit(solution)/shard_map/ppermute | solution.py:282
  89.1 3.4 %collective-permute-start.1 = (bf16[2,64,2048]{2,1,0:T(8,128)(2,1)S(1)}, bf16[2,64,2048]{2,1,0:T(8,128)(2,1)S(1)}, u32[]{:S(2)}, u32[]{:S(2)}) collective-permute-start(bf16[2,64,2048]{2,1,0:T(8,128)(2,1)S(1)} %shard_map.174.refs_3_), channel_id=1, source_target_pairs={{0,256},{128,384},{256,0},{384,128},{1,257},{129,385},{257,1},{385... | collective-permute-start | bytes 1572872 | tf_op jit(solution)/shard_map/ppermute | solution.py:282
  92.5 1.9 %collective-permute-start = (bf16[2,64,2048]{2,1,0:T(8,128)(2,1)S(1)}, bf16[2,64,2048]{2,1,0:T(8,128)(2,1)S(1)}, u32[]{:S(2)}, u32[]{:S(2)}) collective-permute-start(bf16[2,64,2048]{2,1,0:T(8,128)(2,1)S(1)} %shard_map.174.refs_3_), channel_id=1, source_target_pairs={{0,128},{128,256},{256,384},{384,0},{1,129},{129,257},{257,385},{3... | collective-permute-start | bytes 1572872 | tf_op jit(solution)/shard_map/ppermute | solution.py:282
  94.4 6.1 %all-to-all-done.5.refs_2_ = bf16[16,4,1280]{2,1,0:T(4,128)(2,1)S(1)} async-done(((bf16[16,4,1280]{2,1,0:T(4,128)(2,1)}), bf16[16,4,1280]{2,1,0:T(4,128)(2,1)S(1)}, u32[]{:S(2)}, u32[]{:S(2)}) %all-to-all-start.5) | async-done | bytes 163872 | tf_op jit(solution)/shard_map/all_to_all | solution.py:14
  100.6 1.2 copy-done.1
  101.8 2.8 %shard_map.173 = (bf16[4,1024]{1,0:T(4,128)(2,1)}, bf16[16,4,1024]{2,1,0:T(4,128)(2,1)}) custom-call(s32[4,8]{1,0:T(4,128)S(1)} %copy-done.9, s32[4]{0:T(128)S(1)} %copy-done.12, bf16[16,4,1280]{2,1,0:T(4,128)(2,1)S(1)} %all-to-all-done.5.refs_2_, bf16[4,1024]{1,0:T(4,128)(2,1)S(1)} %copy-done.8, bf16[4,128]{1,0:T(4,128)(2,1)S(1)} %copy-done.10, ...), custom_call_target="tpu_custom_call" | custom-call | tf_op jit(solution)/shard_map/pallas_call | solution.py:338
  104.5 5.9 %all-to-all-start.6 = ((bf16[16,4,1024]{2,1,0:T(4,128)(2,1)}), bf16[16,4,1024]{2,1,0:T(4,128)(2,1)S(1)}, u32[]{:S(2)}, u32[]{:S(2)}) async-start(bf16[16,4,1024]{2,1,0:T(4,128)(2,1)} %get-tuple-element.5), calls=%async_computation.6 | async-start | bytes 262144 | tf_op jit(solution)/shard_map/all_to_all | solution.py:14
  110.5 0.9 slice_bitcast_fusion.refs_2_
  111.4 12.3 %all-to-all-done.6 = bf16[16,4,1024]{2,1,0:T(4,128)(2,1)S(1)} async-done(((bf16[16,4,1024]{2,1,0:T(4,128)(2,1)}), bf16[16,4,1024]{2,1,0:T(4,128)(2,1)S(1)}, u32[]{:S(2)}, u32[]{:S(2)}) %all-to-all-start.6) | async-done | bytes 131104 | tf_op jit(solution)/shard_map/all_to_all | solution.py:14
  123.8 1.0 shard_map.175
  124.8 8.5 %all_to_all.49.refs_1_ = f32[8,32,128]{2,1,0:T(8,128)S(1)} all-to-all(f32[8,32,128]{2,1,0:T(8,128)S(1)} %shard_map.175), channel_id=1, replica_groups=mesh['y'=4,'z'=16,'tensor'=8] {'tensor'}, dimensions={0} | all-to-all | bytes 262144 | tf_op jit(solution)/shard_map/all_to_all | solution.py:14
  133.3 1.0 shard_map.176
  134.3 0.1 reshape.51
  134.4 18.2 %all_to_all.50 = bf16[16,4,1024]{2,1,0:T(4,128)(2,1)S(1)} all-to-all(bf16[16,4,1024]{2,1,0:T(4,128)(2,1)S(1)} %reshape.51), channel_id=1, replica_groups=mesh['y'=4,'z'=16,'tensor'=8] {'z'}, dimensions={0} | all-to-all | bytes 262144 | tf_op jit(solution)/shard_map/all_to_all | solution.py:14
  152.5 0.7 reduce_sum.12
  (29 shorter events, 0.2 us)
Async XLA Ops:
  32.4 13.8 %copy-start.2 = (bf16[2,1024,192]{1,2,0:T(8,128)(2,1)S(1)}, bf16[2,1024,192]{1,2,0:T(8,128)(2,1)}, u32[]{:S(2)}) copy-start(bf16[2,1024,192]{1,2,0:T(8,128)(2,1)} %param.26) | copy-start | bytes 2359300
  33.3 12.9 %all-to-all-start.1 = ((bf16[4,64,1152]{2,1,0:T(8,128)(2,1)}), bf16[4,64,1152]{2,1,0:T(8,128)(2,1)S(1)}, u32[]{:S(2)}, u32[]{:S(2)}) async-start(bf16[4,64,1152]{2,1,0:T(8,128)(2,1)} %shard_map.168), calls=%async_computation.1 | async-start | bytes 1179648 | tf_op jit(solution)/shard_map/all_to_all | solution.py:14
  56.6 8.4 %copy-start.3 = (bf16[2,64,1024]{2,1,0:T(8,128)(2,1)S(1)}, bf16[2,64,1024]{2,1,0:T(8,128)(2,1)}, u32[]{:S(2)}) copy-start(bf16[2,64,1024]{2,1,0:T(8,128)(2,1)} %refs_3_.2) | copy-start | bytes 786436
  56.6 8.3 %copy-start.6 = (bf16[2,64,128]{2,1,0:T(8,128)(2,1)S(1)}, bf16[2,64,128]{2,1,0:T(8,128)(2,1)}, u32[]{:S(2)}) copy-start(bf16[2,64,128]{2,1,0:T(8,128)(2,1)} %refs_4_.2) | copy-start | bytes 98308
  56.6 8.3 %copy-start.7 = (bf16[2,64,128]{2,1,0:T(8,128)(2,1)S(1)}, bf16[2,64,128]{2,1,0:T(8,128)(2,1)}, u32[]{:S(2)}) copy-start(bf16[2,64,128]{2,1,0:T(8,128)(2,1)} %refs_5_.2) | copy-start | bytes 98308
  79.3 6.6 %copy-start.4 = (bf16[2,1024,64]{1,2,0:T(8,128)(2,1)S(1)}, bf16[2,1024,64]{1,2,0:T(8,128)(2,1)}, u32[]{:S(2)}) copy-start(bf16[2,1024,64]{1,2,0:T(8,128)(2,1)} %param.30) | copy-start | bytes 786436
  79.3 6.6 %copy-start.5 = (bf16[2,64,1024]{2,1,0:T(8,128)(2,1)S(1)}, bf16[2,64,1024]{2,1,0:T(8,128)(2,1)}, u32[]{:S(2)}) copy-start(bf16[2,64,1024]{2,1,0:T(8,128)(2,1)} %refs_1_.3) | copy-start | bytes 786436
  80.1 20.4 %copy-start = (bf16[32,128,128]{2,1,0:T(8,128)(2,1)S(1)}, bf16[32,128,128]{2,1,0:T(8,128)(2,1)}, u32[]{:S(2)}) copy-start(bf16[32,128,128]{2,1,0:T(8,128)(2,1)} %refs_6_.1) | copy-start | bytes 3145732
  80.1 20.4 %all-to-all-start.5 = ((bf16[16,4,1280]{2,1,0:T(4,128)(2,1)}), bf16[16,4,1280]{2,1,0:T(4,128)(2,1)S(1)}, u32[]{:S(2)}, u32[]{:S(2)}) async-start(bf16[16,4,1280]{2,1,0:T(4,128)(2,1)} %shard_map.172), calls=%async_computation.5 | async-start | bytes 327680 | tf_op jit(solution)/shard_map/all_to_all | solution.py:14
  85.9 14.6 %copy-start.8 = (bf16[4,1024]{1,0:T(4,128)(2,1)S(1)}, bf16[4,1024]{1,0:T(4,128)(2,1)}, u32[]{:S(2)}) copy-start(bf16[4,1024]{1,0:T(4,128)(2,1)} %refs_3_.3) | copy-start | bytes 24580
  85.9 14.6 %copy-start.9 = (s32[4,8]{1,0:T(4,128)S(1)}, s32[4,8]{1,0:T(4,128)}, u32[]{:S(2)}) copy-start(s32[4,8]{1,0:T(4,128)} %refs_0_.1) | copy-start | bytes 388
  85.9 14.6 %copy-start.10 = (bf16[4,128]{1,0:T(4,128)(2,1)S(1)}, bf16[4,128]{1,0:T(4,128)(2,1)}, u32[]{:S(2)}) copy-start(bf16[4,128]{1,0:T(4,128)(2,1)} %refs_4_.3) | copy-start | bytes 3076
  85.9 14.6 %copy-start.11 = (bf16[4,128]{1,0:T(4,128)(2,1)S(1)}, bf16[4,128]{1,0:T(4,128)(2,1)}, u32[]{:S(2)}) copy-start(bf16[4,128]{1,0:T(4,128)(2,1)} %refs_5_.3) | copy-start | bytes 3076
  85.9 14.6 %copy-start.12 = (s32[4]{0:T(128)S(1)}, s32[4]{0:T(128)}, u32[]{:S(2)}) copy-start(s32[4]{0:T(128)} %refs_1_.2) | copy-start | bytes 52
  86.0 37.8 %collective-permute-start.2 = (bf16[2,64,2048]{2,1,0:T(8,128)(2,1)S(1)}, bf16[2,64,2048]{2,1,0:T(8,128)(2,1)S(1)}, u32[]{:S(2)}, u32[]{:S(2)}) collective-permute-start(bf16[2,64,2048]{2,1,0:T(8,128)(2,1)S(1)} %shard_map.174.refs_3_), channel_id=1, source_target_pairs={{0,384},{128,0},{256,128},{384,256},{1,385},{129,1},{257,129},{385... | collective-permute-start | bytes 1572872 | tf_op jit(solution)/shard_map/ppermute | solution.py:282
  89.1 34.7 %collective-permute-start.1 = (bf16[2,64,2048]{2,1,0:T(8,128)(2,1)S(1)}, bf16[2,64,2048]{2,1,0:T(8,128)(2,1)S(1)}, u32[]{:S(2)}, u32[]{:S(2)}) collective-permute-start(bf16[2,64,2048]{2,1,0:T(8,128)(2,1)S(1)} %shard_map.174.refs_3_), channel_id=1, source_target_pairs={{0,256},{128,384},{256,0},{384,128},{1,257},{129,385},{257,1},{385... | collective-permute-start | bytes 1572872 | tf_op jit(solution)/shard_map/ppermute | solution.py:282
  92.5 31.3 %collective-permute-start = (bf16[2,64,2048]{2,1,0:T(8,128)(2,1)S(1)}, bf16[2,64,2048]{2,1,0:T(8,128)(2,1)S(1)}, u32[]{:S(2)}, u32[]{:S(2)}) collective-permute-start(bf16[2,64,2048]{2,1,0:T(8,128)(2,1)S(1)} %shard_map.174.refs_3_), channel_id=1, source_target_pairs={{0,128},{128,256},{256,384},{384,0},{1,129},{129,257},{257,385},{3... | collective-permute-start | bytes 1572872 | tf_op jit(solution)/shard_map/ppermute | solution.py:282
  100.5 1.2 copy-start.1
  104.5 19.2 %all-to-all-start.6 = ((bf16[16,4,1024]{2,1,0:T(4,128)(2,1)}), bf16[16,4,1024]{2,1,0:T(4,128)(2,1)S(1)}, u32[]{:S(2)}, u32[]{:S(2)}) async-start(bf16[16,4,1024]{2,1,0:T(4,128)(2,1)} %get-tuple-element.5), calls=%async_computation.6 | async-start | bytes 262144 | tf_op jit(solution)/shard_map/all_to_all | solution.py:14

commit v9 on v8

--- a/solution.py
+++ b/solution.py
@@ -146,12 +146,11 @@
         )
 
 
-def read_packed(ref):
-    shares, packed_rows, lanes = ref.shape
+def read_packed(packed):
+    packed_rows, lanes = packed[0].shape
     rows = packed_rows * 2 // 3
     first, last = [], []
-    for t in range(shares):
-        share = ref[t].astype(jnp.float32)
+    for share in packed:
         first.append(share[:rows])
         last += [share[rows:, : lanes // 2], share[rows:, lanes // 2 :]]
     return jnp.concatenate([jnp.concatenate(first, 0), jnp.concatenate(last, 0)], axis=1)
@@ -192,20 +191,26 @@
     return (adapter_scale * total).astype(jnp.bfloat16)
 
 
-def up_first(slots_ref, ranks_ref, rows_ref, q_up, k_up, v_up, out_ref):
-    rank = q_up.shape[1]
-    tags = tags_of(rows_ref, rows_ref.shape[1] - 128, rank)
-    ranks = read_packed(ranks_ref)
-    at = 0
-    for i, page in enumerate((q_up, k_up, v_up)):
-        width = page.shape[2]
-        mine = ranks[:, i * rank : (i + 1) * rank]
-        out_ref[:, at : at + width] = grown(slots_ref, tags, mine, [page], 0, width)
-        at += width
-
-
-def term_blocks(from_y_ref, out_ref):
-    out_ref[...] = summed(from_y_ref[...]).reshape(out_ref.shape).astype(jnp.bfloat16)
+def make_up_first(cuts):
+    def up_first(slots_ref, place_ref, ranks_ref, rows_ref, *refs):
+        pages, out_ref = refs[:-1], refs[-1]
+        y_size, shares = len(pages), ranks_ref.shape[0] // len(pages)
+        mine = []
+        for i in range(shares // y_size):
+            share = place_ref[0] * (shares // y_size) + i
+            parts = [ranks_ref[y * shares + share].astype(jnp.float32) for y in range(y_size)]
+            mine.append(sum(parts[1:], parts[0]))
+        ranks = read_packed(mine)
+        rank = pages[0].shape[1]
+        tags = tags_of(rows_ref, rows_ref.shape[1] - 128, rank)
+        for i in range(3):
+            width = cuts[i + 1] - cuts[i]
+            values = ranks[:, i * rank : (i + 1) * rank]
+            term = grown(slots_ref, tags, values, pages, cuts[i], width)
+            blocks = term.astype(jnp.float32).reshape(out_ref.shape[:2] + (width,))
+            out_ref[:, :, cuts[i] : cuts[i + 1]] = blocks.astype(jnp.bfloat16)
+
+    return up_first
 
 
 def make_down_second(at):
@@ -283,6 +288,7 @@
             for k in range(1, y_size)
         ]
 
+    up_pages = packed(query_up_weight, key_up_weight, value_up_weight)
     z_blocks = pl.pallas_call(
         first_blocks,
         out_shape=jax.ShapeDtypeStruct((z_size, local_rows, local_width + 128), jnp.bfloat16),
@@ -301,6 +307,7 @@
         jnp.bfloat16,
         exchange(z_blocks, Z),
         scalars=0,
+        after=up_pages[1:2],
     )
     z_rows = y_blocks[0]
     all_rows = exchange(y_blocks, Y).reshape(y_size * z_size * local_rows, -1)
@@ -315,25 +322,30 @@
         jnp.swapaxes(query_key_value_down, 1, 2),
     )
     ranks = exchange(
-        call(rank_blocks, packed_shape, jnp.bfloat16, exchange(part, T), scalars=0), T
-    )
-    delta = call(
-        up_first,
-        (all_rows.shape[0], cuts[3]),
+        call(
+            rank_blocks,
+            (y_size * t_size,) + packed_shape[1:],
+            jnp.bfloat16,
+            exchange(part, T),
+            scalars=0,
+            after=up_pages[2:],
+        ),
+        (Y, T),
+    )
+    blocks = call(
+        make_up_first(cuts),
+        (z_size, local_rows, cuts[3]),
         jnp.bfloat16,
         column_slots,
+        own_y[None].astype(jnp.int32),
         ranks,
-        all_rows,
-        query_up_weight,
-        key_up_weight,
-        value_up_weight,
-    )
-    from_y = exchange(delta.reshape(y_size, z_size * local_rows, cuts[3]), Y)
-    terms = exchange(
-        call(term_blocks, (z_size, local_rows, cuts[3]), jnp.bfloat16, from_y, scalars=0), Z
-    )
+        z_rows,
+        *up_pages,
+        scalars=2,
+    )
+    terms = exchange(blocks, Z)
     out_pages = packed(
-        jnp.swapaxes(output_down_weight, 1, 2), output_up_weight, after=(from_y,)
+        jnp.swapaxes(output_down_weight, 1, 2), output_up_weight, after=(ranks,)
     )
     attention, out_blocks = pl.pallas_call(
         attend,

time: 156 us -> 158 us (1.013)
  blocking collectives: 88.1 us -> 47.7 us
  starting transfers between devices: 24.6 us -> 60.2 us
  waiting for transfers between devices: 26.7 us -> 31 us
    all_to_all x6 -> x3, blocking collectives: 88.1 us -> 47.7 us  [exchange(): return lax.all_to_all(blocks, axis, 0, 0)]
    all_to_all x3 -> x5, starting transfers between devices: 16.2 us -> 40.1 us  [exchange(): return lax.all_to_all(blocks, axis, 0, 0)]
    ppermute x3 -> x6, starting transfers between devices: 8.37 us -> 20.1 us  [packed(): lax.ppermute(mine, Y, [(i, (i + k) % y_size) for i in range(y_size)])]
    ppermute x3 -> x6, waiting for transfers between devices: 0.01 us -> 8.87 us  [packed(): lax.ppermute(mine, Y, [(i, (i + k) % y_size) for i in range(y_size)])]
    all_to_all x3 -> x5, waiting for transfers between devices: 26.7 us -> 22.2 us  [exchange(): return lax.all_to_all(blocks, axis, 0, 0)]
  transfers between devices with their start and end apart: 6 -> 11, of which waited for: 3 -> 6; matrix products, arithmetic and copies ran while one was open for 1% -> 1% of each run, Pallas kernels for 2% -> 3%
where the time goes in v9:
time: 158 us; the launch traced here: 156 us
  starting transfers between devices  60.2 us (38%)
  blocking collectives  47.7 us (30%)
  waiting for transfers between devices  31 us (20%)
  Pallas kernels  11.3 us (7%)
  local copies, waits for them, and re-layouts  3.6 us (2%)
    all_to_all x3, blocking collectives, exchange(): return lax.all_to_all(blocks, axis, 0, 0)  47.7 us
    all_to_all x5, starting transfers between devices, exchange(): return lax.all_to_all(blocks, axis, 0, 0)  40.1 us
    all_to_all x5, waiting for transfers between devices, exchange(): return lax.all_to_all(blocks, axis, 0, 0)  22.2 us
    ppermute x6, starting transfers between devices, packed(): lax.ppermute(mine, Y, [(i, (i + k) % y_size) for i in range(y_size)])  20.1 us
    ppermute x6, waiting for transfers between devices, packed(): lax.ppermute(mine, Y, [(i, (i + k) % y_size) for i in range(y_size)])  8.87 us
    pallas_call x8, Pallas kernels, call(): pl.pallas_call(run, out_shape=jax.ShapeDtypeStruct(shape, dtype), in_spec...  7.12 us
  transfers between devices with their start and end apart: 11, of which 6 were waited for; matrix products, arithmetic and copies ran while one was open for 1% of the time, Pallas kernels for 3%

profile of v9, /device:TPU:6, one launch (start us, length us, event | category | flops | bytes accessed | tf_op | source)
XLA Modules:
  0.0 155.6 jit_solution(8903354614958972424)
XLA Ops:
  0.6 1.5 shard_map.167
  2.2 15.2 %all-to-all-start = ((bf16[16,4,1152]{2,1,0:T(4,128)(2,1)}), bf16[16,4,1152]{2,1,0:T(4,128)(2,1)S(1)}, u32[]{:S(2)}, u32[]{:S(2)}) async-start(bf16[16,4,1152]{2,1,0:T(4,128)(2,1)} %shard_map.167), calls=%async_computation | async-start | bytes 294912 | tf_op jit(solution)/shard_map/all_to_all | solution.py:14
  17.5 3.5 %collective-permute-start = (bf16[2,64,1280]{2,1,0:T(8,128)(2,1)S(1)}, bf16[2,64,1280]{2,1,0:T(8,128)(2,1)S(1)}, u32[]{:S(2)}, u32[]{:S(2)}) collective-permute-start(bf16[2,64,1280]{2,1,0:T(8,128)(2,1)S(1)} %shard_map.168.refs_4_), channel_id=1, source_target_pairs={{0,128},{128,256},{256,384},{384,0},{1,129},{129,257},{257,385},{3... | collective-permute-start | bytes 983048 | tf_op jit(solution)/shard_map/ppermute | solution.py:287
  21.0 8.9 %collective-permute-done.refs_1_.refs_5_ = bf16[2,64,1280]{2,1,0:T(8,128)(2,1)S(1)} collective-permute-done((bf16[2,64,1280]{2,1,0:T(8,128)(2,1)S(1)}, bf16[2,64,1280]{2,1,0:T(8,128)(2,1)S(1)}, u32[]{:S(2)}, u32[]{:S(2)}) %collective-permute-start) | collective-permute-done | bytes 327712 | tf_op jit(solution)/shard_map/ppermute | solution.py:287
  29.8 2.7 %all-to-all-done.refs_0_ = bf16[16,4,1152]{2,1,0:T(4,128)(2,1)S(1)} async-done(((bf16[16,4,1152]{2,1,0:T(4,128)(2,1)}), bf16[16,4,1152]{2,1,0:T(4,128)(2,1)S(1)}, u32[]{:S(2)}, u32[]{:S(2)}) %all-to-all-start) | async-done | bytes 147488 | tf_op jit(solution)/shard_map/all_to_all | solution.py:14
  32.5 0.9 shard_map.169
  33.4 4.6 %all-to-all-start.1 = ((bf16[4,64,1152]{2,1,0:T(8,128)(2,1)}), bf16[4,64,1152]{2,1,0:T(8,128)(2,1)S(1)}, u32[]{:S(2)}, u32[]{:S(2)}) async-start(bf16[4,64,1152]{2,1,0:T(8,128)(2,1)} %shard_map.169), calls=%async_computation.1 | async-start | bytes 1179648 | tf_op jit(solution)/shard_map/all_to_all | solution.py:14
  38.0 5.1 %collective-permute-start.2 = (bf16[2,64,1280]{2,1,0:T(8,128)(2,1)S(1)}, bf16[2,64,1280]{2,1,0:T(8,128)(2,1)S(1)}, u32[]{:S(2)}, u32[]{:S(2)}) collective-permute-start(bf16[2,64,1280]{2,1,0:T(8,128)(2,1)S(1)} %shard_map.168.refs_4_), channel_id=1, source_target_pairs={{0,384},{128,0},{256,128},{384,256},{1,385},{129,1},{257,129},{385... | collective-permute-start | bytes 983048 | tf_op jit(solution)/shard_map/ppermute | solution.py:287
  43.2 2.8 %collective-permute-start.1 = (bf16[2,64,1280]{2,1,0:T(8,128)(2,1)S(1)}, bf16[2,64,1280]{2,1,0:T(8,128)(2,1)S(1)}, u32[]{:S(2)}, u32[]{:S(2)}) collective-permute-start(bf16[2,64,1280]{2,1,0:T(8,128)(2,1)S(1)} %shard_map.168.refs_4_), channel_id=1, source_target_pairs={{0,256},{128,384},{256,0},{384,128},{1,257},{129,385},{257,1},{385... | collective-permute-start | bytes 983048 | tf_op jit(solution)/shard_map/ppermute | solution.py:287
  46.1 1.9 %all-to-all-done.1 = bf16[4,64,1152]{2,1,0:T(8,128)(2,1)S(1)} async-done(((bf16[4,64,1152]{2,1,0:T(8,128)(2,1)}), bf16[4,64,1152]{2,1,0:T(8,128)(2,1)S(1)}, u32[]{:S(2)}, u32[]{:S(2)}) %all-to-all-start.1) | async-done | bytes 589856 | tf_op jit(solution)/shard_map/all_to_all | solution.py:14
  48.0 1.7 %shard_map.170 = f32[8,48,128]{2,1,0:T(8,128)} custom-call(s32[8]{0:T(128)S(1)} %add.45.refs_0_, bf16[256,1152]{1,0:T(8,128)(2,1)S(1)} %bitcast.6, bf16[2,192,1024]{2,1,0:T(8,128)(2,1)S(1)} %bitcast.7), custom_call_target="tpu_custom_call" | custom-call | tf_op jit(solution)/shard_map/pallas_call | solution.py:40
  49.8 4.8 %all-to-all-start.2 = ((f32[8,48,128]{2,1,0:T(8,128)}), f32[8,48,128]{2,1,0:T(8,128)S(1)}, u32[]{:S(2)}, u32[]{:S(2)}) async-start(f32[8,48,128]{2,1,0:T(8,128)} %shard_map.170), calls=%async_computation.2 | async-start | bytes 393216 | tf_op jit(solution)/shard_map/all_to_all | solution.py:14
  54.6 4.8 %all-to-all-done.2.refs_0_ = f32[8,48,128]{2,1,0:T(8,128)S(1)} async-done(((f32[8,48,128]{2,1,0:T(8,128)}), f32[8,48,128]{2,1,0:T(8,128)S(1)}, u32[]{:S(2)}, u32[]{:S(2)}) %all-to-all-start.2) | async-done | bytes 196640 | tf_op jit(solution)/shard_map/all_to_all | solution.py:14
  59.3 0.8 shard_map.171
  60.1 7.0 %all-to-all-start.3 = ((bf16[32,48,128]{2,1,0:T(8,128)(2,1)}), bf16[32,48,128]{2,1,0:T(8,128)(2,1)S(1)}, u32[]{:S(2)}, u32[]{:S(2)}) async-start(bf16[32,48,128]{2,1,0:T(8,128)(2,1)} %shard_map.171), calls=%async_computation.3 | async-start | bytes 786432 | tf_op jit(solution)/shard_map/all_to_all | solution.py:14
  67.2 0.9 slice_bitcast_fusion.refs_3_.refs_2_
  68.1 7.1 %all-to-all-done.3.refs_2_ = bf16[32,48,128]{2,1,0:T(8,128)(2,1)S(1)} async-done(((bf16[32,48,128]{2,1,0:T(8,128)(2,1)}), bf16[32,48,128]{2,1,0:T(8,128)(2,1)S(1)}, u32[]{:S(2)}, u32[]{:S(2)}) %all-to-all-start.3) | async-done | bytes 393248 | tf_op jit(solution)/shard_map/all_to_all | solution.py:14
  75.2 1.6 %shard_map.172 = bf16[16,4,1280]{2,1,0:T(4,128)(2,1)} custom-call(s32[8]{0:T(128)S(1)} %add.45.refs_0_, s32[1]{0:T(128)} %bitcast.refs_1_, bf16[32,48,128]{2,1,0:T(8,128)(2,1)S(1)} %all-to-all-done.3.refs_2_, bf16[64,1152]{1,0:T(8,128)(2,1)S(1)} %slice_bitcast_fusion.refs_3_.refs_2_, bf16[2,64,1280]{2,1,0:T(8,128)(2,1)S(1)} %shard_map.168.refs_4_, ...), custom_call_target="tpu_custom_call" | custom-call | tf_op jit(solution)/shard_map/pallas_call | solution.py:40
  76.8 8.5 %all-to-all-start.4 = ((bf16[16,4,1280]{2,1,0:T(4,128)(2,1)}), bf16[16,4,1280]{2,1,0:T(4,128)(2,1)S(1)}, u32[]{:S(2)}, u32[]{:S(2)}) async-start(bf16[16,4,1280]{2,1,0:T(4,128)(2,1)} %shard_map.172), calls=%async_computation.4 | async-start | bytes 327680 | tf_op jit(solution)/shard_map/all_to_all | solution.py:14
  85.5 3.0 %collective-permute-start.5 = (bf16[2,64,2048]{2,1,0:T(8,128)(2,1)S(1)}, bf16[2,64,2048]{2,1,0:T(8,128)(2,1)S(1)}, u32[]{:S(2)}, u32[]{:S(2)}) collective-permute-start(bf16[2,64,2048]{2,1,0:T(8,128)(2,1)S(1)} %shard_map.174.refs_3_), channel_id=1, source_target_pairs={{0,384},{128,0},{256,128},{384,256},{1,385},{129,1},{257,129},{385... | collective-permute-start | bytes 1572872 | tf_op jit(solution)/shard_map/ppermute | solution.py:287
  88.5 3.4 %collective-permute-start.4 = (bf16[2,64,2048]{2,1,0:T(8,128)(2,1)S(1)}, bf16[2,64,2048]{2,1,0:T(8,128)(2,1)S(1)}, u32[]{:S(2)}, u32[]{:S(2)}) collective-permute-start(bf16[2,64,2048]{2,1,0:T(8,128)(2,1)S(1)} %shard_map.174.refs_3_), channel_id=1, source_target_pairs={{0,256},{128,384},{256,0},{384,128},{1,257},{129,385},{257,1},{385... | collective-permute-start | bytes 1572872 | tf_op jit(solution)/shard_map/ppermute | solution.py:287
  92.0 2.2 %collective-permute-start.3 = (bf16[2,64,2048]{2,1,0:T(8,128)(2,1)S(1)}, bf16[2,64,2048]{2,1,0:T(8,128)(2,1)S(1)}, u32[]{:S(2)}, u32[]{:S(2)}) collective-permute-start(bf16[2,64,2048]{2,1,0:T(8,128)(2,1)S(1)} %shard_map.174.refs_3_), channel_id=1, source_target_pairs={{0,128},{128,256},{256,384},{384,0},{1,129},{129,257},{257,385},{3... | collective-permute-start | bytes 1572872 | tf_op jit(solution)/shard_map/ppermute | solution.py:287
  94.2 5.7 %all-to-all-done.4.refs_2_ = bf16[16,4,1280]{2,1,0:T(4,128)(2,1)S(1)} async-done(((bf16[16,4,1280]{2,1,0:T(4,128)(2,1)}), bf16[16,4,1280]{2,1,0:T(4,128)(2,1)S(1)}, u32[]{:S(2)}, u32[]{:S(2)}) %all-to-all-start.4) | async-done | bytes 163872 | tf_op jit(solution)/shard_map/all_to_all | solution.py:14
  99.9 1.2 copy-done
  101.1 1.2 copy-done.1
  102.4 2.7 %shard_map.173 = (bf16[4,1024]{1,0:T(4,128)(2,1)}, bf16[16,4,1024]{2,1,0:T(4,128)(2,1)S(1)}) custom-call(s32[4,8]{1,0:T(4,128)S(1)} %copy-done.9, s32[4]{0:T(128)S(1)} %copy-done.12, bf16[16,4,1280]{2,1,0:T(4,128)(2,1)S(1)} %all-to-all-done.4.refs_2_, bf16[4,1024]{1,0:T(4,128)(2,1)S(1)} %copy-done.8, bf16[4,128]{1,0:T(4,128)(2,1)S(1)} %copy-done.10, ...), custom_call_target="tpu_custom_call" | custom-call | tf_op jit(solution)/shard_map/pallas_call | solution.py:350
  105.1 21.0 %all_to_all.40 = bf16[16,4,1024]{2,1,0:T(4,128)(2,1)S(1)} all-to-all(bf16[16,4,1024]{2,1,0:T(4,128)(2,1)S(1)} %get-tuple-element.5), channel_id=1, replica_groups=mesh['y'=4,'z'=16,'tensor'=8] {'z'}, dimensions={0} | all-to-all | bytes 262144 | tf_op jit(solution)/shard_map/all_to_all | solution.py:14
  126.1 1.0 shard_map.175
  127.2 8.4 %all_to_all.41.refs_1_ = f32[8,32,128]{2,1,0:T(8,128)S(1)} all-to-all(f32[8,32,128]{2,1,0:T(8,128)S(1)} %shard_map.175), channel_id=1, replica_groups=mesh['y'=4,'z'=16,'tensor'=8] {'tensor'}, dimensions={0} | all-to-all | bytes 262144 | tf_op jit(solution)/shard_map/all_to_all | solution.py:14
  135.5 1.0 shard_map.176
  136.6 18.4 %all_to_all.42 = bf16[16,4,1024]{2,1,0:T(4,128)(2,1)S(1)} all-to-all(bf16[16,4,1024]{2,1,0:T(4,128)(2,1)S(1)} %reshape.47), channel_id=1, replica_groups=mesh['y'=4,'z'=16,'tensor'=8] {'z'}, dimensions={0} | all-to-all | bytes 262144 | tf_op jit(solution)/shard_map/all_to_all | solution.py:14
  154.9 0.7 reduce_sum.12
  (36 shorter events, 0.4 us)
Async XLA Ops:
  0.6 16.8 %copy-start.3 = (bf16[2,64,1024]{2,1,0:T(8,128)(2,1)S(1)}, bf16[2,64,1024]{2,1,0:T(8,128)(2,1)}, u32[]{:S(2)}) copy-start(bf16[2,64,1024]{2,1,0:T(8,128)(2,1)} %refs_0_.2) | copy-start | bytes 786436
  2.2 15.3 %copy-start.6 = (bf16[2,64,128]{2,1,0:T(8,128)(2,1)S(1)}, bf16[2,64,128]{2,1,0:T(8,128)(2,1)}, u32[]{:S(2)}) copy-start(bf16[2,64,128]{2,1,0:T(8,128)(2,1)} %refs_1_.3) | copy-start | bytes 98308
  2.2 15.2 %copy-start.7 = (bf16[2,64,128]{2,1,0:T(8,128)(2,1)S(1)}, bf16[2,64,128]{2,1,0:T(8,128)(2,1)}, u32[]{:S(2)}) copy-start(bf16[2,64,128]{2,1,0:T(8,128)(2,1)} %refs_2_.1) | copy-start | bytes 98308
  2.2 30.3 %all-to-all-start = ((bf16[16,4,1152]{2,1,0:T(4,128)(2,1)}), bf16[16,4,1152]{2,1,0:T(4,128)(2,1)S(1)}, u32[]{:S(2)}, u32[]{:S(2)}) async-start(bf16[16,4,1152]{2,1,0:T(4,128)(2,1)} %shard_map.167), calls=%async_computation | async-start | bytes 294912 | tf_op jit(solution)/shard_map/all_to_all | solution.py:14
  17.5 12.3 %collective-permute-start = (bf16[2,64,1280]{2,1,0:T(8,128)(2,1)S(1)}, bf16[2,64,1280]{2,1,0:T(8,128)(2,1)S(1)}, u32[]{:S(2)}, u32[]{:S(2)}) collective-permute-start(bf16[2,64,1280]{2,1,0:T(8,128)(2,1)S(1)} %shard_map.168.refs_4_), channel_id=1, source_target_pairs={{0,128},{128,256},{256,384},{384,0},{1,129},{129,257},{257,385},{3... | collective-permute-start | bytes 983048 | tf_op jit(solution)/shard_map/ppermute | solution.py:287
  33.4 14.6 %copy-start.2 = (bf16[2,1024,192]{1,2,0:T(8,128)(2,1)S(1)}, bf16[2,1024,192]{1,2,0:T(8,128)(2,1)}, u32[]{:S(2)}) copy-start(bf16[2,1024,192]{1,2,0:T(8,128)(2,1)} %param.26) | copy-start | bytes 2359300
  33.4 14.6 %all-to-all-start.1 = ((bf16[4,64,1152]{2,1,0:T(8,128)(2,1)}), bf16[4,64,1152]{2,1,0:T(8,128)(2,1)S(1)}, u32[]{:S(2)}, u32[]{:S(2)}) async-start(bf16[4,64,1152]{2,1,0:T(8,128)(2,1)} %shard_map.169), calls=%async_computation.1 | async-start | bytes 1179648 | tf_op jit(solution)/shard_map/all_to_all | solution.py:14
  38.0 16.5 %collective-permute-start.2 = (bf16[2,64,1280]{2,1,0:T(8,128)(2,1)S(1)}, bf16[2,64,1280]{2,1,0:T(8,128)(2,1)S(1)}, u32[]{:S(2)}, u32[]{:S(2)}) collective-permute-start(bf16[2,64,1280]{2,1,0:T(8,128)(2,1)S(1)} %shard_map.168.refs_4_), channel_id=1, source_target_pairs={{0,384},{128,0},{256,128},{384,256},{1,385},{129,1},{257,129},{385... | collective-permute-start | bytes 983048 | tf_op jit(solution)/shard_map/ppermute | solution.py:287
  43.2 11.4 %collective-permute-start.1 = (bf16[2,64,1280]{2,1,0:T(8,128)(2,1)S(1)}, bf16[2,64,1280]{2,1,0:T(8,128)(2,1)S(1)}, u32[]{:S(2)}, u32[]{:S(2)}) collective-permute-start(bf16[2,64,1280]{2,1,0:T(8,128)(2,1)S(1)} %shard_map.168.refs_4_), channel_id=1, source_target_pairs={{0,256},{128,384},{256,0},{384,128},{1,257},{129,385},{257,1},{385... | collective-permute-start | bytes 983048 | tf_op jit(solution)/shard_map/ppermute | solution.py:287
  49.8 9.5 %all-to-all-start.2 = ((f32[8,48,128]{2,1,0:T(8,128)}), f32[8,48,128]{2,1,0:T(8,128)S(1)}, u32[]{:S(2)}, u32[]{:S(2)}) async-start(f32[8,48,128]{2,1,0:T(8,128)} %shard_map.170), calls=%async_computation.2 | async-start | bytes 393216 | tf_op jit(solution)/shard_map/all_to_all | solution.py:14
  60.1 15.1 %all-to-all-start.3 = ((bf16[32,48,128]{2,1,0:T(8,128)(2,1)}), bf16[32,48,128]{2,1,0:T(8,128)(2,1)S(1)}, u32[]{:S(2)}, u32[]{:S(2)}) async-start(bf16[32,48,128]{2,1,0:T(8,128)(2,1)} %shard_map.171), calls=%async_computation.3 | async-start | bytes 786432 | tf_op jit(solution)/shard_map/all_to_all | solution.py:14
  75.2 10.1 %copy-start.5 = (bf16[2,64,1024]{2,1,0:T(8,128)(2,1)S(1)}, bf16[2,64,1024]{2,1,0:T(8,128)(2,1)}, u32[]{:S(2)}) copy-start(bf16[2,64,1024]{2,1,0:T(8,128)(2,1)} %refs_1_.5) | copy-start | bytes 786436
  76.8 8.5 %copy-start.4 = (bf16[2,1024,64]{1,2,0:T(8,128)(2,1)S(1)}, bf16[2,1024,64]{1,2,0:T(8,128)(2,1)}, u32[]{:S(2)}) copy-start(bf16[2,1024,64]{1,2,0:T(8,128)(2,1)} %param.30) | copy-start | bytes 786436
  76.8 23.0 %all-to-all-start.4 = ((bf16[16,4,1280]{2,1,0:T(4,128)(2,1)}), bf16[16,4,1280]{2,1,0:T(4,128)(2,1)S(1)}, u32[]{:S(2)}, u32[]{:S(2)}) async-start(bf16[16,4,1280]{2,1,0:T(4,128)(2,1)} %shard_map.172), calls=%async_computation.4 | async-start | bytes 327680 | tf_op jit(solution)/shard_map/all_to_all | solution.py:14
  85.4 14.5 %copy-start.8 = (bf16[4,1024]{1,0:T(4,128)(2,1)S(1)}, bf16[4,1024]{1,0:T(4,128)(2,1)}, u32[]{:S(2)}) copy-start(bf16[4,1024]{1,0:T(4,128)(2,1)} %refs_3_.1) | copy-start | bytes 24580
  85.4 14.5 %copy-start.9 = (s32[4,8]{1,0:T(4,128)S(1)}, s32[4,8]{1,0:T(4,128)}, u32[]{:S(2)}) copy-start(s32[4,8]{1,0:T(4,128)} %refs_0_.3) | copy-start | bytes 388
  85.4 14.5 %copy-start.10 = (bf16[4,128]{1,0:T(4,128)(2,1)S(1)}, bf16[4,128]{1,0:T(4,128)(2,1)}, u32[]{:S(2)}) copy-start(bf16[4,128]{1,0:T(4,128)(2,1)} %refs_4_.1) | copy-start | bytes 3076
  85.4 14.5 %copy-start.11 = (bf16[4,128]{1,0:T(4,128)(2,1)S(1)}, bf16[4,128]{1,0:T(4,128)(2,1)}, u32[]{:S(2)}) copy-start(bf16[4,128]{1,0:T(4,128)(2,1)} %refs_5_.1) | copy-start | bytes 3076
  85.4 14.5 %copy-start.12 = (s32[4]{0:T(128)S(1)}, s32[4]{0:T(128)}, u32[]{:S(2)}) copy-start(s32[4]{0:T(128)} %refs_1_.4) | copy-start | bytes 52
  85.5 40.6 %collective-permute-start.5 = (bf16[2,64,2048]{2,1,0:T(8,128)(2,1)S(1)}, bf16[2,64,2048]{2,1,0:T(8,128)(2,1)S(1)}, u32[]{:S(2)}, u32[]{:S(2)}) collective-permute-start(bf16[2,64,2048]{2,1,0:T(8,128)(2,1)S(1)} %shard_map.174.refs_3_), channel_id=1, source_target_pairs={{0,384},{128,0},{256,128},{384,256},{1,385},{129,1},{257,129},{385... | collective-permute-start | bytes 1572872 | tf_op jit(solution)/shard_map/ppermute | solution.py:287
  88.5 37.6 %collective-permute-start.4 = (bf16[2,64,2048]{2,1,0:T(8,128)(2,1)S(1)}, bf16[2,64,2048]{2,1,0:T(8,128)(2,1)S(1)}, u32[]{:S(2)}, u32[]{:S(2)}) collective-permute-start(bf16[2,64,2048]{2,1,0:T(8,128)(2,1)S(1)} %shard_map.174.refs_3_), channel_id=1, source_target_pairs={{0,256},{128,384},{256,0},{384,128},{1,257},{129,385},{257,1},{385... | collective-permute-start | bytes 1572872 | tf_op jit(solution)/shard_map/ppermute | solution.py:287
  92.0 34.2 %collective-permute-start.3 = (bf16[2,64,2048]{2,1,0:T(8,128)(2,1)S(1)}, bf16[2,64,2048]{2,1,0:T(8,128)(2,1)S(1)}, u32[]{:S(2)}, u32[]{:S(2)}) collective-permute-start(bf16[2,64,2048]{2,1,0:T(8,128)(2,1)S(1)} %shard_map.174.refs_3_), channel_id=1, source_target_pairs={{0,128},{128,256},{256,384},{384,0},{1,129},{129,257},{257,385},{3... | collective-permute-start | bytes 1572872 | tf_op jit(solution)/shard_map/ppermute | solution.py:287
  99.9 1.2 copy-start
  101.1 1.2 copy-start.1

commit v10 on v8

--- a/solution.py
+++ b/solution.py
@@ -274,14 +274,14 @@
         ((own_y - places[:, None]) % y_size * z_size + lax.axis_index(Z)) * local_count + numbers
     ).reshape(-1)
 
-    def packed(*weights, after=()):
+    def packed_out(after):
+        weights = (jnp.swapaxes(output_down_weight, 1, 2), output_up_weight)
         width = sum(weight.shape[2] for weight in weights)
         shape = (local_count, rank, width)
-        mine = call(pack, shape, jnp.bfloat16, *weights, scalars=0, after=after)
-        return [mine] + [
-            lax.ppermute(mine, Y, [(i, (i + k) % y_size) for i in range(y_size)])
-            for k in range(1, y_size)
-        ]
+        return call(pack, shape, jnp.bfloat16, *weights, scalars=0, after=after)
+
+    def shifted(page, k):
+        return lax.ppermute(page, Y, [(i, (i + k) % y_size) for i in range(y_size)])
 
     z_blocks = pl.pallas_call(
         first_blocks,
@@ -305,6 +305,8 @@
     z_rows = y_blocks[0]
     all_rows = exchange(y_blocks, Y).reshape(y_size * z_size * local_rows, -1)
 
+    early = packed_out((y_blocks,))
+    near = [shifted(early, 1), shifted(early, y_size - 1)]
     packed_shape = (t_size, all_rows.shape[0] // t_size * 3 // 2, 2 * rank)
     part = call(
         down_first,
@@ -315,7 +317,7 @@
         jnp.swapaxes(query_key_value_down, 1, 2),
     )
     ranks = exchange(
-        call(rank_blocks, packed_shape, jnp.bfloat16, exchange(part, T), scalars=0), T
+        call(rank_blocks, packed_shape, jnp.bfloat16, exchange(part, T), scalars=0, after=near), T
     )
     delta = call(
         up_first,
@@ -332,9 +334,8 @@
     terms = exchange(
         call(term_blocks, (z_size, local_rows, cuts[3]), jnp.bfloat16, from_y, scalars=0), Z
     )
-    out_pages = packed(
-        jnp.swapaxes(output_down_weight, 1, 2), output_up_weight, after=(from_y,)
-    )
+    late = packed_out((from_y,))
+    out_pages = [early, near[0], shifted(late, 2), near[1]]
     attention, out_blocks = pl.pallas_call(
         attend,
         out_shape=[

time: 156 us -> 158 us (1.013)
  blocking collectives: 88.1 us -> 78.7 us
  waiting for transfers between devices: 26.7 us -> 30.8 us
  local copies, waits for them, and re-layouts: 2.38 us -> 5.98 us
  starting transfers between devices: 24.6 us -> 28 us
    all_to_all x6 -> x5, blocking collectives: 88.1 us -> 78.7 us  [exchange(): return lax.all_to_all(blocks, axis, 0, 0)]
    unnamed x26 -> x30, local copies, waits for them, and re-layouts: 1.28 us -> 4.88 us
    all_to_all x3 -> x4, waiting for transfers between devices: 26.7 us -> 28.9 us  [exchange(): return lax.all_to_all(blocks, axis, 0, 0)]
    all_to_all x3 -> x4, starting transfers between devices: 16.2 us -> 18.1 us  [exchange(): return lax.all_to_all(blocks, axis, 0, 0)]
    ppermute x3, waiting for transfers between devices: 0.01 us -> 1.88 us  [shifted(): return lax.ppermute(page, Y, [(i, (i + k) % y_size) for i in range(y_size)])]
    pallas_call x8 -> x9, Pallas kernels: 5.7 us -> 6.57 us  [call(): pl.pallas_call(run, out_shape=jax.ShapeDtypeStruct(shape, dtype), in_spec...]
  transfers between devices with their start and end apart: 6 -> 7, of which waited for: 3 -> 5; matrix products, arithmetic and copies ran while one was open for 1% -> 1% of each run, Pallas kernels for 2% -> 4%
where the time goes in v10:
time: 158 us; the launch traced here: 156 us
  blocking collectives  78.7 us (50%)
  waiting for transfers between devices  30.8 us (19%)
  starting transfers between devices  28 us (18%)
  Pallas kernels  11.1 us (7%)
  local copies, waits for them, and re-layouts  5.98 us (4%)
    all_to_all x5, blocking collectives, exchange(): return lax.all_to_all(blocks, axis, 0, 0)  78.7 us
    all_to_all x4, waiting for transfers between devices, exchange(): return lax.all_to_all(blocks, axis, 0, 0)  28.9 us
    all_to_all x4, starting transfers between devices, exchange(): return lax.all_to_all(blocks, axis, 0, 0)  18.1 us
    ppermute x3, starting transfers between devices, shifted(): return lax.ppermute(page, Y, [(i, (i + k) % y_size) for i in range(y_size)])  9.91 us
    pallas_call x9, Pallas kernels, call(): pl.pallas_call(run, out_shape=jax.ShapeDtypeStruct(shape, dtype), in_spec...  6.57 us
    unnamed x30, local copies, waits for them, and re-layouts  4.88 us
  transfers between devices with their start and end apart: 7, of which 5 were waited for; matrix products, arithmetic and copies ran while one was open for 1% of the time, Pallas kernels for 4%

profile of v10, /device:TPU:6, one launch (start us, length us, event | category | flops | bytes accessed | tf_op | source)
XLA Modules:
  0.0 156.1 jit_solution(9503377277175510788)
XLA Ops:
  0.6 1.4 shard_map.167
  2.0 30.3 %all_to_all.45.refs_0_ = bf16[16,4,1152]{2,1,0:T(4,128)(2,1)S(1)} all-to-all(bf16[16,4,1152]{2,1,0:T(4,128)(2,1)} %shard_map.167), channel_id=1, replica_groups=mesh['y'=4,'z'=16,'tensor'=8] {'z'}, dimensions={0} | all-to-all | bytes 294912 | tf_op jit(solution)/shard_map/all_to_all | solution.py:14
  32.4 0.9 shard_map.168.refs_2_
  33.3 4.6 %all-to-all-start.1 = ((bf16[4,64,1152]{2,1,0:T(8,128)(2,1)}), bf16[4,64,1152]{2,1,0:T(8,128)(2,1)S(1)}, u32[]{:S(2)}, u32[]{:S(2)}) async-start(bf16[4,64,1152]{2,1,0:T(8,128)(2,1)} %shard_map.168.refs_2_), calls=%async_computation.1 | async-start | bytes 1179648 | tf_op jit(solution)/shard_map/all_to_all | solution.py:14
  37.9 5.3 %collective-permute-start.1 = (bf16[2,64,2048]{2,1,0:T(8,128)(2,1)S(1)}, bf16[2,64,2048]{2,1,0:T(8,128)(2,1)S(1)}, u32[]{:S(2)}, u32[]{:S(2)}) collective-permute-start(bf16[2,64,2048]{2,1,0:T(8,128)(2,1)S(1)} %shard_map.170.refs_3_), channel_id=1, source_target_pairs={{0,384},{128,0},{256,128},{384,256},{1,385},{129,1},{257,129},{385... | collective-permute-start | bytes 1572872 | tf_op jit(solution)/shard_map/ppermute | solution.py:284
  43.2 1.9 %collective-permute-start = (bf16[2,64,2048]{2,1,0:T(8,128)(2,1)S(1)}, bf16[2,64,2048]{2,1,0:T(8,128)(2,1)S(1)}, u32[]{:S(2)}, u32[]{:S(2)}) collective-permute-start(bf16[2,64,2048]{2,1,0:T(8,128)(2,1)S(1)} %shard_map.170.refs_3_), channel_id=1, source_target_pairs={{0,128},{128,256},{256,384},{384,0},{1,129},{129,257},{257,385},{3... | collective-permute-start | bytes 1572872 | tf_op jit(solution)/shard_map/ppermute | solution.py:284
  45.3 3.7 %all-to-all-done.1 = bf16[4,64,1152]{2,1,0:T(8,128)(2,1)S(1)} async-done(((bf16[4,64,1152]{2,1,0:T(8,128)(2,1)}), bf16[4,64,1152]{2,1,0:T(8,128)(2,1)S(1)}, u32[]{:S(2)}, u32[]{:S(2)}) %all-to-all-start.1) | async-done | bytes 589856 | tf_op jit(solution)/shard_map/all_to_all | solution.py:14
  49.0 1.7 %shard_map.169 = f32[8,48,128]{2,1,0:T(8,128)} custom-call(s32[8]{0:T(128)S(1)} %add.45.refs_0_, bf16[256,1152]{1,0:T(8,128)(2,1)S(1)} %bitcast.6, bf16[2,192,1024]{2,1,0:T(8,128)(2,1)S(1)} %bitcast.11), custom_call_target="tpu_custom_call" | custom-call | tf_op jit(solution)/shard_map/pallas_call | solution.py:40
  50.7 4.8 %all-to-all-start.2 = ((f32[8,48,128]{2,1,0:T(8,128)}), f32[8,48,128]{2,1,0:T(8,128)S(1)}, u32[]{:S(2)}, u32[]{:S(2)}) async-start(f32[8,48,128]{2,1,0:T(8,128)} %shard_map.169), calls=%async_computation.2 | async-start | bytes 393216 | tf_op jit(solution)/shard_map/all_to_all | solution.py:14
  55.5 1.9 %collective-permute-done.refs_1_.refs_4_ = bf16[2,64,2048]{2,1,0:T(8,128)(2,1)S(1)} collective-permute-done((bf16[2,64,2048]{2,1,0:T(8,128)(2,1)S(1)}, bf16[2,64,2048]{2,1,0:T(8,128)(2,1)S(1)}, u32[]{:S(2)}, u32[]{:S(2)}) %collective-permute-start) | collective-permute-done | bytes 524320 | tf_op jit(solution)/shard_map/ppermute | solution.py:284
  57.4 2.9 %all-to-all-done.2.refs_0_ = f32[8,48,128]{2,1,0:T(8,128)S(1)} async-done(((f32[8,48,128]{2,1,0:T(8,128)}), f32[8,48,128]{2,1,0:T(8,128)S(1)}, u32[]{:S(2)}, u32[]{:S(2)}) %all-to-all-start.2) | async-done | bytes 196640 | tf_op jit(solution)/shard_map/all_to_all | solution.py:14
  60.3 8.3 %all_to_all.46.refs_1_ = bf16[8,48,128]{2,1,0:T(8,128)(2,1)S(1)} all-to-all(bf16[8,48,128]{2,1,0:T(8,128)(2,1)S(1)} %shard_map.171), channel_id=1, replica_groups=mesh['y'=4,'z'=16,'tensor'=8] {'tensor'}, dimensions={0} | all-to-all | bytes 196608 | tf_op jit(solution)/shard_map/all_to_all | solution.py:14
  68.6 0.9 shard_map.172
  69.6 13.5 %all_to_all.47.refs_0_.refs_2_ = bf16[4,64,1280]{2,1,0:T(8,128)(2,1)S(1)} all-to-all(bf16[4,64,1280]{2,1,0:T(8,128)(2,1)S(1)} %bitcast.8), channel_id=1, replica_groups=mesh['y'=4,'z'=16,'tensor'=8] {'y'}, dimensions={0} | all-to-all | bytes 1310720 | tf_op jit(solution)/shard_map/all_to_all | solution.py:14
  83.2 0.7 copy-done.6
  83.9 4.3 %all-to-all-start.5 = ((bf16[16,4,1280]{2,1,0:T(4,128)(2,1)}), bf16[16,4,1280]{2,1,0:T(4,128)(2,1)}, u32[]{:S(2)}, u32[]{:S(2)}) async-start(bf16[16,4,1280]{2,1,0:T(4,128)(2,1)} %copy-done.6), calls=%async_computation.5 | async-start | bytes 327680 | tf_op jit(solution)/shard_map/all_to_all | solution.py:14
  88.2 0.9 copy-done.4
  89.1 0.8 shard_map.175
  90.0 2.7 %collective-permute-start.2 = (bf16[2,64,2048]{2,1,0:T(8,128)(2,1)}, bf16[2,64,2048]{2,1,0:T(8,128)(2,1)S(1)}, u32[]{:S(2)}, u32[]{:S(2)}) collective-permute-start(bf16[2,64,2048]{2,1,0:T(8,128)(2,1)} %shard_map.175), channel_id=1, source_target_pairs={{0,256},{128,384},{256,0},{384,128},{1,257},{129,385},{257,1},{385... | collective-permute-start | bytes 1572872 | tf_op jit(solution)/shard_map/ppermute | solution.py:284
  92.7 9.9 %all-to-all-done.5.refs_2_ = bf16[16,4,1280]{2,1,0:T(4,128)(2,1)} async-done(((bf16[16,4,1280]{2,1,0:T(4,128)(2,1)}), bf16[16,4,1280]{2,1,0:T(4,128)(2,1)}, u32[]{:S(2)}, u32[]{:S(2)}) %all-to-all-start.5) | async-done | bytes 163872 | tf_op jit(solution)/shard_map/all_to_all | solution.py:14
  102.6 1.2 copy-done.1
  103.9 0.7 copy-done.12
  104.5 0.7 copy-done.13
  105.9 3.1 %shard_map.174 = (bf16[4,1024]{1,0:T(4,128)(2,1)}, bf16[16,4,1024]{2,1,0:T(4,128)(2,1)}) custom-call(s32[4,8]{1,0:T(4,128)S(1)} %copy-done.11, s32[4]{0:T(128)S(1)} %copy-done.14, bf16[16,4,1280]{2,1,0:T(4,128)(2,1)} %all-to-all-done.5.refs_2_, bf16[4,1024]{1,0:T(4,128)(2,1)S(1)} %copy-done.10, bf16[4,128]{1,0:T(4,128)(2,1)S(1)} %copy-done.12, ...), custom_call_target="tpu_custom_call" | custom-call | tf_op jit(solution)/shard_map/pallas_call | solution.py:339
  109.0 4.4 %all-to-all-start.6 = ((bf16[16,4,1024]{2,1,0:T(4,128)(2,1)}), bf16[16,4,1024]{2,1,0:T(4,128)(2,1)S(1)}, u32[]{:S(2)}, u32[]{:S(2)}) async-start(bf16[16,4,1024]{2,1,0:T(4,128)(2,1)} %get-tuple-element.5), calls=%async_computation.6 | async-start | bytes 262144 | tf_op jit(solution)/shard_map/all_to_all | solution.py:14
  113.4 0.9 slice_bitcast_fusion.refs_2_
  114.3 12.5 %all-to-all-done.6 = bf16[16,4,1024]{2,1,0:T(4,128)(2,1)S(1)} async-done(((bf16[16,4,1024]{2,1,0:T(4,128)(2,1)}), bf16[16,4,1024]{2,1,0:T(4,128)(2,1)S(1)}, u32[]{:S(2)}, u32[]{:S(2)}) %all-to-all-start.6) | async-done | bytes 131104 | tf_op jit(solution)/shard_map/all_to_all | solution.py:14
  126.8 1.0 shard_map.176
  127.9 8.8 %all_to_all.48.refs_1_ = f32[8,32,128]{2,1,0:T(8,128)S(1)} all-to-all(f32[8,32,128]{2,1,0:T(8,128)S(1)} %shard_map.176), channel_id=1, replica_groups=mesh['y'=4,'z'=16,'tensor'=8] {'tensor'}, dimensions={0} | all-to-all | bytes 262144 | tf_op jit(solution)/shard_map/all_to_all | solution.py:14
  136.7 1.0 shard_map.177
  137.7 17.7 %all_to_all.49 = bf16[16,4,1024]{2,1,0:T(4,128)(2,1)S(1)} all-to-all(bf16[16,4,1024]{2,1,0:T(4,128)(2,1)S(1)} %reshape.51), channel_id=1, replica_groups=mesh['y'=4,'z'=16,'tensor'=8] {'z'}, dimensions={0} | all-to-all | bytes 262144 | tf_op jit(solution)/shard_map/all_to_all | solution.py:14
  155.4 0.7 reduce_sum.12
  (35 shorter events, 1.2 us)
Async XLA Ops:
  33.3 4.6 %copy-start.2 = (bf16[2,1024,64]{1,2,0:T(8,128)(2,1)S(1)}, bf16[2,1024,64]{1,2,0:T(8,128)(2,1)}, u32[]{:S(2)}) copy-start(bf16[2,1024,64]{1,2,0:T(8,128)(2,1)} %param.30) | copy-start | bytes 786436
  33.3 4.6 %copy-start.3 = (bf16[2,64,1024]{2,1,0:T(8,128)(2,1)S(1)}, bf16[2,64,1024]{2,1,0:T(8,128)(2,1)}, u32[]{:S(2)}) copy-start(bf16[2,64,1024]{2,1,0:T(8,128)(2,1)} %refs_1_.5) | copy-start | bytes 786436
  33.3 15.7 %all-to-all-start.1 = ((bf16[4,64,1152]{2,1,0:T(8,128)(2,1)}), bf16[4,64,1152]{2,1,0:T(8,128)(2,1)S(1)}, u32[]{:S(2)}, u32[]{:S(2)}) async-start(bf16[4,64,1152]{2,1,0:T(8,128)(2,1)} %shard_map.168.refs_2_), calls=%async_computation.1 | async-start | bytes 1179648 | tf_op jit(solution)/shard_map/all_to_all | solution.py:14
  37.9 11.1 %copy-start.5 = (bf16[2,1024,192]{1,2,0:T(8,128)(2,1)S(1)}, bf16[2,1024,192]{1,2,0:T(8,128)(2,1)}, u32[]{:S(2)}) copy-start(bf16[2,1024,192]{1,2,0:T(8,128)(2,1)} %param.26) | copy-start | bytes 2359300
  37.9 17.6 %collective-permute-start.1 = (bf16[2,64,2048]{2,1,0:T(8,128)(2,1)S(1)}, bf16[2,64,2048]{2,1,0:T(8,128)(2,1)S(1)}, u32[]{:S(2)}, u32[]{:S(2)}) collective-permute-start(bf16[2,64,2048]{2,1,0:T(8,128)(2,1)S(1)} %shard_map.170.refs_3_), channel_id=1, source_target_pairs={{0,384},{128,0},{256,128},{384,256},{1,385},{129,1},{257,129},{385... | collective-permute-start | bytes 1572872 | tf_op jit(solution)/shard_map/ppermute | solution.py:284
  43.2 14.2 %collective-permute-start = (bf16[2,64,2048]{2,1,0:T(8,128)(2,1)S(1)}, bf16[2,64,2048]{2,1,0:T(8,128)(2,1)S(1)}, u32[]{:S(2)}, u32[]{:S(2)}) collective-permute-start(bf16[2,64,2048]{2,1,0:T(8,128)(2,1)S(1)} %shard_map.170.refs_3_), channel_id=1, source_target_pairs={{0,128},{128,256},{256,384},{384,0},{1,129},{129,257},{257,385},{3... | collective-permute-start | bytes 1572872 | tf_op jit(solution)/shard_map/ppermute | solution.py:284
  50.7 9.5 %all-to-all-start.2 = ((f32[8,48,128]{2,1,0:T(8,128)}), f32[8,48,128]{2,1,0:T(8,128)S(1)}, u32[]{:S(2)}, u32[]{:S(2)}) async-start(f32[8,48,128]{2,1,0:T(8,128)} %shard_map.169), calls=%async_computation.2 | async-start | bytes 393216 | tf_op jit(solution)/shard_map/all_to_all | solution.py:14
  60.3 8.4 %copy-start.7 = (bf16[2,64,1024]{2,1,0:T(8,128)(2,1)S(1)}, bf16[2,64,1024]{2,1,0:T(8,128)(2,1)}, u32[]{:S(2)}) copy-start(bf16[2,64,1024]{2,1,0:T(8,128)(2,1)} %refs_3_.2) | copy-start | bytes 786436
  60.3 8.3 %copy-start.8 = (bf16[2,64,128]{2,1,0:T(8,128)(2,1)S(1)}, bf16[2,64,128]{2,1,0:T(8,128)(2,1)}, u32[]{:S(2)}) copy-start(bf16[2,64,128]{2,1,0:T(8,128)(2,1)} %refs_4_.2) | copy-start | bytes 98308
  60.3 8.3 %copy-start.9 = (bf16[2,64,128]{2,1,0:T(8,128)(2,1)S(1)}, bf16[2,64,128]{2,1,0:T(8,128)(2,1)}, u32[]{:S(2)}) copy-start(bf16[2,64,128]{2,1,0:T(8,128)(2,1)} %refs_5_.2) | copy-start | bytes 98308
  83.2 0.7 copy-start.6
  83.9 18.8 %copy-start = (bf16[32,128,128]{2,1,0:T(8,128)(2,1)S(1)}, bf16[32,128,128]{2,1,0:T(8,128)(2,1)}, u32[]{:S(2)}) copy-start(bf16[32,128,128]{2,1,0:T(8,128)(2,1)} %refs_6_.1) | copy-start | bytes 3145732
  83.9 18.8 %all-to-all-start.5 = ((bf16[16,4,1280]{2,1,0:T(4,128)(2,1)}), bf16[16,4,1280]{2,1,0:T(4,128)(2,1)}, u32[]{:S(2)}, u32[]{:S(2)}) async-start(bf16[16,4,1280]{2,1,0:T(4,128)(2,1)} %copy-done.6), calls=%async_computation.5 | async-start | bytes 327680 | tf_op jit(solution)/shard_map/all_to_all | solution.py:14
  88.2 1.0 copy-start.4
  89.1 13.5 %copy-start.10 = (bf16[4,1024]{1,0:T(4,128)(2,1)S(1)}, bf16[4,1024]{1,0:T(4,128)(2,1)}, u32[]{:S(2)}) copy-start(bf16[4,1024]{1,0:T(4,128)(2,1)} %refs_3_.3) | copy-start | bytes 24580
  89.1 13.5 %copy-start.11 = (s32[4,8]{1,0:T(4,128)S(1)}, s32[4,8]{1,0:T(4,128)}, u32[]{:S(2)}) copy-start(s32[4,8]{1,0:T(4,128)} %refs_0_.1) | copy-start | bytes 388
  90.0 36.8 %collective-permute-start.2 = (bf16[2,64,2048]{2,1,0:T(8,128)(2,1)}, bf16[2,64,2048]{2,1,0:T(8,128)(2,1)S(1)}, u32[]{:S(2)}, u32[]{:S(2)}) collective-permute-start(bf16[2,64,2048]{2,1,0:T(8,128)(2,1)} %shard_map.175), channel_id=1, source_target_pairs={{0,256},{128,384},{256,0},{384,128},{1,257},{129,385},{257,1},{385... | collective-permute-start | bytes 1572872 | tf_op jit(solution)/shard_map/ppermute | solution.py:284
  102.6 1.2 copy-start.1
  103.9 0.7 copy-start.12
  104.5 0.7 copy-start.13
  105.2 0.7 copy-start.14
  109.0 17.8 %all-to-all-start.6 = ((bf16[16,4,1024]{2,1,0:T(4,128)(2,1)}), bf16[16,4,1024]{2,1,0:T(4,128)(2,1)S(1)}, u32[]{:S(2)}, u32[]{:S(2)}) async-start(bf16[16,4,1024]{2,1,0:T(4,128)(2,1)} %get-tuple-element.5), calls=%async_computation.6 | async-start | bytes 262144 | tf_op jit(solution)/shard_map/all_to_all | solution.py:14

commit v11 on v8

--- a/solution.py
+++ b/solution.py
@@ -354,7 +354,7 @@
             pltpu.VMEM(paged_value_cache.shape, jnp.bfloat16),
             pltpu.SemaphoreType.DMA((8,)),
         ],
-        compiler_params=pltpu.CompilerParams(vmem_limit_bytes=32 * 2**20),
+        compiler_params=pltpu.CompilerParams(vmem_limit_bytes=52 * 2**20),
     )(
         page_table,
         context_len,

time: 156 us -> 155 us (level)
  no operation moved by 1% of the time
where the time goes in v11:
time: 155 us; the launch traced here: 153 us
  blocking collectives  88.4 us (57%)
  waiting for transfers between devices  26.7 us (17%)
  starting transfers between devices  24.6 us (16%)
  Pallas kernels  10.4 us (7%)
    all_to_all x6, blocking collectives, exchange(): return lax.all_to_all(blocks, axis, 0, 0)  88.4 us
    all_to_all x3, waiting for transfers between devices, exchange(): return lax.all_to_all(blocks, axis, 0, 0)  26.7 us
    all_to_all x3, starting transfers between devices, exchange(): return lax.all_to_all(blocks, axis, 0, 0)  16.2 us
    ppermute x3, starting transfers between devices, packed(): lax.ppermute(mine, Y, [(i, (i + k) % y_size) for i in range(y_size)])  8.37 us
    pallas_call x8, Pallas kernels, call(): pl.pallas_call(run, out_shape=jax.ShapeDtypeStruct(shape, dtype), in_spec...  5.68 us
    pallas_call x1, Pallas kernels, body(): pl.pallas_call(attend, out_shape=[jax.ShapeDtypeStruct(q_base.shape, jnp....  3.3 us
  transfers between devices with their start and end apart: 6, of which 3 were waited for; matrix products, arithmetic and copies ran while one was open for 1% of the time, Pallas kernels for 2%

profile of v11, /device:TPU:6, one launch (start us, length us, event | category | flops | bytes accessed | tf_op | source)
XLA Modules:
  0.0 152.8 jit_solution(10869968912490490745)
XLA Ops:
  0.6 1.4 shard_map.167
  2.0 30.3 %all_to_all.45.refs_0_ = bf16[16,4,1152]{2,1,0:T(4,128)(2,1)S(1)} all-to-all(bf16[16,4,1152]{2,1,0:T(4,128)(2,1)} %shard_map.167), channel_id=1, replica_groups=mesh['y'=4,'z'=16,'tensor'=8] {'z'}, dimensions={0} | all-to-all | bytes 294912 | tf_op jit(solution)/shard_map/all_to_all | solution.py:14
  32.4 0.9 shard_map.168
  33.3 4.5 %all-to-all-start.1 = ((bf16[4,64,1152]{2,1,0:T(8,128)(2,1)}), bf16[4,64,1152]{2,1,0:T(8,128)(2,1)S(1)}, u32[]{:S(2)}, u32[]{:S(2)}) async-start(bf16[4,64,1152]{2,1,0:T(8,128)(2,1)} %shard_map.168), calls=%async_computation.1 | async-start | bytes 1179648 | tf_op jit(solution)/shard_map/all_to_all | solution.py:14
  37.7 0.1 iota_add_fusion
  37.8 0.1 add.45.refs_0_
  37.9 8.3 %all-to-all-done.1 = bf16[4,64,1152]{2,1,0:T(8,128)(2,1)S(1)} async-done(((bf16[4,64,1152]{2,1,0:T(8,128)(2,1)}), bf16[4,64,1152]{2,1,0:T(8,128)(2,1)S(1)}, u32[]{:S(2)}, u32[]{:S(2)}) %all-to-all-start.1) | async-done | bytes 589856 | tf_op jit(solution)/shard_map/all_to_all | solution.py:14
  46.2 1.1 shard_map.169
  47.2 9.3 %all_to_all.46.refs_0_ = f32[8,48,128]{2,1,0:T(8,128)S(1)} all-to-all(f32[8,48,128]{2,1,0:T(8,128)S(1)} %shard_map.169), channel_id=1, replica_groups=mesh['y'=4,'z'=16,'tensor'=8] {'tensor'}, dimensions={0} | all-to-all | bytes 393216 | tf_op jit(solution)/shard_map/all_to_all | solution.py:14
  56.6 0.0 copy-start.5
  56.6 8.3 %all_to_all.47.refs_1_ = bf16[8,48,128]{2,1,0:T(8,128)(2,1)S(1)} all-to-all(bf16[8,48,128]{2,1,0:T(8,128)(2,1)S(1)} %shard_map.170), channel_id=1, replica_groups=mesh['y'=4,'z'=16,'tensor'=8] {'tensor'}, dimensions={0} | all-to-all | bytes 196608 | tf_op jit(solution)/shard_map/all_to_all | solution.py:14
  64.9 0.9 shard_map.171
  65.8 13.4 %all_to_all.48.refs_0_.refs_2_ = bf16[4,64,1280]{2,1,0:T(8,128)(2,1)S(1)} all-to-all(bf16[4,64,1280]{2,1,0:T(8,128)(2,1)S(1)} %bitcast.8), channel_id=1, replica_groups=mesh['y'=4,'z'=16,'tensor'=8] {'y'}, dimensions={0} | all-to-all | bytes 1310720 | tf_op jit(solution)/shard_map/all_to_all | solution.py:14
  79.3 0.8 shard_map.172
  80.1 5.8 %all-to-all-start.5 = ((bf16[16,4,1280]{2,1,0:T(4,128)(2,1)}), bf16[16,4,1280]{2,1,0:T(4,128)(2,1)S(1)}, u32[]{:S(2)}, u32[]{:S(2)}) async-start(bf16[16,4,1280]{2,1,0:T(4,128)(2,1)} %shard_map.172), calls=%async_computation.5 | async-start | bytes 327680 | tf_op jit(solution)/shard_map/all_to_all | solution.py:14
  85.9 0.0 copy-start.7
  85.9 0.0 copy-start.8
  85.9 0.0 copy-start.10
  86.0 3.1 %collective-permute-start.2 = (bf16[2,64,2048]{2,1,0:T(8,128)(2,1)S(1)}, bf16[2,64,2048]{2,1,0:T(8,128)(2,1)S(1)}, u32[]{:S(2)}, u32[]{:S(2)}) collective-permute-start(bf16[2,64,2048]{2,1,0:T(8,128)(2,1)S(1)} %shard_map.174.refs_3_), channel_id=1, source_target_pairs={{0,384},{128,0},{256,128},{384,256},{1,385},{129,1},{257,129},{385... | collective-permute-start | bytes 1572872 | tf_op jit(solution)/shard_map/ppermute | solution.py:282
  89.1 3.4 %collective-permute-start.1 = (bf16[2,64,2048]{2,1,0:T(8,128)(2,1)S(1)}, bf16[2,64,2048]{2,1,0:T(8,128)(2,1)S(1)}, u32[]{:S(2)}, u32[]{:S(2)}) collective-permute-start(bf16[2,64,2048]{2,1,0:T(8,128)(2,1)S(1)} %shard_map.174.refs_3_), channel_id=1, source_target_pairs={{0,256},{128,384},{256,0},{384,128},{1,257},{129,385},{257,1},{385... | collective-permute-start | bytes 1572872 | tf_op jit(solution)/shard_map/ppermute | solution.py:282
  92.4 1.9 %collective-permute-start = (bf16[2,64,2048]{2,1,0:T(8,128)(2,1)S(1)}, bf16[2,64,2048]{2,1,0:T(8,128)(2,1)S(1)}, u32[]{:S(2)}, u32[]{:S(2)}) collective-permute-start(bf16[2,64,2048]{2,1,0:T(8,128)(2,1)S(1)} %shard_map.174.refs_3_), channel_id=1, source_target_pairs={{0,128},{128,256},{256,384},{384,0},{1,129},{129,257},{257,385},{3... | collective-permute-start | bytes 1572872 | tf_op jit(solution)/shard_map/ppermute | solution.py:282
  94.4 6.1 %all-to-all-done.5.refs_2_ = bf16[16,4,1280]{2,1,0:T(4,128)(2,1)S(1)} async-done(((bf16[16,4,1280]{2,1,0:T(4,128)(2,1)}), bf16[16,4,1280]{2,1,0:T(4,128)(2,1)S(1)}, u32[]{:S(2)}, u32[]{:S(2)}) %all-to-all-start.5) | async-done | bytes 163872 | tf_op jit(solution)/shard_map/all_to_all | solution.py:14
  100.5 3.3 %shard_map.173 = (bf16[4,1024]{1,0:T(4,128)(2,1)}, bf16[16,4,1024]{2,1,0:T(4,128)(2,1)}) custom-call(s32[4,8]{1,0:T(4,128)S(1)} %copy-done.8, s32[4]{0:T(128)S(1)} %copy-done.11, bf16[16,4,1280]{2,1,0:T(4,128)(2,1)S(1)} %all-to-all-done.5.refs_2_, bf16[4,1024]{1,0:T(4,128)(2,1)S(1)} %copy-done.7, bf16[4,128]{1,0:T(4,128)(2,1)S(1)} %copy-done.9, ...), custom_call_target="tpu_custom_call" | custom-call | tf_op jit(solution)/shard_map/pallas_call | solution.py:338
  103.8 5.9 %all-to-all-start.6 = ((bf16[16,4,1024]{2,1,0:T(4,128)(2,1)}), bf16[16,4,1024]{2,1,0:T(4,128)(2,1)S(1)}, u32[]{:S(2)}, u32[]{:S(2)}) async-start(bf16[16,4,1024]{2,1,0:T(4,128)(2,1)} %get-tuple-element.5), calls=%async_computation.6 | async-start | bytes 262144 | tf_op jit(solution)/shard_map/all_to_all | solution.py:14
  109.8 0.9 slice_bitcast_fusion.refs_2_
  110.7 12.3 %all-to-all-done.6 = bf16[16,4,1024]{2,1,0:T(4,128)(2,1)S(1)} async-done(((bf16[16,4,1024]{2,1,0:T(4,128)(2,1)}), bf16[16,4,1024]{2,1,0:T(4,128)(2,1)S(1)}, u32[]{:S(2)}, u32[]{:S(2)}) %all-to-all-start.6) | async-done | bytes 131104 | tf_op jit(solution)/shard_map/all_to_all | solution.py:14
  123.1 1.0 shard_map.175
  124.1 8.5 %all_to_all.49.refs_1_ = f32[8,32,128]{2,1,0:T(8,128)S(1)} all-to-all(f32[8,32,128]{2,1,0:T(8,128)S(1)} %shard_map.175), channel_id=1, replica_groups=mesh['y'=4,'z'=16,'tensor'=8] {'tensor'}, dimensions={0} | all-to-all | bytes 262144 | tf_op jit(solution)/shard_map/all_to_all | solution.py:14
  132.6 1.0 shard_map.176
  133.6 0.1 reshape.51
  133.7 18.5 %all_to_all.50 = bf16[16,4,1024]{2,1,0:T(4,128)(2,1)S(1)} all-to-all(bf16[16,4,1024]{2,1,0:T(4,128)(2,1)S(1)} %reshape.51), channel_id=1, replica_groups=mesh['y'=4,'z'=16,'tensor'=8] {'z'}, dimensions={0} | all-to-all | bytes 262144 | tf_op jit(solution)/shard_map/all_to_all | solution.py:14
  152.1 0.7 reduce_sum.12
  (27 shorter events, 0.2 us)
Async XLA Ops:
  32.4 13.8 %copy-start.1 = (bf16[2,1024,192]{1,2,0:T(8,128)(2,1)S(1)}, bf16[2,1024,192]{1,2,0:T(8,128)(2,1)}, u32[]{:S(2)}) copy-start(bf16[2,1024,192]{1,2,0:T(8,128)(2,1)} %param.26) | copy-start | bytes 2359300
  33.3 12.9 %all-to-all-start.1 = ((bf16[4,64,1152]{2,1,0:T(8,128)(2,1)}), bf16[4,64,1152]{2,1,0:T(8,128)(2,1)S(1)}, u32[]{:S(2)}, u32[]{:S(2)}) async-start(bf16[4,64,1152]{2,1,0:T(8,128)(2,1)} %shard_map.168), calls=%async_computation.1 | async-start | bytes 1179648 | tf_op jit(solution)/shard_map/all_to_all | solution.py:14
  56.6 8.4 %copy-start.2 = (bf16[2,64,1024]{2,1,0:T(8,128)(2,1)S(1)}, bf16[2,64,1024]{2,1,0:T(8,128)(2,1)}, u32[]{:S(2)}) copy-start(bf16[2,64,1024]{2,1,0:T(8,128)(2,1)} %refs_3_.2) | copy-start | bytes 786436
  56.6 8.3 %copy-start.5 = (bf16[2,64,128]{2,1,0:T(8,128)(2,1)S(1)}, bf16[2,64,128]{2,1,0:T(8,128)(2,1)}, u32[]{:S(2)}) copy-start(bf16[2,64,128]{2,1,0:T(8,128)(2,1)} %refs_4_.2) | copy-start | bytes 98308
  56.6 8.3 %copy-start.6 = (bf16[2,64,128]{2,1,0:T(8,128)(2,1)S(1)}, bf16[2,64,128]{2,1,0:T(8,128)(2,1)}, u32[]{:S(2)}) copy-start(bf16[2,64,128]{2,1,0:T(8,128)(2,1)} %refs_5_.2) | copy-start | bytes 98308
  79.3 6.6 %copy-start.3 = (bf16[2,1024,64]{1,2,0:T(8,128)(2,1)S(1)}, bf16[2,1024,64]{1,2,0:T(8,128)(2,1)}, u32[]{:S(2)}) copy-start(bf16[2,1024,64]{1,2,0:T(8,128)(2,1)} %param.30) | copy-start | bytes 786436
  79.3 6.6 %copy-start.4 = (bf16[2,64,1024]{2,1,0:T(8,128)(2,1)S(1)}, bf16[2,64,1024]{2,1,0:T(8,128)(2,1)}, u32[]{:S(2)}) copy-start(bf16[2,64,1024]{2,1,0:T(8,128)(2,1)} %refs_1_.3) | copy-start | bytes 786436
  80.1 20.4 %copy-start = (bf16[32,128,128]{2,1,0:T(8,128)(2,1)S(1)}, bf16[32,128,128]{2,1,0:T(8,128)(2,1)}, u32[]{:S(2)}) copy-start(bf16[32,128,128]{2,1,0:T(8,128)(2,1)} %refs_6_.1) | copy-start | bytes 3145732
  80.1 20.4 %all-to-all-start.5 = ((bf16[16,4,1280]{2,1,0:T(4,128)(2,1)}), bf16[16,4,1280]{2,1,0:T(4,128)(2,1)S(1)}, u32[]{:S(2)}, u32[]{:S(2)}) async-start(bf16[16,4,1280]{2,1,0:T(4,128)(2,1)} %shard_map.172), calls=%async_computation.5 | async-start | bytes 327680 | tf_op jit(solution)/shard_map/all_to_all | solution.py:14
  85.9 14.6 %copy-start.7 = (bf16[4,1024]{1,0:T(4,128)(2,1)S(1)}, bf16[4,1024]{1,0:T(4,128)(2,1)}, u32[]{:S(2)}) copy-start(bf16[4,1024]{1,0:T(4,128)(2,1)} %refs_3_.3) | copy-start | bytes 24580
  85.9 14.6 %copy-start.8 = (s32[4,8]{1,0:T(4,128)S(1)}, s32[4,8]{1,0:T(4,128)}, u32[]{:S(2)}) copy-start(s32[4,8]{1,0:T(4,128)} %refs_0_.1) | copy-start | bytes 388
  85.9 14.6 %copy-start.9 = (bf16[4,128]{1,0:T(4,128)(2,1)S(1)}, bf16[4,128]{1,0:T(4,128)(2,1)}, u32[]{:S(2)}) copy-start(bf16[4,128]{1,0:T(4,128)(2,1)} %refs_4_.3) | copy-start | bytes 3076
  85.9 14.6 %copy-start.10 = (bf16[4,128]{1,0:T(4,128)(2,1)S(1)}, bf16[4,128]{1,0:T(4,128)(2,1)}, u32[]{:S(2)}) copy-start(bf16[4,128]{1,0:T(4,128)(2,1)} %refs_5_.3) | copy-start | bytes 3076
  85.9 14.6 %copy-start.11 = (s32[4]{0:T(128)S(1)}, s32[4]{0:T(128)}, u32[]{:S(2)}) copy-start(s32[4]{0:T(128)} %refs_1_.2) | copy-start | bytes 52
  86.0 37.1 %collective-permute-start.2 = (bf16[2,64,2048]{2,1,0:T(8,128)(2,1)S(1)}, bf16[2,64,2048]{2,1,0:T(8,128)(2,1)S(1)}, u32[]{:S(2)}, u32[]{:S(2)}) collective-permute-start(bf16[2,64,2048]{2,1,0:T(8,128)(2,1)S(1)} %shard_map.174.refs_3_), channel_id=1, source_target_pairs={{0,384},{128,0},{256,128},{384,256},{1,385},{129,1},{257,129},{385... | collective-permute-start | bytes 1572872 | tf_op jit(solution)/shard_map/ppermute | solution.py:282
  89.1 34.0 %collective-permute-start.1 = (bf16[2,64,2048]{2,1,0:T(8,128)(2,1)S(1)}, bf16[2,64,2048]{2,1,0:T(8,128)(2,1)S(1)}, u32[]{:S(2)}, u32[]{:S(2)}) collective-permute-start(bf16[2,64,2048]{2,1,0:T(8,128)(2,1)S(1)} %shard_map.174.refs_3_), channel_id=1, source_target_pairs={{0,256},{128,384},{256,0},{384,128},{1,257},{129,385},{257,1},{385... | collective-permute-start | bytes 1572872 | tf_op jit(solution)/shard_map/ppermute | solution.py:282
  92.4 30.6 %collective-permute-start = (bf16[2,64,2048]{2,1,0:T(8,128)(2,1)S(1)}, bf16[2,64,2048]{2,1,0:T(8,128)(2,1)S(1)}, u32[]{:S(2)}, u32[]{:S(2)}) collective-permute-start(bf16[2,64,2048]{2,1,0:T(8,128)(2,1)S(1)} %shard_map.174.refs_3_), channel_id=1, source_target_pairs={{0,128},{128,256},{256,384},{384,0},{1,129},{129,257},{257,385},{3... | collective-permute-start | bytes 1572872 | tf_op jit(solution)/shard_map/ppermute | solution.py:282
  103.8 19.2 %all-to-all-start.6 = ((bf16[16,4,1024]{2,1,0:T(4,128)(2,1)}), bf16[16,4,1024]{2,1,0:T(4,128)(2,1)S(1)}, u32[]{:S(2)}, u32[]{:S(2)}) async-start(bf16[16,4,1024]{2,1,0:T(4,128)(2,1)} %get-tuple-element.5), calls=%async_computation.6 | async-start | bytes 262144 | tf_op jit(solution)/shard_map/all_to_all | solution.py:14

commit v12 on v10

--- a/solution.py
+++ b/solution.py
@@ -306,7 +306,7 @@
     all_rows = exchange(y_blocks, Y).reshape(y_size * z_size * local_rows, -1)
 
     early = packed_out((y_blocks,))
-    near = [shifted(early, 1), shifted(early, y_size - 1)]
+    near = [shifted(early, 1)]
     packed_shape = (t_size, all_rows.shape[0] // t_size * 3 // 2, 2 * rank)
     part = call(
         down_first,
@@ -335,7 +335,7 @@
         call(term_blocks, (z_size, local_rows, cuts[3]), jnp.bfloat16, from_y, scalars=0), Z
     )
     late = packed_out((from_y,))
-    out_pages = [early, near[0], shifted(late, 2), near[1]]
+    out_pages = [early, near[0], shifted(late, 2), shifted(late, 3)]
     attention, out_blocks = pl.pallas_call(
         attend,
         out_shape=[
@@ -355,7 +355,7 @@
             pltpu.VMEM(paged_value_cache.shape, jnp.bfloat16),
             pltpu.SemaphoreType.DMA((8,)),
         ],
-        compiler_params=pltpu.CompilerParams(vmem_limit_bytes=32 * 2**20),
+        compiler_params=pltpu.CompilerParams(vmem_limit_bytes=52 * 2**20),
     )(
         page_table,
         context_len,

time: 158 us -> 156 us (0.987)
  local copies, waits for them, and re-layouts: 5.98 us -> 1.81 us
    unnamed x30 -> x26, local copies, waits for them, and re-layouts: 4.88 us -> 0.71 us
    all_to_all x4, waiting for transfers between devices: 28.9 us -> 31.8 us  [exchange(): return lax.all_to_all(blocks, axis, 0, 0)]
    ppermute x3, waiting for transfers between devices: 1.88 us -> 0.01 us  [shifted(): return lax.ppermute(page, Y, [(i, (i + k) % y_size) for i in range(y_size)])]
  transfers between devices with their start and end apart: 7 -> 7, of which waited for: 5 -> 4; matrix products, arithmetic and copies ran while one was open for 1% -> 1% of each run, Pallas kernels for 4% -> 4%
where the time goes in v12:
time: 156 us; the launch traced here: 154 us
  blocking collectives  78.7 us (50%)
  waiting for transfers between devices  31.8 us (20%)
  starting transfers between devices  28.9 us (19%)
  Pallas kernels  11.2 us (7%)
  local copies, waits for them, and re-layouts  1.81 us (1%)
    all_to_all x5, blocking collectives, exchange(): return lax.all_to_all(blocks, axis, 0, 0)  78.7 us
    all_to_all x4, waiting for transfers between devices, exchange(): return lax.all_to_all(blocks, axis, 0, 0)  31.8 us
    all_to_all x4, starting transfers between devices, exchange(): return lax.all_to_all(blocks, axis, 0, 0)  18.4 us
    ppermute x3, starting transfers between devices, shifted(): return lax.ppermute(page, Y, [(i, (i + k) % y_size) for i in range(y_size)])  10.5 us
    pallas_call x9, Pallas kernels, call(): pl.pallas_call(run, out_shape=jax.ShapeDtypeStruct(shape, dtype), in_spec...  6.55 us
    pallas_call x1, Pallas kernels, body(): pl.pallas_call(attend, out_shape=[jax.ShapeDtypeStruct(q_base.shape, jnp....  3.28 us
  transfers between devices with their start and end apart: 7, of which 4 were waited for; matrix products, arithmetic and copies ran while one was open for 1% of the time, Pallas kernels for 4%

profile of v12, /device:TPU:6, one launch (start us, length us, event | category | flops | bytes accessed | tf_op | source)
XLA Modules:
  0.0 154.0 jit_solution(17432413203598822046)
XLA Ops:
  0.6 1.4 shard_map.167
  2.0 30.3 %all_to_all.45.refs_0_ = bf16[16,4,1152]{2,1,0:T(4,128)(2,1)S(1)} all-to-all(bf16[16,4,1152]{2,1,0:T(4,128)(2,1)} %shard_map.167), channel_id=1, replica_groups=mesh['y'=4,'z'=16,'tensor'=8] {'z'}, dimensions={0} | all-to-all | bytes 294912 | tf_op jit(solution)/shard_map/all_to_all | solution.py:14
  32.4 0.9 shard_map.168.refs_2_
  33.3 4.6 %all-to-all-start.1 = ((bf16[4,64,1152]{2,1,0:T(8,128)(2,1)}), bf16[4,64,1152]{2,1,0:T(8,128)(2,1)S(1)}, u32[]{:S(2)}, u32[]{:S(2)}) async-start(bf16[4,64,1152]{2,1,0:T(8,128)(2,1)} %shard_map.168.refs_2_), calls=%async_computation.1 | async-start | bytes 1179648 | tf_op jit(solution)/shard_map/all_to_all | solution.py:14
  37.9 4.1 %collective-permute-start = (bf16[2,64,2048]{2,1,0:T(8,128)(2,1)S(1)}, bf16[2,64,2048]{2,1,0:T(8,128)(2,1)S(1)}, u32[]{:S(2)}, u32[]{:S(2)}) collective-permute-start(bf16[2,64,2048]{2,1,0:T(8,128)(2,1)S(1)} %shard_map.170.refs_3_), channel_id=1, source_target_pairs={{0,128},{128,256},{256,384},{384,0},{1,129},{129,257},{257,385},{3... | collective-permute-start | bytes 1572872 | tf_op jit(solution)/shard_map/ppermute | solution.py:284
  42.0 0.1 iota_add_fusion
  42.1 0.1 add.45.refs_0_
  42.2 7.4 %all-to-all-done.1 = bf16[4,64,1152]{2,1,0:T(8,128)(2,1)S(1)} async-done(((bf16[4,64,1152]{2,1,0:T(8,128)(2,1)}), bf16[4,64,1152]{2,1,0:T(8,128)(2,1)S(1)}, u32[]{:S(2)}, u32[]{:S(2)}) %all-to-all-start.1) | async-done | bytes 589856 | tf_op jit(solution)/shard_map/all_to_all | solution.py:14
  49.5 1.7 %shard_map.169 = f32[8,48,128]{2,1,0:T(8,128)} custom-call(s32[8]{0:T(128)S(1)} %add.45.refs_0_, bf16[256,1152]{1,0:T(8,128)(2,1)S(1)} %bitcast.6, bf16[2,192,1024]{2,1,0:T(8,128)(2,1)S(1)} %bitcast.11), custom_call_target="tpu_custom_call" | custom-call | tf_op jit(solution)/shard_map/pallas_call | solution.py:40
  51.3 4.8 %all-to-all-start.2 = ((f32[8,48,128]{2,1,0:T(8,128)}), f32[8,48,128]{2,1,0:T(8,128)S(1)}, u32[]{:S(2)}, u32[]{:S(2)}) async-start(f32[8,48,128]{2,1,0:T(8,128)} %shard_map.169), calls=%async_computation.2 | async-start | bytes 393216 | tf_op jit(solution)/shard_map/all_to_all | solution.py:14
  56.0 4.8 %all-to-all-done.2.refs_0_ = f32[8,48,128]{2,1,0:T(8,128)S(1)} async-done(((f32[8,48,128]{2,1,0:T(8,128)}), f32[8,48,128]{2,1,0:T(8,128)S(1)}, u32[]{:S(2)}, u32[]{:S(2)}) %all-to-all-start.2) | async-done | bytes 196640 | tf_op jit(solution)/shard_map/all_to_all | solution.py:14
  60.9 8.3 %all_to_all.46.refs_1_ = bf16[8,48,128]{2,1,0:T(8,128)(2,1)S(1)} all-to-all(bf16[8,48,128]{2,1,0:T(8,128)(2,1)S(1)} %shard_map.171), channel_id=1, replica_groups=mesh['y'=4,'z'=16,'tensor'=8] {'tensor'}, dimensions={0} | all-to-all | bytes 196608 | tf_op jit(solution)/shard_map/all_to_all | solution.py:14
  69.2 0.9 shard_map.172
  70.1 13.4 %all_to_all.47.refs_0_.refs_2_ = bf16[4,64,1280]{2,1,0:T(8,128)(2,1)S(1)} all-to-all(bf16[4,64,1280]{2,1,0:T(8,128)(2,1)S(1)} %bitcast.8), channel_id=1, replica_groups=mesh['y'=4,'z'=16,'tensor'=8] {'y'}, dimensions={0} | all-to-all | bytes 1310720 | tf_op jit(solution)/shard_map/all_to_all | solution.py:14
  83.5 0.1 shard_map.173
  83.7 0.6 copy-done.4
  84.3 4.2 %all-to-all-start.5 = ((bf16[16,4,1280]{2,1,0:T(4,128)(2,1)}), bf16[16,4,1280]{2,1,0:T(4,128)(2,1)S(1)}, u32[]{:S(2)}, u32[]{:S(2)}) async-start(bf16[16,4,1280]{2,1,0:T(4,128)(2,1)} %copy-done.4), calls=%async_computation.5 | async-start | bytes 327680 | tf_op jit(solution)/shard_map/all_to_all | solution.py:14
  88.6 0.0 copy-start.8
  88.6 0.8 shard_map.175
  89.5 3.1 %collective-permute-start.2 = (bf16[2,64,2048]{2,1,0:T(8,128)(2,1)}, bf16[2,64,2048]{2,1,0:T(8,128)(2,1)S(1)}, u32[]{:S(2)}, u32[]{:S(2)}) collective-permute-start(bf16[2,64,2048]{2,1,0:T(8,128)(2,1)} %shard_map.175), channel_id=1, source_target_pairs={{0,384},{128,0},{256,128},{384,256},{1,385},{129,1},{257,129},{385... | collective-permute-start | bytes 1572872 | tf_op jit(solution)/shard_map/ppermute | solution.py:284
  92.5 3.4 %collective-permute-start.1 = (bf16[2,64,2048]{2,1,0:T(8,128)(2,1)}, bf16[2,64,2048]{2,1,0:T(8,128)(2,1)S(1)}, u32[]{:S(2)}, u32[]{:S(2)}) collective-permute-start(bf16[2,64,2048]{2,1,0:T(8,128)(2,1)} %shard_map.175), channel_id=1, source_target_pairs={{0,256},{128,384},{256,0},{384,128},{1,257},{129,385},{257,1},{385... | collective-permute-start | bytes 1572872 | tf_op jit(solution)/shard_map/ppermute | solution.py:284
  95.9 7.3 %all-to-all-done.5.refs_2_ = bf16[16,4,1280]{2,1,0:T(4,128)(2,1)S(1)} async-done(((bf16[16,4,1280]{2,1,0:T(4,128)(2,1)}), bf16[16,4,1280]{2,1,0:T(4,128)(2,1)S(1)}, u32[]{:S(2)}, u32[]{:S(2)}) %all-to-all-start.5) | async-done | bytes 163872 | tf_op jit(solution)/shard_map/all_to_all | solution.py:14
  103.2 3.3 %shard_map.174 = (bf16[4,1024]{1,0:T(4,128)(2,1)}, bf16[16,4,1024]{2,1,0:T(4,128)(2,1)}) custom-call(s32[4,8]{1,0:T(4,128)S(1)} %copy-done.9, s32[4]{0:T(128)S(1)} %copy-done.12, bf16[16,4,1280]{2,1,0:T(4,128)(2,1)S(1)} %all-to-all-done.5.refs_2_, bf16[4,1024]{1,0:T(4,128)(2,1)S(1)} %copy-done.8, bf16[4,128]{1,0:T(4,128)(2,1)S(1)} %copy-done.10, ...), custom_call_target="tpu_custom_call" | custom-call | tf_op jit(solution)/shard_map/pallas_call | solution.py:339
  106.5 4.8 %all-to-all-start.6 = ((bf16[16,4,1024]{2,1,0:T(4,128)(2,1)}), bf16[16,4,1024]{2,1,0:T(4,128)(2,1)S(1)}, u32[]{:S(2)}, u32[]{:S(2)}) async-start(bf16[16,4,1024]{2,1,0:T(4,128)(2,1)} %get-tuple-element.5), calls=%async_computation.6 | async-start | bytes 262144 | tf_op jit(solution)/shard_map/all_to_all | solution.py:14
  111.3 0.9 slice_bitcast_fusion.refs_2_
  112.2 12.4 %all-to-all-done.6 = bf16[16,4,1024]{2,1,0:T(4,128)(2,1)S(1)} async-done(((bf16[16,4,1024]{2,1,0:T(4,128)(2,1)}), bf16[16,4,1024]{2,1,0:T(4,128)(2,1)S(1)}, u32[]{:S(2)}, u32[]{:S(2)}) %all-to-all-start.6) | async-done | bytes 131104 | tf_op jit(solution)/shard_map/all_to_all | solution.py:14
  124.7 1.0 shard_map.176
  125.7 8.5 %all_to_all.48.refs_1_ = f32[8,32,128]{2,1,0:T(8,128)S(1)} all-to-all(f32[8,32,128]{2,1,0:T(8,128)S(1)} %shard_map.176), channel_id=1, replica_groups=mesh['y'=4,'z'=16,'tensor'=8] {'tensor'}, dimensions={0} | all-to-all | bytes 262144 | tf_op jit(solution)/shard_map/all_to_all | solution.py:14
  134.2 1.0 shard_map.177
  135.2 0.1 reshape.51
  135.2 18.1 %all_to_all.49 = bf16[16,4,1024]{2,1,0:T(4,128)(2,1)S(1)} all-to-all(bf16[16,4,1024]{2,1,0:T(4,128)(2,1)S(1)} %reshape.51), channel_id=1, replica_groups=mesh['y'=4,'z'=16,'tensor'=8] {'z'}, dimensions={0} | all-to-all | bytes 262144 | tf_op jit(solution)/shard_map/all_to_all | solution.py:14
  153.3 0.7 reduce_sum.12
  (31 shorter events, 0.2 us)
Async XLA Ops:
  33.3 4.6 %copy-start.1 = (bf16[2,1024,64]{1,2,0:T(8,128)(2,1)S(1)}, bf16[2,1024,64]{1,2,0:T(8,128)(2,1)}, u32[]{:S(2)}) copy-start(bf16[2,1024,64]{1,2,0:T(8,128)(2,1)} %param.30) | copy-start | bytes 786436
  33.3 4.6 %copy-start.2 = (bf16[2,64,1024]{2,1,0:T(8,128)(2,1)S(1)}, bf16[2,64,1024]{2,1,0:T(8,128)(2,1)}, u32[]{:S(2)}) copy-start(bf16[2,64,1024]{2,1,0:T(8,128)(2,1)} %refs_1_.5) | copy-start | bytes 786436
  33.3 16.3 %all-to-all-start.1 = ((bf16[4,64,1152]{2,1,0:T(8,128)(2,1)}), bf16[4,64,1152]{2,1,0:T(8,128)(2,1)S(1)}, u32[]{:S(2)}, u32[]{:S(2)}) async-start(bf16[4,64,1152]{2,1,0:T(8,128)(2,1)} %shard_map.168.refs_2_), calls=%async_computation.1 | async-start | bytes 1179648 | tf_op jit(solution)/shard_map/all_to_all | solution.py:14
  37.9 11.7 %copy-start.3 = (bf16[2,1024,192]{1,2,0:T(8,128)(2,1)S(1)}, bf16[2,1024,192]{1,2,0:T(8,128)(2,1)}, u32[]{:S(2)}) copy-start(bf16[2,1024,192]{1,2,0:T(8,128)(2,1)} %param.26) | copy-start | bytes 2359300
  37.9 18.1 %collective-permute-start = (bf16[2,64,2048]{2,1,0:T(8,128)(2,1)S(1)}, bf16[2,64,2048]{2,1,0:T(8,128)(2,1)S(1)}, u32[]{:S(2)}, u32[]{:S(2)}) collective-permute-start(bf16[2,64,2048]{2,1,0:T(8,128)(2,1)S(1)} %shard_map.170.refs_3_), channel_id=1, source_target_pairs={{0,128},{128,256},{256,384},{384,0},{1,129},{129,257},{257,385},{3... | collective-permute-start | bytes 1572872 | tf_op jit(solution)/shard_map/ppermute | solution.py:284
  51.3 9.5 %all-to-all-start.2 = ((f32[8,48,128]{2,1,0:T(8,128)}), f32[8,48,128]{2,1,0:T(8,128)S(1)}, u32[]{:S(2)}, u32[]{:S(2)}) async-start(f32[8,48,128]{2,1,0:T(8,128)} %shard_map.169), calls=%async_computation.2 | async-start | bytes 393216 | tf_op jit(solution)/shard_map/all_to_all | solution.py:14
  60.8 8.4 %copy-start.5 = (bf16[2,64,1024]{2,1,0:T(8,128)(2,1)S(1)}, bf16[2,64,1024]{2,1,0:T(8,128)(2,1)}, u32[]{:S(2)}) copy-start(bf16[2,64,1024]{2,1,0:T(8,128)(2,1)} %refs_3_.2) | copy-start | bytes 786436
  60.8 8.3 %copy-start.6 = (bf16[2,64,128]{2,1,0:T(8,128)(2,1)S(1)}, bf16[2,64,128]{2,1,0:T(8,128)(2,1)}, u32[]{:S(2)}) copy-start(bf16[2,64,128]{2,1,0:T(8,128)(2,1)} %refs_4_.2) | copy-start | bytes 98308
  60.8 8.3 %copy-start.7 = (bf16[2,64,128]{2,1,0:T(8,128)(2,1)S(1)}, bf16[2,64,128]{2,1,0:T(8,128)(2,1)}, u32[]{:S(2)}) copy-start(bf16[2,64,128]{2,1,0:T(8,128)(2,1)} %refs_5_.2) | copy-start | bytes 98308
  83.6 0.7 copy-start.4
  84.3 18.9 %copy-start = (bf16[32,128,128]{2,1,0:T(8,128)(2,1)S(1)}, bf16[32,128,128]{2,1,0:T(8,128)(2,1)}, u32[]{:S(2)}) copy-start(bf16[32,128,128]{2,1,0:T(8,128)(2,1)} %refs_6_.1) | copy-start | bytes 3145732
  84.3 18.9 %all-to-all-start.5 = ((bf16[16,4,1280]{2,1,0:T(4,128)(2,1)}), bf16[16,4,1280]{2,1,0:T(4,128)(2,1)S(1)}, u32[]{:S(2)}, u32[]{:S(2)}) async-start(bf16[16,4,1280]{2,1,0:T(4,128)(2,1)} %copy-done.4), calls=%async_computation.5 | async-start | bytes 327680 | tf_op jit(solution)/shard_map/all_to_all | solution.py:14
  88.6 14.7 %copy-start.8 = (bf16[4,1024]{1,0:T(4,128)(2,1)S(1)}, bf16[4,1024]{1,0:T(4,128)(2,1)}, u32[]{:S(2)}) copy-start(bf16[4,1024]{1,0:T(4,128)(2,1)} %refs_3_.3) | copy-start | bytes 24580
  88.6 14.6 %copy-start.9 = (s32[4,8]{1,0:T(4,128)S(1)}, s32[4,8]{1,0:T(4,128)}, u32[]{:S(2)}) copy-start(s32[4,8]{1,0:T(4,128)} %refs_0_.1) | copy-start | bytes 388
  88.6 14.6 %copy-start.10 = (bf16[4,128]{1,0:T(4,128)(2,1)S(1)}, bf16[4,128]{1,0:T(4,128)(2,1)}, u32[]{:S(2)}) copy-start(bf16[4,128]{1,0:T(4,128)(2,1)} %refs_4_.3) | copy-start | bytes 3076
  88.6 14.6 %copy-start.11 = (bf16[4,128]{1,0:T(4,128)(2,1)S(1)}, bf16[4,128]{1,0:T(4,128)(2,1)}, u32[]{:S(2)}) copy-start(bf16[4,128]{1,0:T(4,128)(2,1)} %refs_5_.3) | copy-start | bytes 3076
  88.6 14.6 %copy-start.12 = (s32[4]{0:T(128)S(1)}, s32[4]{0:T(128)}, u32[]{:S(2)}) copy-start(s32[4]{0:T(128)} %refs_1_.4) | copy-start | bytes 52
  89.5 35.2 %collective-permute-start.2 = (bf16[2,64,2048]{2,1,0:T(8,128)(2,1)}, bf16[2,64,2048]{2,1,0:T(8,128)(2,1)S(1)}, u32[]{:S(2)}, u32[]{:S(2)}) collective-permute-start(bf16[2,64,2048]{2,1,0:T(8,128)(2,1)} %shard_map.175), channel_id=1, source_target_pairs={{0,384},{128,0},{256,128},{384,256},{1,385},{129,1},{257,129},{385... | collective-permute-start | bytes 1572872 | tf_op jit(solution)/shard_map/ppermute | solution.py:284
  92.5 32.1 %collective-permute-start.1 = (bf16[2,64,2048]{2,1,0:T(8,128)(2,1)}, bf16[2,64,2048]{2,1,0:T(8,128)(2,1)S(1)}, u32[]{:S(2)}, u32[]{:S(2)}) collective-permute-start(bf16[2,64,2048]{2,1,0:T(8,128)(2,1)} %shard_map.175), channel_id=1, source_target_pairs={{0,256},{128,384},{256,0},{384,128},{1,257},{129,385},{257,1},{385... | collective-permute-start | bytes 1572872 | tf_op jit(solution)/shard_map/ppermute | solution.py:284
  106.5 18.1 %all-to-all-start.6 = ((bf16[16,4,1024]{2,1,0:T(4,128)(2,1)}), bf16[16,4,1024]{2,1,0:T(4,128)(2,1)S(1)}, u32[]{:S(2)}, u32[]{:S(2)}) async-start(bf16[16,4,1024]{2,1,0:T(4,128)(2,1)} %get-tuple-element.5), calls=%async_computation.6 | async-start | bytes 262144 | tf_op jit(solution)/shard_map/all_to_all | solution.py:14

commit v13 on v12

--- a/solution.py
+++ b/solution.py
@@ -71,10 +71,16 @@
 
 
 def attend(*refs):
-    sources, (out_ref, block_ref), held, sems = refs[:8], refs[8:10], refs[10:18], refs[18]
-    table_ref, length_ref, terms_ref, q_ref, k_ref, v_ref, keys_ref, values_ref = held
+    keys_ref, sources, (out_ref, block_ref), held, sems = (
+        refs[0],
+        refs[1:8],
+        refs[8:10],
+        refs[10:17],
+        refs[17],
+    )
+    table_ref, length_ref, terms_ref, q_ref, k_ref, v_ref, values_ref = held
     copies = fetch(sources, held, sems)
-    for copy in copies[:7]:
+    for copy in copies[:6]:
         copy.wait()
     rows, width_q = q_ref.shape
     size = k_ref.shape[1]
@@ -105,7 +111,7 @@
         own_weight = jnp.exp(own - top)
         total = jnp.sum(weights, axis=1, keepdims=True) + own_weight
         if r == 0:
-            copies[7].wait()
+            copies[6].wait()
         values = jnp.concatenate([values_ref[page] for page in pages], axis=0)
         mixed = jnp.dot(weights.astype(jnp.bfloat16), values, preferred_element_type=jnp.float32)
         own_rounded = own_weight.astype(jnp.bfloat16).astype(jnp.float32)
@@ -342,7 +348,7 @@
             jax.ShapeDtypeStruct(q_base.shape, jnp.bfloat16),
             jax.ShapeDtypeStruct((z_size,) + q_base.shape, jnp.bfloat16),
         ],
-        in_specs=[ANY] * 8,
+        in_specs=[VMEM] + [ANY] * 7,
         out_specs=[VMEM] * 2,
         scratch_shapes=[
             pltpu.SMEM(page_table.shape, jnp.int32),
@@ -351,19 +357,18 @@
             pltpu.VMEM(q_base.shape, jnp.bfloat16),
             pltpu.VMEM(base_key.shape, jnp.bfloat16),
             pltpu.VMEM(base_value.shape, jnp.bfloat16),
-            pltpu.VMEM(paged_key_cache.shape, jnp.bfloat16),
             pltpu.VMEM(paged_value_cache.shape, jnp.bfloat16),
-            pltpu.SemaphoreType.DMA((8,)),
+            pltpu.SemaphoreType.DMA((7,)),
         ],
         compiler_params=pltpu.CompilerParams(vmem_limit_bytes=52 * 2**20),
     )(
+        paged_key_cache,
         page_table,
         context_len,
         terms,
         q_base,
         base_key,
         base_value,
-        paged_key_cache,
         paged_value_cache,
     )
     out_rows = exchange(out_blocks, Z).reshape(z_size * local_rows, -1)

time: 156 us -> 156 us (level)
  no operation moved by 1% of the time
where the time goes in v13:
time: 156 us; the launch traced here: 154 us
  blocking collectives  78.7 us (50%)
  waiting for transfers between devices  31.8 us (20%)
  starting transfers between devices  28.9 us (19%)
  Pallas kernels  11.2 us (7%)
  local copies, waits for them, and re-layouts  1.81 us (1%)
    all_to_all x5, blocking collectives, exchange(): return lax.all_to_all(blocks, axis, 0, 0)  78.7 us
    all_to_all x4, waiting for transfers between devices, exchange(): return lax.all_to_all(blocks, axis, 0, 0)  31.8 us
    all_to_all x4, starting transfers between devices, exchange(): return lax.all_to_all(blocks, axis, 0, 0)  18.4 us
    ppermute x3, starting transfers between devices, shifted(): return lax.ppermute(page, Y, [(i, (i + k) % y_size) for i in range(y_size)])  10.5 us
    pallas_call x9, Pallas kernels, call(): pl.pallas_call(run, out_shape=jax.ShapeDtypeStruct(shape, dtype), in_spec...  6.55 us
    pallas_call x1, Pallas kernels, body(): pl.pallas_call(attend, out_shape=[jax.ShapeDtypeStruct(q_base.shape, jnp....  3.21 us
  transfers between devices with their start and end apart: 7, of which 4 were waited for; matrix products, arithmetic and copies ran while one was open for 1% of the time, Pallas kernels for 4%

profile of v13, /device:TPU:6, one launch (start us, length us, event | category | flops | bytes accessed | tf_op | source)
XLA Modules:
  0.0 153.9 jit_solution(13246203928569253276)
XLA Ops:
  0.6 1.4 shard_map.167
  2.0 30.3 %all_to_all.45.refs_0_ = bf16[16,4,1152]{2,1,0:T(4,128)(2,1)S(1)} all-to-all(bf16[16,4,1152]{2,1,0:T(4,128)(2,1)} %shard_map.167), channel_id=1, replica_groups=mesh['y'=4,'z'=16,'tensor'=8] {'z'}, dimensions={0} | all-to-all | bytes 294912 | tf_op jit(solution)/shard_map/all_to_all | solution.py:14
  32.4 0.9 shard_map.168.refs_2_
  33.3 4.6 %all-to-all-start.1 = ((bf16[4,64,1152]{2,1,0:T(8,128)(2,1)}), bf16[4,64,1152]{2,1,0:T(8,128)(2,1)S(1)}, u32[]{:S(2)}, u32[]{:S(2)}) async-start(bf16[4,64,1152]{2,1,0:T(8,128)(2,1)} %shard_map.168.refs_2_), calls=%async_computation.1 | async-start | bytes 1179648 | tf_op jit(solution)/shard_map/all_to_all | solution.py:14
  37.9 4.1 %collective-permute-start = (bf16[2,64,2048]{2,1,0:T(8,128)(2,1)S(1)}, bf16[2,64,2048]{2,1,0:T(8,128)(2,1)S(1)}, u32[]{:S(2)}, u32[]{:S(2)}) collective-permute-start(bf16[2,64,2048]{2,1,0:T(8,128)(2,1)S(1)} %shard_map.170.refs_3_), channel_id=1, source_target_pairs={{0,128},{128,256},{256,384},{384,0},{1,129},{129,257},{257,385},{3... | collective-permute-start | bytes 1572872 | tf_op jit(solution)/shard_map/ppermute | solution.py:290
  42.0 0.1 iota_add_fusion
  42.1 0.1 add.45.refs_0_
  42.2 7.4 %all-to-all-done.1 = bf16[4,64,1152]{2,1,0:T(8,128)(2,1)S(1)} async-done(((bf16[4,64,1152]{2,1,0:T(8,128)(2,1)}), bf16[4,64,1152]{2,1,0:T(8,128)(2,1)S(1)}, u32[]{:S(2)}, u32[]{:S(2)}) %all-to-all-start.1) | async-done | bytes 589856 | tf_op jit(solution)/shard_map/all_to_all | solution.py:14
  49.5 1.7 %shard_map.169 = f32[8,48,128]{2,1,0:T(8,128)} custom-call(s32[8]{0:T(128)S(1)} %add.45.refs_0_, bf16[256,1152]{1,0:T(8,128)(2,1)S(1)} %bitcast.6, bf16[2,192,1024]{2,1,0:T(8,128)(2,1)S(1)} %bitcast.11), custom_call_target="tpu_custom_call" | custom-call | tf_op jit(solution)/shard_map/pallas_call | solution.py:40
  51.3 4.8 %all-to-all-start.2 = ((f32[8,48,128]{2,1,0:T(8,128)}), f32[8,48,128]{2,1,0:T(8,128)S(1)}, u32[]{:S(2)}, u32[]{:S(2)}) async-start(f32[8,48,128]{2,1,0:T(8,128)} %shard_map.169), calls=%async_computation.2 | async-start | bytes 393216 | tf_op jit(solution)/shard_map/all_to_all | solution.py:14
  56.0 4.8 %all-to-all-done.2.refs_0_ = f32[8,48,128]{2,1,0:T(8,128)S(1)} async-done(((f32[8,48,128]{2,1,0:T(8,128)}), f32[8,48,128]{2,1,0:T(8,128)S(1)}, u32[]{:S(2)}, u32[]{:S(2)}) %all-to-all-start.2) | async-done | bytes 196640 | tf_op jit(solution)/shard_map/all_to_all | solution.py:14
  60.8 0.0 copy-start.6
  60.9 8.3 %all_to_all.46.refs_1_ = bf16[8,48,128]{2,1,0:T(8,128)(2,1)S(1)} all-to-all(bf16[8,48,128]{2,1,0:T(8,128)(2,1)S(1)} %shard_map.171), channel_id=1, replica_groups=mesh['y'=4,'z'=16,'tensor'=8] {'tensor'}, dimensions={0} | all-to-all | bytes 196608 | tf_op jit(solution)/shard_map/all_to_all | solution.py:14
  69.2 0.9 shard_map.172
  70.1 13.4 %all_to_all.47.refs_0_.refs_2_ = bf16[4,64,1280]{2,1,0:T(8,128)(2,1)S(1)} all-to-all(bf16[4,64,1280]{2,1,0:T(8,128)(2,1)S(1)} %bitcast.8), channel_id=1, replica_groups=mesh['y'=4,'z'=16,'tensor'=8] {'y'}, dimensions={0} | all-to-all | bytes 1310720 | tf_op jit(solution)/shard_map/all_to_all | solution.py:14
  83.5 0.1 shard_map.173
  83.7 0.6 copy-done.4
  84.3 4.2 %all-to-all-start.5 = ((bf16[16,4,1280]{2,1,0:T(4,128)(2,1)}), bf16[16,4,1280]{2,1,0:T(4,128)(2,1)S(1)}, u32[]{:S(2)}, u32[]{:S(2)}) async-start(bf16[16,4,1280]{2,1,0:T(4,128)(2,1)} %copy-done.4), calls=%async_computation.5 | async-start | bytes 327680 | tf_op jit(solution)/shard_map/all_to_all | solution.py:14
  88.6 0.8 shard_map.175
  89.5 3.1 %collective-permute-start.2 = (bf16[2,64,2048]{2,1,0:T(8,128)(2,1)}, bf16[2,64,2048]{2,1,0:T(8,128)(2,1)S(1)}, u32[]{:S(2)}, u32[]{:S(2)}) collective-permute-start(bf16[2,64,2048]{2,1,0:T(8,128)(2,1)} %shard_map.175), channel_id=1, source_target_pairs={{0,384},{128,0},{256,128},{384,256},{1,385},{129,1},{257,129},{385... | collective-permute-start | bytes 1572872 | tf_op jit(solution)/shard_map/ppermute | solution.py:290
  92.5 3.4 %collective-permute-start.1 = (bf16[2,64,2048]{2,1,0:T(8,128)(2,1)}, bf16[2,64,2048]{2,1,0:T(8,128)(2,1)S(1)}, u32[]{:S(2)}, u32[]{:S(2)}) collective-permute-start(bf16[2,64,2048]{2,1,0:T(8,128)(2,1)} %shard_map.175), channel_id=1, source_target_pairs={{0,256},{128,384},{256,0},{384,128},{1,257},{129,385},{257,1},{385... | collective-permute-start | bytes 1572872 | tf_op jit(solution)/shard_map/ppermute | solution.py:290
  95.9 7.3 %all-to-all-done.5.refs_3_ = bf16[16,4,1280]{2,1,0:T(4,128)(2,1)S(1)} async-done(((bf16[16,4,1280]{2,1,0:T(4,128)(2,1)}), bf16[16,4,1280]{2,1,0:T(4,128)(2,1)S(1)}, u32[]{:S(2)}, u32[]{:S(2)}) %all-to-all-start.5) | async-done | bytes 163872 | tf_op jit(solution)/shard_map/all_to_all | solution.py:14
  103.2 3.2 %shard_map.174 = (bf16[4,1024]{1,0:T(4,128)(2,1)}, bf16[16,4,1024]{2,1,0:T(4,128)(2,1)}) custom-call(bf16[32,128,128]{2,1,0:T(8,128)(2,1)S(1)} %copy-done, s32[4,8]{1,0:T(4,128)S(1)} %copy-done.9, s32[4]{0:T(128)S(1)} %copy-done.12, bf16[16,4,1280]{2,1,0:T(4,128)(2,1)S(1)} %all-to-all-done.5.refs_3_, bf16[4,1024]{1,0:T(4,128)(2,1)S(1)} %copy-done.8, ...), custom_call_target="tpu_custom_call" | custom-call | tf_op jit(solution)/shard_map/pallas_call | solution.py:345
  106.5 4.8 %all-to-all-start.6 = ((bf16[16,4,1024]{2,1,0:T(4,128)(2,1)}), bf16[16,4,1024]{2,1,0:T(4,128)(2,1)S(1)}, u32[]{:S(2)}, u32[]{:S(2)}) async-start(bf16[16,4,1024]{2,1,0:T(4,128)(2,1)} %get-tuple-element.5), calls=%async_computation.6 | async-start | bytes 262144 | tf_op jit(solution)/shard_map/all_to_all | solution.py:14
  111.2 0.9 slice_bitcast_fusion.refs_2_
  112.2 12.4 %all-to-all-done.6 = bf16[16,4,1024]{2,1,0:T(4,128)(2,1)S(1)} async-done(((bf16[16,4,1024]{2,1,0:T(4,128)(2,1)}), bf16[16,4,1024]{2,1,0:T(4,128)(2,1)S(1)}, u32[]{:S(2)}, u32[]{:S(2)}) %all-to-all-start.6) | async-done | bytes 131104 | tf_op jit(solution)/shard_map/all_to_all | solution.py:14
  124.6 1.0 shard_map.176
  125.6 8.5 %all_to_all.48.refs_1_ = f32[8,32,128]{2,1,0:T(8,128)S(1)} all-to-all(f32[8,32,128]{2,1,0:T(8,128)S(1)} %shard_map.176), channel_id=1, replica_groups=mesh['y'=4,'z'=16,'tensor'=8] {'tensor'}, dimensions={0} | all-to-all | bytes 262144 | tf_op jit(solution)/shard_map/all_to_all | solution.py:14
  134.1 1.0 shard_map.177
  135.1 0.1 reshape.51
  135.2 18.1 %all_to_all.49 = bf16[16,4,1024]{2,1,0:T(4,128)(2,1)S(1)} all-to-all(bf16[16,4,1024]{2,1,0:T(4,128)(2,1)S(1)} %reshape.51), channel_id=1, replica_groups=mesh['y'=4,'z'=16,'tensor'=8] {'z'}, dimensions={0} | all-to-all | bytes 262144 | tf_op jit(solution)/shard_map/all_to_all | solution.py:14
  153.3 0.7 reduce_sum.12
  (31 shorter events, 0.2 us)
Async XLA Ops:
  33.3 4.6 %copy-start.1 = (bf16[2,1024,64]{1,2,0:T(8,128)(2,1)S(1)}, bf16[2,1024,64]{1,2,0:T(8,128)(2,1)}, u32[]{:S(2)}) copy-start(bf16[2,1024,64]{1,2,0:T(8,128)(2,1)} %param.30) | copy-start | bytes 786436
  33.3 4.6 %copy-start.2 = (bf16[2,64,1024]{2,1,0:T(8,128)(2,1)S(1)}, bf16[2,64,1024]{2,1,0:T(8,128)(2,1)}, u32[]{:S(2)}) copy-start(bf16[2,64,1024]{2,1,0:T(8,128)(2,1)} %refs_1_.5) | copy-start | bytes 786436
  33.3 16.3 %all-to-all-start.1 = ((bf16[4,64,1152]{2,1,0:T(8,128)(2,1)}), bf16[4,64,1152]{2,1,0:T(8,128)(2,1)S(1)}, u32[]{:S(2)}, u32[]{:S(2)}) async-start(bf16[4,64,1152]{2,1,0:T(8,128)(2,1)} %shard_map.168.refs_2_), calls=%async_computation.1 | async-start | bytes 1179648 | tf_op jit(solution)/shard_map/all_to_all | solution.py:14
  37.9 11.7 %copy-start.3 = (bf16[2,1024,192]{1,2,0:T(8,128)(2,1)S(1)}, bf16[2,1024,192]{1,2,0:T(8,128)(2,1)}, u32[]{:S(2)}) copy-start(bf16[2,1024,192]{1,2,0:T(8,128)(2,1)} %param.26) | copy-start | bytes 2359300
  37.9 18.1 %collective-permute-start = (bf16[2,64,2048]{2,1,0:T(8,128)(2,1)S(1)}, bf16[2,64,2048]{2,1,0:T(8,128)(2,1)S(1)}, u32[]{:S(2)}, u32[]{:S(2)}) collective-permute-start(bf16[2,64,2048]{2,1,0:T(8,128)(2,1)S(1)} %shard_map.170.refs_3_), channel_id=1, source_target_pairs={{0,128},{128,256},{256,384},{384,0},{1,129},{129,257},{257,385},{3... | collective-permute-start | bytes 1572872 | tf_op jit(solution)/shard_map/ppermute | solution.py:290
  51.3 9.5 %all-to-all-start.2 = ((f32[8,48,128]{2,1,0:T(8,128)}), f32[8,48,128]{2,1,0:T(8,128)S(1)}, u32[]{:S(2)}, u32[]{:S(2)}) async-start(f32[8,48,128]{2,1,0:T(8,128)} %shard_map.169), calls=%async_computation.2 | async-start | bytes 393216 | tf_op jit(solution)/shard_map/all_to_all | solution.py:14
  60.8 8.4 %copy-start.5 = (bf16[2,64,1024]{2,1,0:T(8,128)(2,1)S(1)}, bf16[2,64,1024]{2,1,0:T(8,128)(2,1)}, u32[]{:S(2)}) copy-start(bf16[2,64,1024]{2,1,0:T(8,128)(2,1)} %refs_3_.1) | copy-start | bytes 786436
  60.8 8.3 %copy-start.6 = (bf16[2,64,128]{2,1,0:T(8,128)(2,1)S(1)}, bf16[2,64,128]{2,1,0:T(8,128)(2,1)}, u32[]{:S(2)}) copy-start(bf16[2,64,128]{2,1,0:T(8,128)(2,1)} %refs_4_.2) | copy-start | bytes 98308
  60.8 8.3 %copy-start.7 = (bf16[2,64,128]{2,1,0:T(8,128)(2,1)S(1)}, bf16[2,64,128]{2,1,0:T(8,128)(2,1)}, u32[]{:S(2)}) copy-start(bf16[2,64,128]{2,1,0:T(8,128)(2,1)} %refs_5_.2) | copy-start | bytes 98308
  83.6 0.7 copy-start.4
  84.3 18.9 %copy-start = (bf16[32,128,128]{2,1,0:T(8,128)(2,1)S(1)}, bf16[32,128,128]{2,1,0:T(8,128)(2,1)}, u32[]{:S(2)}) copy-start(bf16[32,128,128]{2,1,0:T(8,128)(2,1)} %refs_0_.1) | copy-start | bytes 3145732
  84.3 18.9 %all-to-all-start.5 = ((bf16[16,4,1280]{2,1,0:T(4,128)(2,1)}), bf16[16,4,1280]{2,1,0:T(4,128)(2,1)S(1)}, u32[]{:S(2)}, u32[]{:S(2)}) async-start(bf16[16,4,1280]{2,1,0:T(4,128)(2,1)} %copy-done.4), calls=%async_computation.5 | async-start | bytes 327680 | tf_op jit(solution)/shard_map/all_to_all | solution.py:14
  88.6 14.7 %copy-start.8 = (bf16[4,1024]{1,0:T(4,128)(2,1)S(1)}, bf16[4,1024]{1,0:T(4,128)(2,1)}, u32[]{:S(2)}) copy-start(bf16[4,1024]{1,0:T(4,128)(2,1)} %refs_4_.3) | copy-start | bytes 24580
  88.6 14.6 %copy-start.9 = (s32[4,8]{1,0:T(4,128)S(1)}, s32[4,8]{1,0:T(4,128)}, u32[]{:S(2)}) copy-start(s32[4,8]{1,0:T(4,128)} %refs_1_.4) | copy-start | bytes 388
  88.6 14.6 %copy-start.10 = (bf16[4,128]{1,0:T(4,128)(2,1)S(1)}, bf16[4,128]{1,0:T(4,128)(2,1)}, u32[]{:S(2)}) copy-start(bf16[4,128]{1,0:T(4,128)(2,1)} %refs_5_.3) | copy-start | bytes 3076
  88.6 14.6 %copy-start.11 = (bf16[4,128]{1,0:T(4,128)(2,1)S(1)}, bf16[4,128]{1,0:T(4,128)(2,1)}, u32[]{:S(2)}) copy-start(bf16[4,128]{1,0:T(4,128)(2,1)} %refs_6_.1) | copy-start | bytes 3076
  88.6 14.6 %copy-start.12 = (s32[4]{0:T(128)S(1)}, s32[4]{0:T(128)}, u32[]{:S(2)}) copy-start(s32[4]{0:T(128)} %refs_2_.1) | copy-start | bytes 52
  89.5 35.1 %collective-permute-start.2 = (bf16[2,64,2048]{2,1,0:T(8,128)(2,1)}, bf16[2,64,2048]{2,1,0:T(8,128)(2,1)S(1)}, u32[]{:S(2)}, u32[]{:S(2)}) collective-permute-start(bf16[2,64,2048]{2,1,0:T(8,128)(2,1)} %shard_map.175), channel_id=1, source_target_pairs={{0,384},{128,0},{256,128},{384,256},{1,385},{129,1},{257,129},{385... | collective-permute-start | bytes 1572872 | tf_op jit(solution)/shard_map/ppermute | solution.py:290
  92.5 32.1 %collective-permute-start.1 = (bf16[2,64,2048]{2,1,0:T(8,128)(2,1)}, bf16[2,64,2048]{2,1,0:T(8,128)(2,1)S(1)}, u32[]{:S(2)}, u32[]{:S(2)}) collective-permute-start(bf16[2,64,2048]{2,1,0:T(8,128)(2,1)} %shard_map.175), channel_id=1, source_target_pairs={{0,256},{128,384},{256,0},{384,128},{1,257},{129,385},{257,1},{385... | collective-permute-start | bytes 1572872 | tf_op jit(solution)/shard_map/ppermute | solution.py:290
  106.5 18.1 %all-to-all-start.6 = ((bf16[16,4,1024]{2,1,0:T(4,128)(2,1)}), bf16[16,4,1024]{2,1,0:T(4,128)(2,1)S(1)}, u32[]{:S(2)}, u32[]{:S(2)}) async-start(bf16[16,4,1024]{2,1,0:T(4,128)(2,1)} %get-tuple-element.5), calls=%async_computation.6 | async-start | bytes 262144 | tf_op jit(solution)/shard_map/all_to_all | solution.py:14
